TPU v7x, 128 devices: a whole 4x4x4 slice. The times are simulated.
128 devices in a mesh: blk: 8 (over y_hi, x), tp: 16 (over z, y_lo, core).
Axes of the slice: x: 4, y: 4 (y_hi: 2, y_lo: 2; y = y_hi * 2 + y_lo), z: 4, core: 2. Of those that a mesh axis runs over, the one named last changes fastest.
Arguments:
- tokens: bfloat16 [4096, 8192], P('blk')
- segment_ids: int32 [8, 512], P('blk'), may hold values from 0 to 3, never falling along the last dimension, each value on 1 to 256 neighbouring positions
- q_weight: bfloat16 [8192, 8192], P('blk', 'tp'), may hold values from -0.0625 to 0.0625
- key_value_weight: bfloat16 [8192, 2048], P('blk', 'tp'), may hold values from -0.0625 to 0.0625
- o_weight: bfloat16 [8192, 8192], P('blk', 'tp'), may hold values from -0.0625 to 0.0625
- cotangent: bfloat16 [4096, 8192], P('blk'), may hold values from -6 to 6
Outputs:
- mixed: bfloat16 [4096, 8192], P('blk')
- d_tokens: bfloat16 [4096, 8192], P('blk', 'tp')
- q_grad: bfloat16 [8192, 8192], P('blk', 'tp')
- key_value_gradient: bfloat16 [8192, 2048], P('blk', 'tp')
- o_grad: bfloat16 [8192, 8192], P('blk', 'tp')
Inputs may be any that keep to these rules, and one draw needn't show every extreme that they name: `segment_ids`: in each micro-batch the document numbers never fall; each document has 1 to 256 tokens, one exactly 256.
All inputs are finite; a program needn't handle non-finite values.
Results may differ from a plain program's by a relative error of at most 0.025.
Values may be sent and summed in bfloat16 or wider, within the bound.
A program may use at most 256 MiB of HBM per device.

v0:
```python
import math

import jax
import jax.numpy as jnp
from jax import lax
from jax.sharding import PartitionSpec as P

HEAD_SIZE = 128


THETA = 10000.0


def partner(block, axis, stride):
    count = lax.axis_size(axis)
    route = []
    for low in range(count):
        high = low | 1 << stride
        if high != low and high < count:
            route += [(low, high), (high, low)]
    return lax.ppermute(block, axis, route)


def rope_tables(length, width):
    half_width = width // 2
    position = jnp.arange(length, dtype=jnp.float32)[:, None]
    channel = jnp.arange(half_width, dtype=jnp.float32)[None, :]
    angle = position * jnp.power(THETA, -2.0 * channel / width)
    return (jnp.cos(angle), jnp.sin(angle))


def rotate(vector, cosine, sine):
    front_half, back_half = jnp.split(vector, 2, axis=-1)
    return jnp.concatenate(
        [front_half * cosine - back_half * sine, back_half * cosine + front_half * sine], axis=-1
    )


def rotate_back(vector, cosine, sine):
    front_half, back_half = jnp.split(vector, 2, axis=-1)
    return jnp.concatenate(
        [front_half * cosine + back_half * sine, back_half * cosine - front_half * sine], axis=-1
    )


def allowed_mask(segment_row):
    length = segment_row.shape[0]
    places = jnp.arange(length)
    causal = places[None, :] <= places[:, None]
    return causal & (segment_row[:, None] == segment_row[None, :])


def pair_swap(local_part):
    return partner(local_part, "tp", 0)


def shards(tokens, segment_ids, q_weight, key_value_weight, o_weight, cotangent):
    length = tokens.shape[0]
    kv_width = key_value_weight.shape[1] // 2
    q_width = q_weight.shape[1]
    local_heads = q_width // HEAD_SIZE
    score_scale = 1.0 / math.sqrt(HEAD_SIZE)
    parity = lax.axis_index("tp") % 2
    full_q, full_kv, full_o = (
        lax.all_gather(q_weight, "blk", axis=0, tiled=True),
        lax.all_gather(key_value_weight, "blk", axis=0, tiled=True),
        lax.all_gather(o_weight, "blk", axis=0, tiled=True),
    )
    cosine, sine = rope_tables(length, HEAD_SIZE)
    cos_heads = cosine[:, None, :]
    sin_heads = sine[:, None, :]
    query = jnp.dot(tokens, full_q, preferred_element_type=jnp.float32).reshape(
        length, local_heads, HEAD_SIZE
    )
    kv_local = jnp.dot(tokens, full_kv, preferred_element_type=jnp.float32).astype(jnp.bfloat16)
    kv_other = pair_swap(kv_local)
    lower_part = jnp.where(parity == 0, kv_local, kv_other)
    upper_part = jnp.where(parity == 0, kv_other, kv_local)
    key_matrix_rows = jnp.concatenate([lower_part[:, :kv_width], upper_part[:, :kv_width]], axis=1)
    value_matrix_rows = jnp.concatenate(
        [lower_part[:, kv_width:], upper_part[:, kv_width:]], axis=1
    )
    query_rot = rotate(query, cos_heads, sin_heads).astype(jnp.bfloat16)
    key_rot = rotate(key_matrix_rows.astype(jnp.float32), cosine, sine).astype(jnp.bfloat16)
    scores = (
        jnp.einsum("qhd,kd->hqk", query_rot, key_rot, preferred_element_type=jnp.float32)
        * score_scale
    )
    allowed = allowed_mask(segment_ids[0])
    scores = jnp.where(allowed[None], scores, -jnp.inf)
    top = jnp.max(scores, axis=-1, keepdims=True)
    raised = jnp.exp(scores - top)
    probs = raised / jnp.sum(raised, axis=-1, keepdims=True)
    probs_low = probs.astype(jnp.bfloat16)
    attn = jnp.einsum(
        "hqk,kd->qhd", probs_low, value_matrix_rows, preferred_element_type=jnp.float32
    )
    attn = attn.astype(jnp.bfloat16).reshape(length, q_width)
    partial_value = jnp.einsum("tc,dc->td", attn, full_o, preferred_element_type=jnp.float32)
    mixed = lax.psum(partial_value.astype(jnp.bfloat16), "tp")
    d_attn = jnp.dot(cotangent, full_o, preferred_element_type=jnp.float32).astype(jnp.bfloat16)
    d_attn = d_attn.reshape(length, local_heads, HEAD_SIZE)
    d_prob = jnp.einsum(
        "qhd,kd->hqk", d_attn, value_matrix_rows, preferred_element_type=jnp.float32
    )
    row_delta = jnp.sum(probs * d_prob, axis=-1, keepdims=True)
    d_score = (probs * (d_prob - row_delta) * score_scale).astype(jnp.bfloat16)
    d_query = jnp.einsum("hqk,kd->qhd", d_score, key_rot, preferred_element_type=jnp.float32)
    d_query = (
        rotate_back(d_query, cos_heads, sin_heads).astype(jnp.bfloat16).reshape(length, q_width)
    )
    key_part = jnp.einsum("hqk,qhd->kd", d_score, query_rot, preferred_element_type=jnp.float32)
    key_part = rotate_back(key_part, cosine, sine).astype(jnp.bfloat16)
    value_part = jnp.einsum(
        "hqk,qhd->kd", probs_low, d_attn, preferred_element_type=jnp.float32
    ).astype(jnp.bfloat16)
    own_key = jnp.where(parity == 0, key_part[:, :kv_width], key_part[:, kv_width:])
    other_key = jnp.where(parity == 0, key_part[:, kv_width:], key_part[:, :kv_width])
    own_value = jnp.where(parity == 0, value_part[:, :kv_width], value_part[:, kv_width:])
    other_value = jnp.where(parity == 0, value_part[:, kv_width:], value_part[:, :kv_width])
    own_part = jnp.concatenate([own_key, own_value], axis=1)
    other_part = jnp.concatenate([other_key, other_value], axis=1)
    received = pair_swap(other_part)
    kv_grad_rows = (own_part.astype(jnp.float32) + received.astype(jnp.float32)).astype(
        jnp.bfloat16
    )
    input_term = jnp.einsum("tc,dc->td", d_query, full_q, preferred_element_type=jnp.float32)
    input_term = input_term + jnp.einsum(
        "tc,dc->td", kv_grad_rows, full_kv, preferred_element_type=jnp.float32
    )
    d_tokens = lax.psum_scatter(
        input_term.astype(jnp.bfloat16), "tp", scatter_dimension=1, tiled=True
    )
    grad_cols = jnp.concatenate([d_query, kv_grad_rows], axis=1)
    projection_part = jnp.einsum("tr,tc->rc", tokens, grad_cols, preferred_element_type=jnp.float32)
    output_part = jnp.einsum("tr,tc->rc", cotangent, attn, preferred_element_type=jnp.float32)
    summed = lax.psum_scatter(
        jnp.concatenate([projection_part, output_part], axis=1).astype(jnp.bfloat16),
        "blk",
        scatter_dimension=0,
        tiled=True,
    ).astype(jnp.float32)
    q_grad = summed[:, :q_width].astype(jnp.bfloat16)
    key_value_gradient = summed[:, q_width : q_width + 2 * kv_width].astype(jnp.bfloat16)
    o_grad = summed[:, q_width + 2 * kv_width :].astype(jnp.bfloat16)
    return (mixed, d_tokens, q_grad, key_value_gradient, o_grad)


def solution(mesh):
    in_specs = (
        P("blk", None),
        P("blk", None),
        P("blk", "tp"),
        P("blk", "tp"),
        P("blk", "tp"),
        P("blk", None),
    )
    out_specs = (P("blk", None), P("blk", "tp"), P("blk", "tp"), P("blk", "tp"), P("blk", "tp"))
    return jax.shard_map(shards, mesh=mesh, in_specs=in_specs, out_specs=out_specs, check_vma=False)
```

profile of v0, /device:TPU:73, one launch (start us, length us, event | category | flops | bytes accessed | tf_op | source)
XLA Modules:
  0.0 871.0 jit_solution(7166626157736335881)
XLA Ops:
  7.2 0.0 all-gather.4.cloned.1.call-start
  7.2 0.7 all-gather.4.cloned.1.call-update
  7.9 0.0 all-gather.6.cloned.1.call-start
  7.9 0.7 all-gather.6.cloned.1.call-update
  8.6 0.0 all-gather.8.cloned.1.call-start
  8.7 0.7 all-gather.8.cloned.1.call-update
  9.4 0.0 copy-start.4
  9.4 0.0 reduce-scatter.5.cloned.1.call-start
  9.4 55.2 %all-gather.4.cloned.1.call-done = bf16[8192,128]{1,0:T(8,128)(2,1)} async-done(((bf16[1024,128]{1,0:T(8,128)(2,1)}), bf16[8192,128]{1,0:T(8,128)(2,1)}) %all-gather.4.cloned.1.call-update) | async-done | bytes 2097168 | tf_op jit(solution)/shard_map/all_gather | solution.py:66
  64.6 6.9 convolution_convert_fusion.5
  71.5 2.1 collective-permute-start
  73.5 0.0 copy-done.4
  73.5 0.2 fusion.19
  73.8 0.7 collective-permute-done
  74.6 1.2 fusion.26
  75.8 0.1 copy.29
  76.0 0.1 copy.31
  76.1 99.5 %all-gather.6.cloned.1.call-done = bf16[8192,512]{1,0:T(8,128)(2,1)} async-done(((bf16[1024,512]{1,0:T(8,128)(2,1)}), bf16[8192,512]{1,0:T(8,128)(2,1)}) %all-gather.6.cloned.1.call-update) | async-done | bytes 8388624 | tf_op jit(solution)/shard_map/all_gather | solution.py:65
  175.6 9.6 %fusion.48 = f32[512,512]{0,1:T(8,128)S(1)} fusion(bf16[512,8192]{1,0:T(8,128)(2,1)} %param.6, bf16[8192,512]{1,0:T(8,128)(2,1)} %all-gather.6.cloned.1.call-done), kind=kOutput, calls=%fused_computation.83 | convolution fusion | flops 4294967296 | bytes 17825792 | tf_op jit(solution)/shard_map/dot_general | solution.py:72
  185.2 0.1 fusion.44
  185.3 0.3 copy.57
  185.7 0.3 copy.56
  186.0 1.1 subtract_convert_fusion.1
  187.1 5.1 fusion.47
  192.2 92.6 %all-gather.8.cloned.1.call-done = bf16[8192,512]{1,0:T(8,128)(2,1)} async-done(((bf16[1024,512]{1,0:T(8,128)(2,1)}), bf16[8192,512]{1,0:T(8,128)(2,1)}) %all-gather.8.cloned.1.call-update) | async-done | bytes 8388624 | tf_op jit(solution)/shard_map/all_gather | solution.py:67
  284.8 10.3 %convolution_convert_fusion.4 = bf16[512,512]{0,1:T(8,128)(2,1)S(1)} fusion(bf16[512,8192]{1,0:T(8,128)(2,1)} %param.11, bf16[8192,512]{1,0:T(8,128)(2,1)} %all-gather.8.cloned.1.call-done), kind=kOutput, calls=%fused_computation.26 | convolution fusion | flops 4295229440 | bytes 17301504 | tf_op jit(solution)/shard_map/dot_general | solution.py:101
  295.1 0.0 copy-start.7
  295.1 3.2 fusion.16
  298.3 0.3 copy-done.7
  298.5 0.5 convolution_convert_fusion.3
  299.0 0.0 copy-start.5
  299.0 0.0 copy-start.1
  299.1 2.8 fusion.27
  301.9 0.0 copy-done.1
  301.9 8.2 fusion.15
  310.1 7.2 fusion.14
  317.3 0.6 broadcast_select_fusion.5
  317.9 1.2 collective-permute-start.1
  319.1 0.0 copy-done.5
  319.1 10.1 %fusion.3 = bf16[8192,512]{0,1:T(8,128)(2,1)} fusion(bf16[512,512]{0,1:T(8,128)(2,1)S(1)} %bitcast.100, bf16[512,8192]{1,0:T(8,128)(2,1)} %param.11), kind=kOutput, calls=%fused_computation.8 | convolution fusion | flops 4299161600 | bytes 17301504 | tf_op jit(solution)/shard_map/tr,tc->rc/dot_general | solution.py:136
  329.2 0.4 add_convert_fusion.1
  329.6 0.3 pad_maximum_fusion.2
  329.9 0.2 copy.38
  330.1 0.0 collective-permute-done.1
  330.2 9.5 %fusion.2 = bf16[8192,640]{0,1:T(8,128)(2,1)S(1)} fusion(bf16[512,8192]{1,0:T(8,128)(2,1)} %param.6, bf16[512,128]{0,1:T(8,128)(2,1)S(1)} %add_convert_fusion.3, bf16[512,512]{0,1:T(8,128)(2,1)S(1)} %bitcast.94), kind=kOutput, calls=%fused_computation.7 | convolution fusion | flops 5375262720 | bytes 19529728 | tf_op jit(solution)/shard_map/tr,tc->rc/dot_general | solution.py:135
  339.7 13.9 %pad_maximum_fusion = bf16[8192,1152]{0,1:T(8,128)(2,1)} fusion(bf16[8192,512]{0,1:T(8,128)(2,1)} %fusion.3, bf16[8192,640]{0,1:T(8,128)(2,1)S(1)} %fusion.2), kind=kLoop, calls=%fused_computation.2 | loop fusion | flops 37748736 | bytes 37748736 | tf_op jit(solution)/shard_map/concatenate | solution.py:138
  353.6 0.0 reduce-scatter.5.cloned.1.call-update
  353.6 0.0 all-reduce.2.cloned.1.call-start
  353.6 1.0 copy-done.6
  354.6 10.3 %convolution_convert_fusion.2 = bf16[512,8192]{1,0:T(8,128)(2,1)} fusion(bf16[512,512]{0,1:T(8,128)(2,1)S(1)} %bitcast.101, bf16[8192,512]{1,0:T(8,128)(2,1)} %all-gather.8.cloned.1.call-done), kind=kOutput, calls=%fused_computation.6 | convolution fusion | flops 4299161600 | bytes 17301504 | tf_op jit(solution)/shard_map/tc,dc->td/dot_general | solution.py:99
  364.9 0.0 all-reduce.2.cloned.1.call-update
  364.9 0.0 reduce-scatter.3.cloned.1.call-start
  365.0 12.1 %fusion.49 = f32[512,8192]{1,0:T(8,128)} fusion(bf16[512,512]{0,1:T(8,128)(2,1)S(1)} %bitcast.95, bf16[8192,512]{1,0:T(8,128)(2,1)} %all-gather.6.cloned.1.call-done), kind=kOutput, calls=%fused_computation.84 | convolution fusion | flops 4294967296 | bytes 25690112 | tf_op jit(solution)/shard_map/tc,dc->td/dot_general | solution.py:127
  377.1 0.0 copy-done
  377.1 11.9 %add_convert_fusion = bf16[512,8192]{1,0:T(8,128)(2,1)} fusion(f32[512,8192]{1,0:T(8,128)} %fusion.49, bf16[512,128]{0,1:T(8,128)(2,1)S(1)} %add_convert_fusion.3, bf16[8192,128]{1,0:T(8,128)(2,1)S(1)} %copy-done), kind=kOutput, calls=%fused_computation.3 | convolution fusion | flops 1082130432 | bytes 27394048 | tf_op jit(solution)/shard_map/tc,dc->td/dot_general | solution.py:128
  389.0 0.0 reduce-scatter.3.cloned.1.call-update
  389.0 169.9 %reduce-scatter.5.cloned.1.call-done = bf16[1024,1152]{0,1:T(8,128)(2,1)} async-done(((bf16[8192,1152]{0,1:T(8,128)(2,1)}), bf16[1024,1152]{0,1:T(8,128)(2,1)}) %reduce-scatter.5.cloned.1.call-update) | async-done | bytes 2359312 | tf_op jit(solution)/shard_map/reduce_scatter | solution.py:137
  558.9 1.8 fusion.43
  560.6 1.3 copy.44
  562.0 0.8 copy.43
  562.8 1.3 copy.42
  564.1 192.8 %all-reduce.2.cloned.1.call-done = bf16[512,8192]{1,0:T(8,128)(2,1)} async-done(((bf16[512,8192]{1,0:T(8,128)(2,1)}), bf16[512,8192]{1,0:T(8,128)(2,1)}) %all-reduce.2.cloned.1.call-update) | async-done | bytes 8388624 | tf_op jit(solution)/shard_map/psum | solution.py:100
  757.0 99.5 %reduce-scatter.3.cloned.1.call-done = bf16[512,512]{1,0:T(8,128)(2,1)} async-done(((bf16[512,8192]{1,0:T(8,128)(2,1)}), bf16[512,512]{1,0:T(8,128)(2,1)}) %reduce-scatter.3.cloned.1.call-update) | async-done | bytes 524304 | tf_op jit(solution)/shard_map/reduce_scatter | solution.py:131
  856.4 7.8 copy.59
  (16 shorter events, 0.2 us)
Async XLA Ops:
  7.2 57.5 %all-gather.4.cloned.1.call-start = ((), (), s32[]{:S(2)}) async-start(), calls=%async_computation.2 | async-start | bytes 2359296 | tf_op jit(solution)/shard_map/all_gather | solution.py:66
  7.9 167.7 %all-gather.6.cloned.1.call-start = ((), (), s32[]{:S(2)}) async-start(), calls=%async_computation.3 | async-start | bytes 9437184 | tf_op jit(solution)/shard_map/all_gather | solution.py:65
  8.6 276.1 %all-gather.8.cloned.1.call-start = ((), (), s32[]{:S(2)}) async-start(), calls=%async_computation.4 | async-start | bytes 9437184 | tf_op jit(solution)/shard_map/all_gather | solution.py:67
  9.4 64.2 %copy-start.4 = (s32[1,512]{1,0:T(1,128)S(1)}, s32[1,512]{1,0:T(1,128)}, u32[]{:S(2)}) copy-start(s32[1,512]{1,0:T(1,128)} %param.7) | copy-start | bytes 6148
  9.4 549.5 %reduce-scatter.5.cloned.1.call-start = ((), (), s32[]{:S(2)}) async-start(), calls=%async_computation.7 | async-start | bytes 21233664 | tf_op jit(solution)/shard_map/reduce_scatter | solution.py:137
  71.5 3.1 collective-permute-start
  295.1 3.5 copy-start.7
  299.0 20.0 %copy-start.5 = (bf16[128,4,512]{2,0,1:T(8,128)(2,1)}, bf16[128,4,512]{2,0,1:T(8,128)(2,1)S(1)}, u32[]{:S(2)}) copy-start(bf16[128,4,512]{2,0,1:T(8,128)(2,1)S(1)} %convolution_convert_fusion.3) | copy-start | bytes 1572868
  299.0 2.8 copy-start.1
  301.9 8.2 copy-start.2
  301.9 8.2 copy-start.3
  317.9 12.2 %collective-permute-start.1 = (bf16[512,128]{0,1:T(8,128)(2,1)S(1)}, bf16[512,128]{0,1:T(8,128)(2,1)S(1)}, u32[]{:S(2)}, u32[]{:S(2)}) collective-permute-start(bf16[512,128]{0,1:T(8,128)(2,1)S(1)} %pad_maximum_fusion.3), channel_id=1, source_target_pairs={{0,1},{1,0},{2,3},{3,2},{4,5},{5,4},{6,7},{7,6},{8,9},{9,8},{10,11... | collective-permute-start | bytes 393224 | tf_op jit(solution)/shard_map/ppermute | solution.py:21
  353.6 1.0 copy-start.6
  353.6 403.4 %all-reduce.2.cloned.1.call-start = ((), (), s32[]{:S(2)}) async-start(), calls=%async_computation.5 | async-start | bytes 16777216 | tf_op jit(solution)/shard_map/psum | solution.py:100
  364.9 12.1 %copy-start = (bf16[8192,128]{1,0:T(8,128)(2,1)S(1)}, bf16[8192,128]{1,0:T(8,128)(2,1)}, u32[]{:S(2)}) copy-start(bf16[8192,128]{1,0:T(8,128)(2,1)} %all-gather.4.cloned.1.call-done) | copy-start | bytes 6291460
  364.9 491.5 %reduce-scatter.3.cloned.1.call-start = ((), (), s32[]{:S(2)}) async-start(), calls=%async_computation.6 | async-start | bytes 8912896 | tf_op jit(solution)/shard_map/reduce_scatter | solution.py:131
  558.9 3.1 slice-start
Sparse Core Ops, SparseCore 0:
  10.3 54.2 all-gather.3
  66.9 108.6 all-gather.5
  177.9 106.7 all-gather.7
  353.7 205.1 reduce-scatter.4
  562.0 194.9 all-reduce.1
  759.9 96.4 reduce-scatter.2
where the time goes:
time: 875 us; the launch traced here: 871 us
  waiting for transfers between devices  712 us (81%)
  matrix products  108 us (12%)
  other arithmetic  17.8 us (2%)
  local copies, waits for them, and re-layouts  15.6 us (2%)
  between operations  14.4 us (2%)
    psum x1, waiting for transfers between devices, shards(): mixed = lax.psum(partial_value.astype(jnp.bfloat16), 'tp')  193 us
    reduce_scatter x1, waiting for transfers between devices, shards(): lax.psum_scatter(jnp.concatenate([projection_part, output_part], axis=1)....  170 us
    all_gather x1, waiting for transfers between devices, shards(): lax.all_gather(q_weight, 'blk', axis=0, tiled=True)  99.5 us
    reduce_scatter x1, waiting for transfers between devices, shards(): lax.psum_scatter(input_term.astype(jnp.bfloat16), 'tp', scatter_dimension...  99.5 us
    all_gather x1, waiting for transfers between devices, shards(): lax.all_gather(o_weight, 'blk', axis=0, tiled=True)  92.6 us
    all_gather x1, waiting for transfers between devices, shards(): lax.all_gather(key_value_weight, 'blk', axis=0, tiled=True)  55.2 us
  transfers between devices with their start and end apart: 8, of which 7 were waited for; matrix products, arithmetic and copies ran while one was open for 9% of the time, Pallas kernels for 0%

commit v1 on v0

v1 whole, which is shorter than its diff:
```python
import math

import jax
import jax.numpy as jnp
from jax import lax
from jax.sharding import PartitionSpec as P

HEAD_SIZE = 128


THETA = 10000.0


def rope_tables(length, width):
    half_width = width // 2
    position = jnp.arange(length, dtype=jnp.float32)[:, None]
    channel = jnp.arange(half_width, dtype=jnp.float32)[None, :]
    angle = position * jnp.power(THETA, -2.0 * channel / width)
    return (jnp.cos(angle), jnp.sin(angle))


def rotate(vector, cosine, sine):
    front_half, back_half = jnp.split(vector, 2, axis=-1)
    return jnp.concatenate(
        [front_half * cosine - back_half * sine, back_half * cosine + front_half * sine], axis=-1
    )


def rotate_back(vector, cosine, sine):
    front_half, back_half = jnp.split(vector, 2, axis=-1)
    return jnp.concatenate(
        [front_half * cosine + back_half * sine, back_half * cosine - front_half * sine], axis=-1
    )


def allowed_mask(segment_row):
    length = segment_row.shape[0]
    places = jnp.arange(length)
    causal = places[None, :] <= places[:, None]
    return causal & (segment_row[:, None] == segment_row[None, :])


def places(device):
    blk, tp = divmod(device, 16)
    return (*divmod(blk, 4), tp // 4, tp // 2 % 2, tp % 2)


def device_at(h, x, z, low, core):
    return (h * 4 + x) * 16 + z * 4 + low * 2 + core


def move(block, dh=0, dx=0, dz=0, dl=0, dc=0):
    route = []
    for device in range(128):
        h, x, z, low, core = places(device)
        target = device_at(h ^ dh, (x + dx) % 4, (z + dz) % 4, low ^ dl, core ^ dc)
        route.append((device, target))
    return lax.ppermute(block, ("blk", "tp"), route)


def hand_over(block):
    route = []
    for device in range(128):
        h, x, z, low, core = places(device)
        dh, dx = divmod(z * 2 + low, 4)
        blk = (h ^ dh) * 4 + (x - dx) % 4
        route.append((device, blk * 16 + (h * 4 + x) * 2 + core))
    return lax.ppermute(block, ("blk", "tp"), route)


def low_bits(array):
    return array.astype(jnp.bfloat16)


def product(left, right):
    return jnp.dot(left, right, preferred_element_type=jnp.float32)


def product_t(left, right):
    return jnp.einsum("tc,dc->td", left, right, preferred_element_type=jnp.float32)


def column_block(rows, place):
    h, x, z, _, core = place
    height = rows.shape[0] // 8
    width = rows.shape[1] // 8
    mine = lax.dynamic_slice(rows, ((z * 2 + core) * height, 0), (height, rows.shape[1]))
    mine = mine.reshape(height, 8, width)
    pieces = []
    for dh in range(2):
        for dx in range(4):
            target = (h ^ dh) * 4 + (x + dx) % 4
            piece = lax.dynamic_index_in_dim(mine, target, 1, keepdims=False)
            pieces.append(move(piece, dh=dh, dx=dx) if dh or dx else piece)
    own = jnp.stack(pieces)
    below = move(own, dz=1)
    above = move(own, dz=-1)
    far = jnp.concatenate([move(below[:4], dz=1), move(above[4:], dz=-1)])
    buffer = jnp.zeros((8, 8, height, width), rows.dtype)
    for dz, part in ((0, own), (-1, below), (1, above), (2, far)):
        level = (z + dz) % 4
        for other in range(2):
            piece = move(part, dc=1) if other else part
            at = level * 2 + (core ^ other)
            buffer = lax.dynamic_update_slice(buffer, piece[:, None], (0, at, 0, 0))
    return buffer.reshape(8, 8 * height, width)


def reduce_blk(block, weight):
    def term(dh, dx):
        return product(block[dh * 4 + dx], weight)

    first = move(low_bits(term(0, 2)), dx=-1)
    second = move(low_bits(term(1, 2)), dx=1)
    near_right = move(low_bits(term(1, 1)), dx=-1)
    near_left = move(low_bits(term(0, 3)), dx=1)
    sum_left = move(low_bits(term(0, 1) + first), dx=-1)
    sum_right = move(low_bits(term(1, 3) + second), dx=1)
    other = move(low_bits(term(1, 0) + near_right + sum_right), dh=1)
    return term(0, 0) + near_left + sum_left + other


def spread_ring(block, side, ring):
    beside = move(block, **{side: 1})
    left = [move(part, **{ring: 1}) for part in (block, beside)]
    right = [move(part, **{ring: -1}) for part in (block, beside)]
    far = [move(left[0], **{ring: 1}), move(right[1], **{ring: -1})]
    return [block, left[0], far[0], right[0], beside, left[1], far[1], right[1]]


def reduce_tp(pairs, place):
    _, _, z, low, core = place

    def term(dz, half):
        total = 0.0
        for rows, weight in pairs:
            level = (z + dz) % 4
            part = lax.dynamic_index_in_dim(
                rows.reshape(4, rows.shape[0] // 4, -1), level, 0, keepdims=False
            )
            columns = lax.dynamic_index_in_dim(
                weight.reshape(2, weight.shape[0] // 2, -1), half, 0, keepdims=False
            )
            total = total + product_t(part, columns)
        return total

    def both(dz):
        other = move(low_bits(term(dz, 1 - core)), dc=1)
        total = term(dz, core) + other
        return total.reshape(2, total.shape[0] // 2, -1)

    distant = low_bits(both(2))
    first = move(distant[0], dz=-1)
    second = move(distant[1], dz=1)
    lower = both(-1)
    upper = both(1)
    from_above_one = move(low_bits(lower[1]), dz=-1)
    from_below_zero = move(low_bits(upper[0]), dz=1)
    from_above_zero = move(low_bits(lower[0] + first), dz=-1)
    from_below_one = move(low_bits(upper[1] + second), dz=1)
    own = both(0)
    zero = own[0] + from_above_zero + from_below_zero
    one = own[1] + from_above_one + from_below_one
    beside = move(low_bits(jnp.where(low == 0, one, zero)), dl=1)
    return hand_over(low_bits(jnp.where(low == 0, zero, one) + beside))


def spread_tp(block, place):
    _, _, z, low, core = place
    width = block.shape[1]
    result = jnp.zeros((block.shape[0], 16 * width), block.dtype)
    for index, part in enumerate(spread_ring(block, "dl", "dz")):
        dl, dz = divmod(index, 4)
        base = (z - dz) % 4 * 4 + (low ^ dl) * 2
        for other in range(2):
            piece = move(part, dc=1) if other else part
            at = (base + (core ^ other)) * width
            result = lax.dynamic_update_slice(result, piece, (0, at))
    return result


def shards(tokens, segment_ids, q_weight, key_value_weight, o_weight, cotangent):
    length = tokens.shape[0]
    kv_width = key_value_weight.shape[1] // 2
    q_width = q_weight.shape[1]
    local_heads = q_width // HEAD_SIZE
    score_scale = 1.0 / math.sqrt(HEAD_SIZE)
    blk, tp = lax.axis_index("blk"), lax.axis_index("tp")
    place = (blk // 4, blk % 4, tp // 4, tp // 2 % 2, tp % 2)
    core = place[4]
    token_block = column_block(tokens, place)
    cot_block = column_block(cotangent, place)
    in_weight = jnp.concatenate([q_weight, key_value_weight], axis=1)
    projected = reduce_blk(token_block, in_weight)
    d_attn = low_bits(reduce_blk(cot_block, o_weight))
    cosine, sine = rope_tables(length, HEAD_SIZE)
    cos_heads = cosine[:, None, :]
    sin_heads = sine[:, None, :]
    query = projected[:, :q_width].reshape(length, local_heads, HEAD_SIZE)
    kv_local = low_bits(projected[:, q_width:])
    kv_other = move(kv_local, dc=1)
    lower_part = jnp.where(core == 0, kv_local, kv_other)
    upper_part = jnp.where(core == 0, kv_other, kv_local)
    key_matrix_rows = jnp.concatenate([lower_part[:, :kv_width], upper_part[:, :kv_width]], axis=1)
    value_matrix_rows = jnp.concatenate(
        [lower_part[:, kv_width:], upper_part[:, kv_width:]], axis=1
    )
    query_rot = low_bits(rotate(query, cos_heads, sin_heads))
    key_rot = low_bits(rotate(key_matrix_rows.astype(jnp.float32), cosine, sine))
    scores = (
        jnp.einsum("qhd,kd->hqk", query_rot, key_rot, preferred_element_type=jnp.float32)
        * score_scale
    )
    allowed = allowed_mask(segment_ids[0])
    scores = jnp.where(allowed[None], scores, -jnp.inf)
    top = jnp.max(scores, axis=-1, keepdims=True)
    raised = jnp.exp(scores - top)
    probs = raised / jnp.sum(raised, axis=-1, keepdims=True)
    probs_low = low_bits(probs)
    attn = jnp.einsum(
        "hqk,kd->qhd", probs_low, value_matrix_rows, preferred_element_type=jnp.float32
    )
    attn = low_bits(attn).reshape(length, q_width)
    attn_all = jnp.concatenate(spread_ring(attn, "dh", "dx"))
    mixed = spread_tp(reduce_tp([(attn_all, o_weight)], place), place)
    d_attn = d_attn.reshape(length, local_heads, HEAD_SIZE)
    d_prob = jnp.einsum(
        "qhd,kd->hqk", d_attn, value_matrix_rows, preferred_element_type=jnp.float32
    )
    row_delta = jnp.sum(probs * d_prob, axis=-1, keepdims=True)
    d_score = low_bits(probs * (d_prob - row_delta) * score_scale)
    d_query = jnp.einsum("hqk,kd->qhd", d_score, key_rot, preferred_element_type=jnp.float32)
    d_query = low_bits(rotate_back(d_query, cos_heads, sin_heads)).reshape(length, q_width)
    key_part = jnp.einsum("hqk,qhd->kd", d_score, query_rot, preferred_element_type=jnp.float32)
    key_part = low_bits(rotate_back(key_part, cosine, sine))
    value_part = low_bits(
        jnp.einsum("hqk,qhd->kd", probs_low, d_attn, preferred_element_type=jnp.float32)
    )
    own_key = jnp.where(core == 0, key_part[:, :kv_width], key_part[:, kv_width:])
    other_key = jnp.where(core == 0, key_part[:, kv_width:], key_part[:, :kv_width])
    own_value = jnp.where(core == 0, value_part[:, :kv_width], value_part[:, kv_width:])
    other_value = jnp.where(core == 0, value_part[:, kv_width:], value_part[:, :kv_width])
    own_part = jnp.concatenate([own_key, own_value], axis=1)
    other_part = jnp.concatenate([other_key, other_value], axis=1)
    received = move(other_part, dc=1)
    kv_grad_rows = low_bits(own_part.astype(jnp.float32) + received.astype(jnp.float32))
    grad_cols = jnp.concatenate([d_query, kv_grad_rows], axis=1)
    grad_all = jnp.concatenate(spread_ring(grad_cols, "dh", "dx"))
    d_tokens = reduce_tp([(grad_all, in_weight)], place)
    token_rows = token_block.reshape(-1, token_block.shape[2])
    cot_rows = cot_block.reshape(-1, cot_block.shape[2])
    projection_grad = low_bits(
        jnp.einsum("tr,tc->rc", token_rows, grad_all, preferred_element_type=jnp.float32)
    )
    o_grad = low_bits(
        jnp.einsum("tr,tc->rc", cot_rows, attn_all, preferred_element_type=jnp.float32)
    )
    return (mixed, d_tokens, projection_grad[:, :q_width], projection_grad[:, q_width:], o_grad)


def solution(mesh):
    in_specs = (
        P("blk", None),
        P("blk", None),
        P("blk", "tp"),
        P("blk", "tp"),
        P("blk", "tp"),
        P("blk", None),
    )
    out_specs = (P("blk", None), P("blk", "tp"), P("blk", "tp"), P("blk", "tp"), P("blk", "tp"))
    return jax.shard_map(shards, mesh=mesh, in_specs=in_specs, out_specs=out_specs, check_vma=False)
```

time: 875 us -> 587 us (0.67)
  the two profiles are of different devices: /device:TPU:73 before, /device:TPU:1 now
where the time goes in v1:
time: 587 us; the launch traced here: 577 us
  waiting for transfers between devices  195 us (33%)
  starting transfers between devices  177 us (30%)
  local copies, waits for them, and re-layouts  94.4 us (16%)
  matrix products  92.4 us (16%)
  other arithmetic  15.7 us (3%)
    ppermute x97, waiting for transfers between devices, move(): return lax.ppermute(block, ('blk', 'tp'), route)  195 us
    ppermute x97, starting transfers between devices, move(): return lax.ppermute(block, ('blk', 'tp'), route)  171 us
    unnamed x99, local copies, waits for them, and re-layouts  41.7 us
    dot_general x16, matrix products, product_t(): jnp.einsum('tc,dc->td', left, right, preferred_element_type=jnp.float32)  27 us
    dot_general x16, matrix products, product(): return jnp.dot(left, right, preferred_element_type=jnp.float32)  15 us
  transfers between devices with their start and end apart: 99, of which 32 were waited for; matrix products, arithmetic and copies ran while one was open for 30% of the time, Pallas kernels for 0%

profile of v1, /device:TPU:1, one launch (start us, length us, event | category | flops | bytes accessed | tf_op | source)
XLA Modules:
  0.0 576.8 jit_solution(10119906894515267035)
XLA Ops:
  7.7 2.5 collective-permute-start.58
  11.6 3.0 collective-permute-start.60
  19.5 3.5 collective-permute-start.62
  32.1 2.9 collective-permute-start.3
  36.3 3.6 collective-permute-start.5
  52.7 5.2 collective-permute-start.64
  60.2 6.0 %collective-permute-done.65 = bf16[8,64,1024]{2,1,0:T(8,128)(2,1)} collective-permute-done((bf16[8,64,1024]{2,1,0:T(8,128)(2,1)}, bf16[8,64,1024]{2,1,0:T(8,128)(2,1)}, u32[]{:S(2)}, u32[]{:S(2)}) %collective-permute-start.65) | collective-permute-done | bytes 1048608 | tf_op jit(solution)/shard_map/ppermute | solution.py:58
  66.2 9.5 %collective-permute-start.7 = (bf16[8,64,1024]{2,1,0:T(8,128)(2,1)}, bf16[8,64,1024]{2,1,0:T(8,128)(2,1)S(1)}, u32[]{:S(2)}, u32[]{:S(2)}) collective-permute-start(bf16[8,64,1024]{2,1,0:T(8,128)(2,1)} %bitcast_dynamic-update-slice_fusion.25), channel_id=1, source_target_pairs={{0,1},{1,0},{2,3},{3,2},{4,5},{5,4},{6,7},{7,6},{8,9},{9,8},{10,11... | collective-permute-start | bytes 3145736 | tf_op jit(solution)/shard_map/ppermute | solution.py:58
  81.7 6.9 %collective-permute-done.8 = bf16[8,64,1024]{2,1,0:T(8,128)(2,1)} collective-permute-done((bf16[8,64,1024]{2,1,0:T(8,128)(2,1)}, bf16[8,64,1024]{2,1,0:T(8,128)(2,1)}, u32[]{:S(2)}, u32[]{:S(2)}) %collective-permute-start.8) | collective-permute-done | bytes 1048608 | tf_op jit(solution)/shard_map/ppermute | solution.py:58
  92.4 2.5 collective-permute-start.13
  97.5 11.0 %collective-permute-start.66 = (bf16[8,64,1024]{2,1,0:T(8,128)(2,1)}, bf16[8,64,1024]{2,1,0:T(8,128)(2,1)S(1)}, u32[]{:S(2)}, u32[]{:S(2)}) collective-permute-start(bf16[8,64,1024]{2,1,0:T(8,128)(2,1)} %collective-permute-done.65), channel_id=1, source_target_pairs={{0,1},{1,0},{2,3},{3,2},{4,5},{5,4},{6,7},{7,6},{8,9},{9,8},{10,11... | collective-permute-start | bytes 3145736 | tf_op jit(solution)/shard_map/ppermute | solution.py:58
  111.0 5.0 collective-permute-start.9
  123.9 2.3 copy-done.1
  134.6 2.4 copy-done.2
  142.7 14.7 %collective-permute-done.76 = bf16[512,512]{0,1:T(8,128)(2,1)S(1)} collective-permute-done((bf16[512,512]{0,1:T(8,128)(2,1)S(1)}, bf16[512,512]{0,1:T(8,128)(2,1)S(1)}, u32[]{:S(2)}, u32[]{:S(2)}) %collective-permute-start.76) | collective-permute-done | bytes 524320 | tf_op jit(solution)/shard_map/ppermute | solution.py:58
  160.7 7.9 %collective-permute-done.73 = bf16[512,512]{0,1:T(8,128)(2,1)S(1)} collective-permute-done((bf16[512,512]{0,1:T(8,128)(2,1)S(1)}, bf16[512,512]{0,1:T(8,128)(2,1)S(1)}, u32[]{:S(2)}, u32[]{:S(2)}) %collective-permute-start.73) | collective-permute-done | bytes 524320 | tf_op jit(solution)/shard_map/ppermute | solution.py:58
  172.2 7.6 %collective-permute-done.75 = bf16[512,512]{0,1:T(8,128)(2,1)S(1)} collective-permute-done((bf16[512,512]{0,1:T(8,128)(2,1)S(1)}, bf16[512,512]{0,1:T(8,128)(2,1)S(1)}, u32[]{:S(2)}, u32[]{:S(2)}) %collective-permute-start.75) | collective-permute-done | bytes 524320 | tf_op jit(solution)/shard_map/ppermute | solution.py:58
  184.1 2.5 collective-permute-done.20
  189.9 22.0 %collective-permute-done.72 = bf16[512,512]{0,1:T(8,128)(2,1)S(1)} collective-permute-done((bf16[512,512]{0,1:T(8,128)(2,1)S(1)}, bf16[512,512]{0,1:T(8,128)(2,1)S(1)}, u32[]{:S(2)}, u32[]{:S(2)}) %collective-permute-start.72) | collective-permute-done | bytes 524320 | tf_op jit(solution)/shard_map/ppermute | solution.py:58
  216.7 11.0 %collective-permute-done.21 = bf16[512,640]{1,0:T(8,128)(2,1)S(1)} collective-permute-done((bf16[512,640]{1,0:T(8,128)(2,1)S(1)}, bf16[512,640]{1,0:T(8,128)(2,1)S(1)}, u32[]{:S(2)}, u32[]{:S(2)}) %collective-permute-start.21) | collective-permute-done | bytes 655392 | tf_op jit(solution)/shard_map/ppermute | solution.py:58
  231.8 2.9 collective-permute-start.22
  240.3 5.2 fusion.163
  245.5 3.7 convolution_convert_fusion.18
  249.2 2.5 collective-permute-start.26
  251.6 2.7 fusion.131
  254.4 7.2 %fusion.15 = f32[512,4,128]{2,0,1:T(8,128)S(1)} fusion(f32[512,512,4]{1,0,2:T(8,128)} %fusion.131, bf16[512,64]{1,0:T(8,128)(2,1)} %get-tuple-element.64, bf16[512,64]{1,0:T(8,128)(2,1)} %get-tuple-element.65, f32[4,512,512]{1,2,0:T(8,128)} %get-tuple-element.67, f32[4,512]{1,0:T(4,128)S(1)} %get-tuple-element.66), kind=kOutput, calls=%fused_computation.42 | convolution fusion | flops 276040192 | bytes 9576448 | tf_op jit(solution)/shard_map/hqk,kd->qhd/dot_general | solution.py:232
  261.6 9.0 %fusion.46 = f32[512,128]{1,0:T(8,128)} fusion(f32[512,512,4]{1,0,2:T(8,128)} %fusion.131, bf16[512,4,64]{2,0,1:T(8,128)(2,1)} %copy-done.21, bf16[512,4,64]{2,0,1:T(8,128)(2,1)} %copy-done.20, f32[4,512,512]{1,2,0:T(8,128)} %get-tuple-element.67, f32[4,512]{1,0:T(4,128)S(1)} %get-tuple-element.66), kind=kOutput, calls=%fused_computation.78 | convolution fusion | flops 276826624 | bytes 9183232 | tf_op jit(solution)/shard_map/hqk,qhd->kd/dot_general | solution.py:234
  270.6 3.1 fusion.55
  281.4 3.0 collective-permute-start.25
  287.1 8.2 %collective-permute-done.25 = bf16[512,512]{0,1:T(8,128)(2,1)} collective-permute-done((bf16[512,512]{0,1:T(8,128)(2,1)}, bf16[512,512]{0,1:T(8,128)(2,1)}, u32[]{:S(2)}, u32[]{:S(2)}) %collective-permute-start.25) | collective-permute-done | bytes 524320 | tf_op jit(solution)/shard_map/ppermute | solution.py:58
  295.3 3.4 collective-permute-start.28
  298.7 2.7 collective-permute-start.85
  303.3 6.4 %collective-permute-done.24 = bf16[512,512]{0,1:T(8,128)(2,1)} collective-permute-done((bf16[512,512]{0,1:T(8,128)(2,1)}, bf16[512,512]{0,1:T(8,128)(2,1)}, u32[]{:S(2)}, u32[]{:S(2)}) %collective-permute-start.24) | collective-permute-done | bytes 524320 | tf_op jit(solution)/shard_map/ppermute | solution.py:58
  315.0 5.9 %collective-permute-done.27 = bf16[512,512]{0,1:T(8,128)(2,1)} collective-permute-done((bf16[512,512]{0,1:T(8,128)(2,1)}, bf16[512,512]{0,1:T(8,128)(2,1)}, u32[]{:S(2)}, u32[]{:S(2)}) %collective-permute-start.27) | collective-permute-done | bytes 524320 | tf_op jit(solution)/shard_map/ppermute | solution.py:58
  324.8 2.7 collective-permute-start.29
  330.1 4.8 collective-permute-done.81
  338.6 10.3 %collective-permute-done.84 = bf16[512,640]{0,1:T(8,128)(2,1)S(1)} collective-permute-done((bf16[512,640]{0,1:T(8,128)(2,1)S(1)}, bf16[512,640]{0,1:T(8,128)(2,1)S(1)}, u32[]{:S(2)}, u32[]{:S(2)}) %collective-permute-start.84) | collective-permute-done | bytes 655392 | tf_op jit(solution)/shard_map/ppermute | solution.py:58
  351.6 6.5 %copy.84 = bf16[4096,512]{1,0:T(8,128)(2,1)} copy(bf16[4096,512]{0,1:T(8,128)(2,1)} %constant_dynamic-update-slice_fusion.4) | data formatting | bytes 8388608 | tf_op jit(solution)/shard_map/concatenate | solution.py:224
  358.1 3.1 convolution_convert_fusion.7
  361.2 2.6 collective-permute-start.32
  363.8 2.9 convolution_convert_fusion.8
  374.7 7.8 %copy.139 = bf16[4096,640]{1,0:T(8,128)(2,1)} copy(bf16[4096,640]{0,1:T(8,128)(2,1)} %constant_dynamic-update-slice_fusion.14) | data formatting | bytes 10485760 | tf_op jit(solution)/shard_map/reshape | solution.py:139
  382.6 2.5 convolution_convert_fusion.3
  397.8 2.7 collective-permute-start.33
  405.7 5.6 collective-permute-done.38
  413.2 9.3 %collective-permute-done.95 = bf16[512,512]{1,0:T(8,128)(2,1)S(1)} collective-permute-done((bf16[512,512]{1,0:T(8,128)(2,1)S(1)}, bf16[512,512]{1,0:T(8,128)(2,1)S(1)}, u32[]{:S(2)}, u32[]{:S(2)}) %collective-permute-start.95) | collective-permute-done | bytes 524320 | tf_op jit(solution)/shard_map/ppermute | solution.py:58
  422.5 11.0 %collective-permute-done.90 = bf16[512,512]{1,0:T(8,128)(2,1)S(1)} collective-permute-done((bf16[512,512]{1,0:T(8,128)(2,1)S(1)}, bf16[512,512]{1,0:T(8,128)(2,1)S(1)}, u32[]{:S(2)}, u32[]{:S(2)}) %collective-permute-start.90) | collective-permute-done | bytes 524320 | tf_op jit(solution)/shard_map/ppermute | solution.py:58
  433.5 3.4 collective-permute-start.34
  438.9 6.1 %collective-permute-done.39 = bf16[512,512]{1,0:T(8,128)(2,1)S(1)} collective-permute-done((bf16[512,512]{1,0:T(8,128)(2,1)S(1)}, bf16[512,512]{1,0:T(8,128)(2,1)S(1)}, u32[]{:S(2)}, u32[]{:S(2)}) %collective-permute-start.39) | collective-permute-done | bytes 524320 | tf_op jit(solution)/shard_map/ppermute | solution.py:58
  446.5 3.4 collective-permute-start.91
  452.1 5.6 collective-permute-done.94
  457.8 9.7 %collective-permute-done.96 = bf16[512,512]{1,0:T(8,128)(2,1)S(1)} collective-permute-done((bf16[512,512]{1,0:T(8,128)(2,1)S(1)}, bf16[512,512]{1,0:T(8,128)(2,1)S(1)}, u32[]{:S(2)}, u32[]{:S(2)}) %collective-permute-start.96) | collective-permute-done | bytes 524320 | tf_op jit(solution)/shard_map/ppermute | solution.py:58
  472.2 5.4 collective-permute-start.41
  477.6 3.9 collective-permute-done.97
  484.5 4.6 collective-permute-start.43
  489.1 12.6 %collective-permute-start.49 = (bf16[512,512]{1,0:T(8,128)(2,1)}, bf16[512,512]{1,0:T(8,128)(2,1)S(1)}, u32[]{:S(2)}, u32[]{:S(2)}) collective-permute-start(bf16[512,512]{1,0:T(8,128)(2,1)} %collective-permute-done.41), channel_id=1, source_target_pairs={{0,2},{1,3},{2,0},{3,1},{4,6},{5,7},{6,4},{7,5},{8,10},{9,11},{10,... | collective-permute-start | bytes 1572872 | tf_op jit(solution)/shard_map/ppermute | solution.py:58
  501.7 10.2 %convolution_convert_fusion.1 = bf16[1024,512]{1,0:T(8,128)(2,1)} fusion(bf16[4096,1024]{1,0:T(8,128)(2,1)} %bitcast.377, bf16[4096,512]{0,1:T(8,128)(2,1)} %constant_dynamic-update-slice_fusion.4), kind=kOutput, calls=%fused_computation.26 | convolution fusion | flops 4295491584 | bytes 13631488 | tf_op jit(solution)/shard_map/tr,tc->rc/dot_general | solution.py:256
  511.9 4.0 collective-permute-start.42
  516.0 11.1 %collective-permute-start.47 = (bf16[512,512]{1,0:T(8,128)(2,1)}, bf16[512,512]{1,0:T(8,128)(2,1)S(1)}, u32[]{:S(2)}, u32[]{:S(2)}) collective-permute-start(bf16[512,512]{1,0:T(8,128)(2,1)} %collective-permute-done.41), channel_id=1, source_target_pairs={{0,12},{1,13},{2,14},{3,15},{4,0},{5,1},{6,2},{7,3},{8,4},{9,5},{1... | collective-permute-start | bytes 1572872 | tf_op jit(solution)/shard_map/ppermute | solution.py:58
  527.3 5.8 %collective-permute-start.45 = (bf16[512,512]{1,0:T(8,128)(2,1)S(1)}, bf16[512,512]{1,0:T(8,128)(2,1)S(1)}, u32[]{:S(2)}, u32[]{:S(2)}) collective-permute-start(bf16[512,512]{1,0:T(8,128)(2,1)S(1)} %collective-permute-done.43), channel_id=1, source_target_pairs={{0,4},{1,5},{2,6},{3,7},{4,8},{5,9},{6,10},{7,11},{8,12},{9,13},{1... | collective-permute-start | bytes 1572872 | tf_op jit(solution)/shard_map/ppermute | solution.py:58
  534.0 9.3 %convolution_convert_fusion = bf16[1024,640]{1,0:T(8,128)(2,1)S(1)} fusion(bf16[4096,1024]{1,0:T(8,128)(2,1)S(1)} %bitcast.376, bf16[4096,640]{0,1:T(8,128)(2,1)} %constant_dynamic-update-slice_fusion.14), kind=kOutput, calls=%fused_computation.25 | convolution fusion | flops 5369364480 | bytes 14942208 | tf_op jit(solution)/shard_map/tr,tc->rc/dot_general | solution.py:253
  547.1 9.7 %collective-permute-done.53 = bf16[512,512]{1,0:T(8,128)(2,1)S(1)} collective-permute-done((bf16[512,512]{1,0:T(8,128)(2,1)S(1)}, bf16[512,512]{1,0:T(8,128)(2,1)S(1)}, u32[]{:S(2)}, u32[]{:S(2)}) %collective-permute-start.53) | collective-permute-done | bytes 524320 | tf_op jit(solution)/shard_map/ppermute | solution.py:58
  560.7 9.0 %collective-permute-done.54 = bf16[512,512]{1,0:T(8,128)(2,1)S(1)} collective-permute-done((bf16[512,512]{1,0:T(8,128)(2,1)S(1)}, bf16[512,512]{1,0:T(8,128)(2,1)S(1)}, u32[]{:S(2)}, u32[]{:S(2)}) %collective-permute-start.54) | collective-permute-done | bytes 524320 | tf_op jit(solution)/shard_map/ppermute | solution.py:58
  573.7 2.7 copy-done.6
  (365 shorter events, 188.4 us)
Async XLA Ops:
  7.7 16.0 %collective-permute-start.58 = (bf16[64,1024]{1,0:T(8,128)(2,1)S(1)}, bf16[64,1024]{1,0:T(8,128)(2,1)S(1)}, u32[]{:S(2)}, u32[]{:S(2)}) collective-permute-start(bf16[64,1024]{1,0:T(8,128)(2,1)S(1)} %bitcast.437), channel_id=1, source_target_pairs={{0,32},{1,33},{2,34},{3,35},{4,36},{5,37},{6,38},{7,39},{8,40},{9,... | collective-permute-start | bytes 393224 | tf_op jit(solution)/shard_map/ppermute | solution.py:58
  43.0 23.2 %collective-permute-start.65 = (bf16[8,64,1024]{2,1,0:T(8,128)(2,1)}, bf16[8,64,1024]{2,1,0:T(8,128)(2,1)}, u32[]{:S(2)}, u32[]{:S(2)}) collective-permute-start(bf16[8,64,1024]{2,1,0:T(8,128)(2,1)} %bitcast_dynamic-update-slice_fusion.18), channel_id=1, source_target_pairs={{0,4},{1,5},{2,6},{3,7},{4,8},{5,9},{6,10},{7,11},{8,12},{9,13},{1... | collective-permute-start | bytes 3145736 | tf_op jit(solution)/shard_map/ppermute | solution.py:58
  45.3 36.3 %collective-permute-start.67 = (bf16[8,64,1024]{2,1,0:T(8,128)(2,1)}, bf16[8,64,1024]{2,1,0:T(8,128)(2,1)S(1)}, u32[]{:S(2)}, u32[]{:S(2)}) collective-permute-start(bf16[8,64,1024]{2,1,0:T(8,128)(2,1)} %bitcast_dynamic-update-slice_fusion.18), channel_id=1, source_target_pairs={{0,12},{1,13},{2,14},{3,15},{4,0},{5,1},{6,2},{7,3},{8,4},{9,5},{1... | collective-permute-start | bytes 3145736 | tf_op jit(solution)/shard_map/ppermute | solution.py:58
  50.1 38.6 %collective-permute-start.8 = (bf16[8,64,1024]{2,1,0:T(8,128)(2,1)}, bf16[8,64,1024]{2,1,0:T(8,128)(2,1)}, u32[]{:S(2)}, u32[]{:S(2)}) collective-permute-start(bf16[8,64,1024]{2,1,0:T(8,128)(2,1)} %bitcast_dynamic-update-slice_fusion.25), channel_id=1, source_target_pairs={{0,4},{1,5},{2,6},{3,7},{4,8},{5,9},{6,10},{7,11},{8,12},{9,13},{1... | collective-permute-start | bytes 3145736 | tf_op jit(solution)/shard_map/ppermute | solution.py:58
  50.5 40.4 %collective-permute-start.10 = (bf16[8,64,1024]{2,1,0:T(8,128)(2,1)}, bf16[8,64,1024]{2,1,0:T(8,128)(2,1)}, u32[]{:S(2)}, u32[]{:S(2)}) collective-permute-start(bf16[8,64,1024]{2,1,0:T(8,128)(2,1)} %bitcast_dynamic-update-slice_fusion.25), channel_id=1, source_target_pairs={{0,12},{1,13},{2,14},{3,15},{4,0},{5,1},{6,2},{7,3},{8,4},{9,5},{1... | collective-permute-start | bytes 3145736 | tf_op jit(solution)/shard_map/ppermute | solution.py:58
  52.7 39.6 %collective-permute-start.64 = (bf16[8,64,1024]{2,1,0:T(8,128)(2,1)}, bf16[8,64,1024]{2,1,0:T(8,128)(2,1)}, u32[]{:S(2)}, u32[]{:S(2)}) collective-permute-start(bf16[8,64,1024]{2,1,0:T(8,128)(2,1)} %bitcast_dynamic-update-slice_fusion.18), channel_id=1, source_target_pairs={{0,1},{1,0},{2,3},{3,2},{4,5},{5,4},{6,7},{7,6},{8,9},{9,8},{10,11... | collective-permute-start | bytes 3145736 | tf_op jit(solution)/shard_map/ppermute | solution.py:58
  66.2 31.3 %collective-permute-start.7 = (bf16[8,64,1024]{2,1,0:T(8,128)(2,1)}, bf16[8,64,1024]{2,1,0:T(8,128)(2,1)S(1)}, u32[]{:S(2)}, u32[]{:S(2)}) collective-permute-start(bf16[8,64,1024]{2,1,0:T(8,128)(2,1)} %bitcast_dynamic-update-slice_fusion.25), channel_id=1, source_target_pairs={{0,1},{1,0},{2,3},{3,2},{4,5},{5,4},{6,7},{7,6},{8,9},{9,8},{10,11... | collective-permute-start | bytes 3145736 | tf_op jit(solution)/shard_map/ppermute | solution.py:58
  81.6 28.3 %collective-permute-start.69 = (bf16[4,64,1024]{2,1,0:T(8,128)(2,1)S(1)}, bf16[4,64,1024]{2,1,0:T(8,128)(2,1)S(1)}, u32[]{:S(2)}, u32[]{:S(2)}) collective-permute-start(bf16[4,64,1024]{2,1,0:T(8,128)(2,1)S(1)} %slice.257), channel_id=1, source_target_pairs={{0,4},{1,5},{2,6},{3,7},{4,8},{5,9},{6,10},{7,11},{8,12},{9,13},{1... | collective-permute-start | bytes 1572872 | tf_op jit(solution)/shard_map/ppermute | solution.py:58
  88.7 27.4 %collective-permute-start.70 = (bf16[4,64,1024]{2,1,0:T(8,128)(2,1)S(1)}, bf16[4,64,1024]{2,1,0:T(8,128)(2,1)S(1)}, u32[]{:S(2)}, u32[]{:S(2)}) collective-permute-start(bf16[4,64,1024]{2,1,0:T(8,128)(2,1)S(1)} %slice.258), channel_id=1, source_target_pairs={{0,12},{1,13},{2,14},{3,15},{4,0},{5,1},{6,2},{7,3},{8,4},{9,5},{1... | collective-permute-start | bytes 1572872 | tf_op jit(solution)/shard_map/ppermute | solution.py:58
  90.9 20.1 %collective-permute-start.12 = (bf16[4,64,1024]{2,1,0:T(8,128)(2,1)S(1)}, bf16[4,64,1024]{2,1,0:T(8,128)(2,1)S(1)}, u32[]{:S(2)}, u32[]{:S(2)}) collective-permute-start(bf16[4,64,1024]{2,1,0:T(8,128)(2,1)S(1)} %slice.233), channel_id=1, source_target_pairs={{0,4},{1,5},{2,6},{3,7},{4,8},{5,9},{6,10},{7,11},{8,12},{9,13},{1... | collective-permute-start | bytes 1572872 | tf_op jit(solution)/shard_map/ppermute | solution.py:58
  92.4 23.8 %collective-permute-start.13 = (bf16[4,64,1024]{2,1,0:T(8,128)(2,1)S(1)}, bf16[4,64,1024]{2,1,0:T(8,128)(2,1)S(1)}, u32[]{:S(2)}, u32[]{:S(2)}) collective-permute-start(bf16[4,64,1024]{2,1,0:T(8,128)(2,1)S(1)} %slice.234), channel_id=1, source_target_pairs={{0,12},{1,13},{2,14},{3,15},{4,0},{5,1},{6,2},{7,3},{8,4},{9,5},{1... | collective-permute-start | bytes 1572872 | tf_op jit(solution)/shard_map/ppermute | solution.py:58
  97.5 19.3 %collective-permute-start.66 = (bf16[8,64,1024]{2,1,0:T(8,128)(2,1)}, bf16[8,64,1024]{2,1,0:T(8,128)(2,1)S(1)}, u32[]{:S(2)}, u32[]{:S(2)}) collective-permute-start(bf16[8,64,1024]{2,1,0:T(8,128)(2,1)} %collective-permute-done.65), channel_id=1, source_target_pairs={{0,1},{1,0},{2,3},{3,2},{4,5},{5,4},{6,7},{7,6},{8,9},{9,8},{10,11... | collective-permute-start | bytes 3145736 | tf_op jit(solution)/shard_map/ppermute | solution.py:58
  116.2 16.9 %collective-permute-start.71 = (bf16[8,64,1024]{2,1,0:T(8,128)(2,1)S(1)}, bf16[8,64,1024]{2,1,0:T(8,128)(2,1)S(1)}, u32[]{:S(2)}, u32[]{:S(2)}) collective-permute-start(bf16[8,64,1024]{2,1,0:T(8,128)(2,1)S(1)} %constant_dynamic-update-slice_fusion.12), channel_id=1, source_target_pairs={{0,1},{1,0},{2,3},{3,2},{4,5},{5,4},{6,7},{7,6},{8,9},{9,8},{10,11... | collective-permute-start | bytes 3145736 | tf_op jit(solution)/shard_map/ppermute | solution.py:58
  127.3 42.6 %collective-permute-start.16 = (bf16[512,640]{1,0:T(8,128)(2,1)S(1)}, bf16[512,640]{1,0:T(8,128)(2,1)S(1)}, u32[]{:S(2)}, u32[]{:S(2)}) collective-permute-start(bf16[512,640]{1,0:T(8,128)(2,1)S(1)} %convolution_convert_fusion.12), channel_id=1, source_target_pairs={{0,48},{1,49},{2,50},{3,51},{4,52},{5,53},{6,54},{7,55},{8,56},{9,... | collective-permute-start | bytes 1966088 | tf_op jit(solution)/shard_map/ppermute | solution.py:58
  128.8 29.9 %collective-permute-start.19 = (bf16[512,640]{1,0:T(8,128)(2,1)S(1)}, bf16[512,640]{1,0:T(8,128)(2,1)S(1)}, u32[]{:S(2)}, u32[]{:S(2)}) collective-permute-start(bf16[512,640]{1,0:T(8,128)(2,1)S(1)} %convolution_convert_fusion.10), channel_id=1, source_target_pairs={{0,16},{1,17},{2,18},{3,19},{4,20},{5,21},{6,22},{7,23},{8,24},{9,... | collective-permute-start | bytes 1966088 | tf_op jit(solution)/shard_map/ppermute | solution.py:58
  131.2 52.0 %collective-permute-start.18 = (bf16[512,640]{1,0:T(8,128)(2,1)S(1)}, bf16[512,640]{1,0:T(8,128)(2,1)S(1)}, u32[]{:S(2)}, u32[]{:S(2)}) collective-permute-start(bf16[512,640]{1,0:T(8,128)(2,1)S(1)} %convolution_convert_fusion.11), channel_id=1, source_target_pairs={{0,48},{1,49},{2,50},{3,51},{4,52},{5,53},{6,54},{7,55},{8,56},{9,... | collective-permute-start | bytes 1966088 | tf_op jit(solution)/shard_map/ppermute | solution.py:58
  137.8 30.7 %collective-permute-start.73 = (bf16[512,512]{0,1:T(8,128)(2,1)S(1)}, bf16[512,512]{0,1:T(8,128)(2,1)S(1)}, u32[]{:S(2)}, u32[]{:S(2)}) collective-permute-start(bf16[512,512]{0,1:T(8,128)(2,1)S(1)} %convolution_convert_fusion.16), channel_id=1, source_target_pairs={{0,48},{1,49},{2,50},{3,51},{4,52},{5,53},{6,54},{7,55},{8,56},{9,... | collective-permute-start | bytes 1572872 | tf_op jit(solution)/shard_map/ppermute | solution.py:58
  139.3 18.1 %collective-permute-start.76 = (bf16[512,512]{0,1:T(8,128)(2,1)S(1)}, bf16[512,512]{0,1:T(8,128)(2,1)S(1)}, u32[]{:S(2)}, u32[]{:S(2)}) collective-permute-start(bf16[512,512]{0,1:T(8,128)(2,1)S(1)} %convolution_convert_fusion.14), channel_id=1, source_target_pairs={{0,16},{1,17},{2,18},{3,19},{4,20},{5,21},{6,22},{7,23},{8,24},{9,... | collective-permute-start | bytes 1572872 | tf_op jit(solution)/shard_map/ppermute | solution.py:58
  157.4 22.4 %collective-permute-start.75 = (bf16[512,512]{0,1:T(8,128)(2,1)S(1)}, bf16[512,512]{0,1:T(8,128)(2,1)S(1)}, u32[]{:S(2)}, u32[]{:S(2)}) collective-permute-start(bf16[512,512]{0,1:T(8,128)(2,1)S(1)} %convolution_convert_fusion.15), channel_id=1, source_target_pairs={{0,48},{1,49},{2,50},{3,51},{4,52},{5,53},{6,54},{7,55},{8,56},{9,... | collective-permute-start | bytes 1572872 | tf_op jit(solution)/shard_map/ppermute | solution.py:58
  158.8 21.5 %collective-permute-start.77 = (bf16[512,512]{0,1:T(8,128)(2,1)S(1)}, bf16[512,512]{0,1:T(8,128)(2,1)S(1)}, u32[]{:S(2)}, u32[]{:S(2)}) collective-permute-start(bf16[512,512]{0,1:T(8,128)(2,1)S(1)} %fusion.43), channel_id=1, source_target_pairs={{0,16},{1,17},{2,18},{3,19},{4,20},{5,21},{6,22},{7,23},{8,24},{9,... | collective-permute-start | bytes 1572872 | tf_op jit(solution)/shard_map/ppermute | solution.py:58
  168.5 18.0 %collective-permute-start.20 = (bf16[512,640]{1,0:T(8,128)(2,1)S(1)}, bf16[512,640]{1,0:T(8,128)(2,1)S(1)}, u32[]{:S(2)}, u32[]{:S(2)}) collective-permute-start(bf16[512,640]{1,0:T(8,128)(2,1)S(1)} %fusion.21), channel_id=1, source_target_pairs={{0,16},{1,17},{2,18},{3,19},{4,20},{5,21},{6,22},{7,23},{8,24},{9,... | collective-permute-start | bytes 1966088 | tf_op jit(solution)/shard_map/ppermute | solution.py:58
  169.9 46.8 %collective-permute-start.15 = (bf16[512,640]{1,0:T(8,128)(2,1)S(1)}, bf16[512,640]{1,0:T(8,128)(2,1)S(1)}, u32[]{:S(2)}, u32[]{:S(2)}) collective-permute-start(bf16[512,640]{1,0:T(8,128)(2,1)S(1)} %convolution_convert_fusion.13), channel_id=1, source_target_pairs={{0,16},{1,17},{2,18},{3,19},{4,20},{5,21},{6,22},{7,23},{8,24},{9,... | collective-permute-start | bytes 1966088 | tf_op jit(solution)/shard_map/ppermute | solution.py:58
  179.8 32.1 %collective-permute-start.72 = (bf16[512,512]{0,1:T(8,128)(2,1)S(1)}, bf16[512,512]{0,1:T(8,128)(2,1)S(1)}, u32[]{:S(2)}, u32[]{:S(2)}) collective-permute-start(bf16[512,512]{0,1:T(8,128)(2,1)S(1)} %convolution_convert_fusion.17), channel_id=1, source_target_pairs={{0,16},{1,17},{2,18},{3,19},{4,20},{5,21},{6,22},{7,23},{8,24},{9,... | collective-permute-start | bytes 1572872 | tf_op jit(solution)/shard_map/ppermute | solution.py:58
  180.3 34.7 %collective-permute-start.74 = (bf16[512,512]{0,1:T(8,128)(2,1)S(1)}, bf16[512,512]{0,1:T(8,128)(2,1)S(1)}, u32[]{:S(2)}, u32[]{:S(2)}) collective-permute-start(bf16[512,512]{0,1:T(8,128)(2,1)S(1)} %fusion.42), channel_id=1, source_target_pairs={{0,48},{1,49},{2,50},{3,51},{4,52},{5,53},{6,54},{7,55},{8,56},{9,... | collective-permute-start | bytes 1572872 | tf_op jit(solution)/shard_map/ppermute | solution.py:58
  183.3 33.4 %collective-permute-start.17 = (bf16[512,640]{1,0:T(8,128)(2,1)S(1)}, bf16[512,640]{1,0:T(8,128)(2,1)S(1)}, u32[]{:S(2)}, u32[]{:S(2)}) collective-permute-start(bf16[512,640]{1,0:T(8,128)(2,1)S(1)} %fusion.19), channel_id=1, source_target_pairs={{0,48},{1,49},{2,50},{3,51},{4,52},{5,53},{6,54},{7,55},{8,56},{9,... | collective-permute-start | bytes 1966088 | tf_op jit(solution)/shard_map/ppermute | solution.py:58
  186.6 28.5 %collective-permute-start.78 = (bf16[512,512]{0,1:T(8,128)(2,1)S(1)}, bf16[512,512]{0,1:T(8,128)(2,1)S(1)}, u32[]{:S(2)}, u32[]{:S(2)}) collective-permute-start(bf16[512,512]{0,1:T(8,128)(2,1)S(1)} %fusion.45), channel_id=1, source_target_pairs={{0,64},{1,65},{2,66},{3,67},{4,68},{5,69},{6,70},{7,71},{8,72},{9,... | collective-permute-start | bytes 1572872 | tf_op jit(solution)/shard_map/ppermute | solution.py:58
  211.9 15.8 %collective-permute-start.21 = (bf16[512,640]{1,0:T(8,128)(2,1)S(1)}, bf16[512,640]{1,0:T(8,128)(2,1)S(1)}, u32[]{:S(2)}, u32[]{:S(2)}) collective-permute-start(bf16[512,640]{1,0:T(8,128)(2,1)S(1)} %fusion.20), channel_id=1, source_target_pairs={{0,64},{1,65},{2,66},{3,67},{4,68},{5,69},{6,70},{7,71},{8,72},{9,... | collective-permute-start | bytes 1966088 | tf_op jit(solution)/shard_map/ppermute | solution.py:58
  249.2 35.2 %collective-permute-start.23 = (bf16[512,512]{0,1:T(8,128)(2,1)}, bf16[512,512]{0,1:T(8,128)(2,1)}, u32[]{:S(2)}, u32[]{:S(2)}) collective-permute-start(bf16[512,512]{0,1:T(8,128)(2,1)} %bitcast.36), channel_id=1, source_target_pairs={{0,16},{1,17},{2,18},{3,19},{4,20},{5,21},{6,22},{7,23},{8,24},{9,... | collective-permute-start | bytes 1572872 | tf_op jit(solution)/shard_map/ppermute | solution.py:58
  249.2 35.2 %collective-permute-start.26 = (bf16[512,512]{0,1:T(8,128)(2,1)}, bf16[512,512]{0,1:T(8,128)(2,1)}, u32[]{:S(2)}, u32[]{:S(2)}) collective-permute-start(bf16[512,512]{0,1:T(8,128)(2,1)} %bitcast.36), channel_id=1, source_target_pairs={{0,64},{1,65},{2,66},{3,67},{4,68},{5,69},{6,70},{7,71},{8,72},{9,... | collective-permute-start | bytes 1572872 | tf_op jit(solution)/shard_map/ppermute | solution.py:58
  281.0 17.7 %collective-permute-start.80 = (bf16[512,640]{0,1:T(8,128)(2,1)}, bf16[512,640]{0,1:T(8,128)(2,1)}, u32[]{:S(2)}, u32[]{:S(2)}) collective-permute-start(bf16[512,640]{0,1:T(8,128)(2,1)} %get-tuple-element.50), channel_id=1, source_target_pairs={{0,16},{1,17},{2,18},{3,19},{4,20},{5,21},{6,22},{7,23},{8,24},{9,... | collective-permute-start | bytes 1966088 | tf_op jit(solution)/shard_map/ppermute | solution.py:58
  281.0 17.8 %collective-permute-start.83 = (bf16[512,640]{0,1:T(8,128)(2,1)}, bf16[512,640]{0,1:T(8,128)(2,1)S(1)}, u32[]{:S(2)}, u32[]{:S(2)}) collective-permute-start(bf16[512,640]{0,1:T(8,128)(2,1)} %get-tuple-element.50), channel_id=1, source_target_pairs={{0,64},{1,65},{2,66},{3,67},{4,68},{5,69},{6,70},{7,71},{8,72},{9,... | collective-permute-start | bytes 1966088 | tf_op jit(solution)/shard_map/ppermute | solution.py:58
  284.4 25.3 %collective-permute-start.24 = (bf16[512,512]{0,1:T(8,128)(2,1)}, bf16[512,512]{0,1:T(8,128)(2,1)}, u32[]{:S(2)}, u32[]{:S(2)}) collective-permute-start(bf16[512,512]{0,1:T(8,128)(2,1)} %collective-permute-done.23), channel_id=1, source_target_pairs={{0,16},{1,17},{2,18},{3,19},{4,20},{5,21},{6,22},{7,23},{8,24},{9,... | collective-permute-start | bytes 1572872 | tf_op jit(solution)/shard_map/ppermute | solution.py:58
  284.4 36.6 %collective-permute-start.27 = (bf16[512,512]{0,1:T(8,128)(2,1)}, bf16[512,512]{0,1:T(8,128)(2,1)}, u32[]{:S(2)}, u32[]{:S(2)}) collective-permute-start(bf16[512,512]{0,1:T(8,128)(2,1)} %collective-permute-done.26), channel_id=1, source_target_pairs={{0,16},{1,17},{2,18},{3,19},{4,20},{5,21},{6,22},{7,23},{8,24},{9,... | collective-permute-start | bytes 1572872 | tf_op jit(solution)/shard_map/ppermute | solution.py:58
  295.3 29.5 %collective-permute-start.28 = (bf16[512,512]{0,1:T(8,128)(2,1)}, bf16[512,512]{0,1:T(8,128)(2,1)S(1)}, u32[]{:S(2)}, u32[]{:S(2)}) collective-permute-start(bf16[512,512]{0,1:T(8,128)(2,1)} %collective-permute-done.26), channel_id=1, source_target_pairs={{0,48},{1,49},{2,50},{3,51},{4,52},{5,53},{6,54},{7,55},{8,56},{9,... | collective-permute-start | bytes 1572872 | tf_op jit(solution)/shard_map/ppermute | solution.py:58
  298.7 36.2 %collective-permute-start.81 = (bf16[512,640]{0,1:T(8,128)(2,1)}, bf16[512,640]{0,1:T(8,128)(2,1)S(1)}, u32[]{:S(2)}, u32[]{:S(2)}) collective-permute-start(bf16[512,640]{0,1:T(8,128)(2,1)} %collective-permute-done.80), channel_id=1, source_target_pairs={{0,16},{1,17},{2,18},{3,19},{4,20},{5,21},{6,22},{7,23},{8,24},{9,... | collective-permute-start | bytes 1966088 | tf_op jit(solution)/shard_map/ppermute | solution.py:58
  298.7 30.6 %collective-permute-start.85 = (bf16[512,640]{0,1:T(8,128)(2,1)S(1)}, bf16[512,640]{0,1:T(8,128)(2,1)}, u32[]{:S(2)}, u32[]{:S(2)}) collective-permute-start(bf16[512,640]{0,1:T(8,128)(2,1)S(1)} %collective-permute-done.83), channel_id=1, source_target_pairs={{0,48},{1,49},{2,50},{3,51},{4,52},{5,53},{6,54},{7,55},{8,56},{9,... | collective-permute-start | bytes 1966088 | tf_op jit(solution)/shard_map/ppermute | solution.py:58
  309.7 27.1 %collective-permute-start.82 = (bf16[512,640]{0,1:T(8,128)(2,1)}, bf16[512,640]{0,1:T(8,128)(2,1)S(1)}, u32[]{:S(2)}, u32[]{:S(2)}) collective-permute-start(bf16[512,640]{0,1:T(8,128)(2,1)} %get-tuple-element.50), channel_id=1, source_target_pairs={{0,48},{1,49},{2,50},{3,51},{4,52},{5,53},{6,54},{7,55},{8,56},{9,... | collective-permute-start | bytes 1966088 | tf_op jit(solution)/shard_map/ppermute | solution.py:58
  320.9 28.0 %collective-permute-start.84 = (bf16[512,640]{0,1:T(8,128)(2,1)S(1)}, bf16[512,640]{0,1:T(8,128)(2,1)S(1)}, u32[]{:S(2)}, u32[]{:S(2)}) collective-permute-start(bf16[512,640]{0,1:T(8,128)(2,1)S(1)} %collective-permute-done.83), channel_id=1, source_target_pairs={{0,16},{1,17},{2,18},{3,19},{4,20},{5,21},{6,22},{7,23},{8,24},{9,... | collective-permute-start | bytes 1966088 | tf_op jit(solution)/shard_map/ppermute | solution.py:58
  324.8 25.1 %collective-permute-start.29 = (bf16[512,512]{0,1:T(8,128)(2,1)S(1)}, bf16[512,512]{0,1:T(8,128)(2,1)S(1)}, u32[]{:S(2)}, u32[]{:S(2)}) collective-permute-start(bf16[512,512]{0,1:T(8,128)(2,1)S(1)} %collective-permute-done.28), channel_id=1, source_target_pairs={{0,48},{1,49},{2,50},{3,51},{4,52},{5,53},{6,54},{7,55},{8,56},{9,... | collective-permute-start | bytes 1572872 | tf_op jit(solution)/shard_map/ppermute | solution.py:58
  329.4 41.3 %collective-permute-start.86 = (bf16[512,640]{0,1:T(8,128)(2,1)}, bf16[512,640]{0,1:T(8,128)(2,1)}, u32[]{:S(2)}, u32[]{:S(2)}) collective-permute-start(bf16[512,640]{0,1:T(8,128)(2,1)} %collective-permute-done.85), channel_id=1, source_target_pairs={{0,48},{1,49},{2,50},{3,51},{4,52},{5,53},{6,54},{7,55},{8,56},{9,... | collective-permute-start | bytes 1966088 | tf_op jit(solution)/shard_map/ppermute | solution.py:58
  361.2 33.6 %collective-permute-start.32 = (bf16[1024,512]{1,0:T(8,128)(2,1)}, bf16[1024,512]{1,0:T(8,128)(2,1)}, u32[]{:S(2)}, u32[]{:S(2)}) collective-permute-start(bf16[1024,512]{1,0:T(8,128)(2,1)} %convolution_convert_fusion.7), channel_id=1, source_target_pairs={{0,1},{1,0},{2,3},{3,2},{4,5},{5,4},{6,7},{7,6},{8,9},{9,8},{10,11... | collective-permute-start | bytes 3145736 | tf_op jit(solution)/shard_map/ppermute | solution.py:58
  366.7 23.3 %collective-permute-start.31 = (bf16[1024,512]{1,0:T(8,128)(2,1)}, bf16[1024,512]{1,0:T(8,128)(2,1)}, u32[]{:S(2)}, u32[]{:S(2)}) collective-permute-start(bf16[1024,512]{1,0:T(8,128)(2,1)} %convolution_convert_fusion.8), channel_id=1, source_target_pairs={{0,1},{1,0},{2,3},{3,2},{4,5},{5,4},{6,7},{7,6},{8,9},{9,8},{10,11... | collective-permute-start | bytes 3145736 | tf_op jit(solution)/shard_map/ppermute | solution.py:58
  368.4 23.8 %collective-permute-start.35 = (bf16[1024,512]{1,0:T(8,128)(2,1)}, bf16[1024,512]{1,0:T(8,128)(2,1)}, u32[]{:S(2)}, u32[]{:S(2)}) collective-permute-start(bf16[1024,512]{1,0:T(8,128)(2,1)} %convolution_convert_fusion.6), channel_id=1, source_target_pairs={{0,1},{1,0},{2,3},{3,2},{4,5},{5,4},{6,7},{7,6},{8,9},{9,8},{10,11... | collective-permute-start | bytes 3145736 | tf_op jit(solution)/shard_map/ppermute | solution.py:58
  370.7 26.3 %collective-permute-start.30 = (bf16[1024,512]{1,0:T(8,128)(2,1)}, bf16[1024,512]{1,0:T(8,128)(2,1)S(1)}, u32[]{:S(2)}, u32[]{:S(2)}) collective-permute-start(bf16[1024,512]{1,0:T(8,128)(2,1)} %convolution_convert_fusion.9), channel_id=1, source_target_pairs={{0,1},{1,0},{2,3},{3,2},{4,5},{5,4},{6,7},{7,6},{8,9},{9,8},{10,11... | collective-permute-start | bytes 3145736 | tf_op jit(solution)/shard_map/ppermute | solution.py:58
  385.0 16.6 %collective-permute-start.89 = (bf16[1024,512]{1,0:T(8,128)(2,1)S(1)}, bf16[1024,512]{1,0:T(8,128)(2,1)S(1)}, u32[]{:S(2)}, u32[]{:S(2)}) collective-permute-start(bf16[1024,512]{1,0:T(8,128)(2,1)S(1)} %convolution_convert_fusion.3), channel_id=1, source_target_pairs={{0,1},{1,0},{2,3},{3,2},{4,5},{5,4},{6,7},{7,6},{8,9},{9,8},{10,11... | collective-permute-start | bytes 3145736 | tf_op jit(solution)/shard_map/ppermute | solution.py:58
  394.8 55.6 %collective-permute-start.87 = (bf16[1024,512]{1,0:T(8,128)(2,1)S(1)}, bf16[1024,512]{1,0:T(8,128)(2,1)S(1)}, u32[]{:S(2)}, u32[]{:S(2)}) collective-permute-start(bf16[1024,512]{1,0:T(8,128)(2,1)S(1)} %convolution_convert_fusion.5), channel_id=1, source_target_pairs={{0,1},{1,0},{2,3},{3,2},{4,5},{5,4},{6,7},{7,6},{8,9},{9,8},{10,11... | collective-permute-start | bytes 3145736 | tf_op jit(solution)/shard_map/ppermute | solution.py:58
  401.7 35.7 %collective-permute-start.37 = (bf16[512,512]{1,0:T(8,128)(2,1)S(1)}, bf16[512,512]{1,0:T(8,128)(2,1)S(1)}, u32[]{:S(2)}, u32[]{:S(2)}) collective-permute-start(bf16[512,512]{1,0:T(8,128)(2,1)S(1)} %slice.332), channel_id=1, source_target_pairs={{0,12},{1,13},{2,14},{3,15},{4,0},{5,1},{6,2},{7,3},{8,4},{9,5},{1... | collective-permute-start | bytes 1572872 | tf_op jit(solution)/shard_map/ppermute | solution.py:58
  403.3 19.3 %collective-permute-start.95 = (bf16[512,512]{1,0:T(8,128)(2,1)S(1)}, bf16[512,512]{1,0:T(8,128)(2,1)S(1)}, u32[]{:S(2)}, u32[]{:S(2)}) collective-permute-start(bf16[512,512]{1,0:T(8,128)(2,1)S(1)} %get-tuple-element.28), channel_id=1, source_target_pairs={{0,4},{1,5},{2,6},{3,7},{4,8},{5,9},{6,10},{7,11},{8,12},{9,13},{1... | collective-permute-start | bytes 1572872 | tf_op jit(solution)/shard_map/ppermute | solution.py:58
  411.3 22.2 %collective-permute-start.90 = (bf16[512,512]{1,0:T(8,128)(2,1)S(1)}, bf16[512,512]{1,0:T(8,128)(2,1)S(1)}, u32[]{:S(2)}, u32[]{:S(2)}) collective-permute-start(bf16[512,512]{1,0:T(8,128)(2,1)S(1)} %get-tuple-element.29), channel_id=1, source_target_pairs={{0,12},{1,13},{2,14},{3,15},{4,0},{5,1},{6,2},{7,3},{8,4},{9,5},{1... | collective-permute-start | bytes 1572872 | tf_op jit(solution)/shard_map/ppermute | solution.py:58
  411.7 25.7 %collective-permute-start.36 = (bf16[512,512]{1,0:T(8,128)(2,1)S(1)}, bf16[512,512]{1,0:T(8,128)(2,1)S(1)}, u32[]{:S(2)}, u32[]{:S(2)}) collective-permute-start(bf16[512,512]{1,0:T(8,128)(2,1)S(1)} %slice.333), channel_id=1, source_target_pairs={{0,4},{1,5},{2,6},{3,7},{4,8},{5,9},{6,10},{7,11},{8,12},{9,13},{1... | collective-permute-start | bytes 1572872 | tf_op jit(solution)/shard_map/ppermute | solution.py:58
  422.5 22.5 %collective-permute-start.39 = (bf16[512,512]{1,0:T(8,128)(2,1)S(1)}, bf16[512,512]{1,0:T(8,128)(2,1)S(1)}, u32[]{:S(2)}, u32[]{:S(2)}) collective-permute-start(bf16[512,512]{1,0:T(8,128)(2,1)S(1)} %fusion.60), channel_id=1, source_target_pairs={{0,4},{1,5},{2,6},{3,7},{4,8},{5,9},{6,10},{7,11},{8,12},{9,13},{1... | collective-permute-start | bytes 1572872 | tf_op jit(solution)/shard_map/ppermute | solution.py:58
  437.3 20.4 %collective-permute-start.94 = (bf16[512,512]{1,0:T(8,128)(2,1)S(1)}, bf16[512,512]{1,0:T(8,128)(2,1)S(1)}, u32[]{:S(2)}, u32[]{:S(2)}) collective-permute-start(bf16[512,512]{1,0:T(8,128)(2,1)S(1)} %slice.330), channel_id=1, source_target_pairs={{0,12},{1,13},{2,14},{3,15},{4,0},{5,1},{6,2},{7,3},{8,4},{9,5},{1... | collective-permute-start | bytes 1572872 | tf_op jit(solution)/shard_map/ppermute | solution.py:58
  437.4 20.3 %collective-permute-start.93 = (bf16[512,512]{1,0:T(8,128)(2,1)S(1)}, bf16[512,512]{1,0:T(8,128)(2,1)S(1)}, u32[]{:S(2)}, u32[]{:S(2)}) collective-permute-start(bf16[512,512]{1,0:T(8,128)(2,1)S(1)} %slice.331), channel_id=1, source_target_pairs={{0,4},{1,5},{2,6},{3,7},{4,8},{5,9},{6,10},{7,11},{8,12},{9,13},{1... | collective-permute-start | bytes 1572872 | tf_op jit(solution)/shard_map/ppermute | solution.py:58
  445.0 22.5 %collective-permute-start.96 = (bf16[512,512]{1,0:T(8,128)(2,1)S(1)}, bf16[512,512]{1,0:T(8,128)(2,1)S(1)}, u32[]{:S(2)}, u32[]{:S(2)}) collective-permute-start(bf16[512,512]{1,0:T(8,128)(2,1)S(1)} %fusion.56), channel_id=1, source_target_pairs={{0,4},{1,5},{2,6},{3,7},{4,8},{5,9},{6,10},{7,11},{8,12},{9,13},{1... | collective-permute-start | bytes 1572872 | tf_op jit(solution)/shard_map/ppermute | solution.py:58
  446.5 22.5 %collective-permute-start.91 = (bf16[512,512]{1,0:T(8,128)(2,1)S(1)}, bf16[512,512]{1,0:T(8,128)(2,1)S(1)}, u32[]{:S(2)}, u32[]{:S(2)}) collective-permute-start(bf16[512,512]{1,0:T(8,128)(2,1)S(1)} %fusion.58), channel_id=1, source_target_pairs={{0,12},{1,13},{2,14},{3,15},{4,0},{5,1},{6,2},{7,3},{8,4},{9,5},{1... | collective-permute-start | bytes 1572872 | tf_op jit(solution)/shard_map/ppermute | solution.py:58
  450.4 20.5 %collective-permute-start.40 = (bf16[512,512]{1,0:T(8,128)(2,1)S(1)}, bf16[512,512]{1,0:T(8,128)(2,1)S(1)}, u32[]{:S(2)}, u32[]{:S(2)}) collective-permute-start(bf16[512,512]{1,0:T(8,128)(2,1)S(1)} %select_convert_fusion.1), channel_id=1, source_target_pairs={{0,2},{1,3},{2,0},{3,1},{4,6},{5,7},{6,4},{7,5},{8,10},{9,11},{10,... | collective-permute-start | bytes 1572872 | tf_op jit(solution)/shard_map/ppermute | solution.py:58
  483.8 43.6 %collective-permute-start.98 = (bf16[512,512]{1,0:T(8,128)(2,1)S(1)}, bf16[512,512]{1,0:T(8,128)(2,1)S(1)}, u32[]{:S(2)}, u32[]{:S(2)}) collective-permute-start(bf16[512,512]{1,0:T(8,128)(2,1)S(1)} %add_convert_fusion.2), channel_id=1, source_target_pairs={{0,0},{1,1},{2,48},{3,49},{4,32},{5,33},{6,16},{7,17},{8,64},{9,65... | collective-permute-start | bytes 1572872 | tf_op jit(solution)/shard_map/ppermute | solution.py:68
  484.5 42.6 %collective-permute-start.43 = (bf16[512,512]{1,0:T(8,128)(2,1)}, bf16[512,512]{1,0:T(8,128)(2,1)S(1)}, u32[]{:S(2)}, u32[]{:S(2)}) collective-permute-start(bf16[512,512]{1,0:T(8,128)(2,1)} %collective-permute-done.41), channel_id=1, source_target_pairs={{0,4},{1,5},{2,6},{3,7},{4,8},{5,9},{6,10},{7,11},{8,12},{9,13},{1... | collective-permute-start | bytes 1572872 | tf_op jit(solution)/shard_map/ppermute | solution.py:58
  489.1 44.0 %collective-permute-start.49 = (bf16[512,512]{1,0:T(8,128)(2,1)}, bf16[512,512]{1,0:T(8,128)(2,1)S(1)}, u32[]{:S(2)}, u32[]{:S(2)}) collective-permute-start(bf16[512,512]{1,0:T(8,128)(2,1)} %collective-permute-done.41), channel_id=1, source_target_pairs={{0,2},{1,3},{2,0},{3,1},{4,6},{5,7},{6,4},{7,5},{8,10},{9,11},{10,... | collective-permute-start | bytes 1572872 | tf_op jit(solution)/shard_map/ppermute | solution.py:58
  511.9 33.1 %collective-permute-start.42 = (bf16[512,512]{1,0:T(8,128)(2,1)}, bf16[512,512]{1,0:T(8,128)(2,1)S(1)}, u32[]{:S(2)}, u32[]{:S(2)}) collective-permute-start(bf16[512,512]{1,0:T(8,128)(2,1)} %collective-permute-done.41), channel_id=1, source_target_pairs={{0,1},{1,0},{2,3},{3,2},{4,5},{5,4},{6,7},{7,6},{8,9},{9,8},{10,11... | collective-permute-start | bytes 1572872 | tf_op jit(solution)/shard_map/ppermute | solution.py:58
  516.0 43.0 %collective-permute-start.47 = (bf16[512,512]{1,0:T(8,128)(2,1)}, bf16[512,512]{1,0:T(8,128)(2,1)S(1)}, u32[]{:S(2)}, u32[]{:S(2)}) collective-permute-start(bf16[512,512]{1,0:T(8,128)(2,1)} %collective-permute-done.41), channel_id=1, source_target_pairs={{0,12},{1,13},{2,14},{3,15},{4,0},{5,1},{6,2},{7,3},{8,4},{9,5},{1... | collective-permute-start | bytes 1572872 | tf_op jit(solution)/shard_map/ppermute | solution.py:58
  527.0 32.7 %collective-permute-start.44 = (bf16[512,512]{1,0:T(8,128)(2,1)S(1)}, bf16[512,512]{1,0:T(8,128)(2,1)S(1)}, u32[]{:S(2)}, u32[]{:S(2)}) collective-permute-start(bf16[512,512]{1,0:T(8,128)(2,1)S(1)} %collective-permute-done.43), channel_id=1, source_target_pairs={{0,1},{1,0},{2,3},{3,2},{4,5},{5,4},{6,7},{7,6},{8,9},{9,8},{10,11... | collective-permute-start | bytes 1572872 | tf_op jit(solution)/shard_map/ppermute | solution.py:58
  527.3 18.7 %collective-permute-start.45 = (bf16[512,512]{1,0:T(8,128)(2,1)S(1)}, bf16[512,512]{1,0:T(8,128)(2,1)S(1)}, u32[]{:S(2)}, u32[]{:S(2)}) collective-permute-start(bf16[512,512]{1,0:T(8,128)(2,1)S(1)} %collective-permute-done.43), channel_id=1, source_target_pairs={{0,4},{1,5},{2,6},{3,7},{4,8},{5,9},{6,10},{7,11},{8,12},{9,13},{1... | collective-permute-start | bytes 1572872 | tf_op jit(solution)/shard_map/ppermute | solution.py:58
  533.1 23.6 %collective-permute-start.53 = (bf16[512,512]{1,0:T(8,128)(2,1)S(1)}, bf16[512,512]{1,0:T(8,128)(2,1)S(1)}, u32[]{:S(2)}, u32[]{:S(2)}) collective-permute-start(bf16[512,512]{1,0:T(8,128)(2,1)S(1)} %collective-permute-done.49), channel_id=1, source_target_pairs={{0,12},{1,13},{2,14},{3,15},{4,0},{5,1},{6,2},{7,3},{8,4},{9,5},{1... | collective-permute-start | bytes 1572872 | tf_op jit(solution)/shard_map/ppermute | solution.py:58
  (61 other events, 1132.9 us)

commit v2 on v1

--- a/solution.py
+++ b/solution.py
@@ -3,6 +3,8 @@
 import jax
 import jax.numpy as jnp
 from jax import lax
+from jax.experimental import pallas as pl
+from jax.experimental.pallas import tpu as pltpu
 from jax.sharding import PartitionSpec as P
 
 HEAD_SIZE = 128
@@ -80,44 +82,229 @@
     return jnp.einsum("tc,dc->td", left, right, preferred_element_type=jnp.float32)
 
 
-def column_block(rows, place):
-    h, x, z, _, core = place
-    height = rows.shape[0] // 8
-    width = rows.shape[1] // 8
-    mine = lax.dynamic_slice(rows, ((z * 2 + core) * height, 0), (height, rows.shape[1]))
-    mine = mine.reshape(height, 8, width)
-    pieces = []
-    for dh in range(2):
-        for dx in range(4):
-            target = (h ^ dh) * 4 + (x + dx) % 4
-            piece = lax.dynamic_index_in_dim(mine, target, 1, keepdims=False)
-            pieces.append(move(piece, dh=dh, dx=dx) if dh or dx else piece)
-    own = jnp.stack(pieces)
-    below = move(own, dz=1)
-    above = move(own, dz=-1)
-    far = jnp.concatenate([move(below[:4], dz=1), move(above[4:], dz=-1)])
-    buffer = jnp.zeros((8, 8, height, width), rows.dtype)
-    for dz, part in ((0, own), (-1, below), (1, above), (2, far)):
-        level = (z + dz) % 4
-        for other in range(2):
-            piece = move(part, dc=1) if other else part
-            at = level * 2 + (core ^ other)
-            buffer = lax.dynamic_update_slice(buffer, piece[:, None], (0, at, 0, 0))
-    return buffer.reshape(8, 8 * height, width)
-
-
-def reduce_blk(block, weight):
-    def term(dh, dx):
-        return product(block[dh * 4 + dx], weight)
-
-    first = move(low_bits(term(0, 2)), dx=-1)
-    second = move(low_bits(term(1, 2)), dx=1)
-    near_right = move(low_bits(term(1, 1)), dx=-1)
-    near_left = move(low_bits(term(0, 3)), dx=1)
-    sum_left = move(low_bits(term(0, 1) + first), dx=-1)
-    sum_right = move(low_bits(term(1, 3) + second), dx=1)
-    other = move(low_bits(term(1, 0) + near_right + sum_right), dh=1)
-    return term(0, 0) + near_left + sum_left + other
+MESH = pl.DeviceIdType.MESH
+BF16 = jnp.bfloat16
+F32 = jnp.float32
+MIB = 1 << 20
+
+
+def here():
+    blk, tp = lax.axis_index("blk"), lax.axis_index("tp")
+    return blk // 4, blk % 4, tp // 4, tp // 2 % 2, tp % 2
+
+
+def near(place, dh=0, dx=0, dz=0, dl=0, dc=0):
+    h, x, z, low, core = place
+    h, low, core = (h + dh) % 2, (low + dl) % 2, (core + dc) % 2
+    x, z = (x + dx + 4) % 4, (z + dz + 4) % 4
+    return h * 4 + x, z * 4 + low * 2 + core
+
+
+def greet(devices):
+    barrier = pltpu.get_barrier_semaphore()
+    for device in devices:
+        pl.semaphore_signal(barrier, inc=1, device_id=device, device_id_type=MESH)
+    pl.semaphore_wait(barrier, len(devices))
+
+
+def send(source, target, sems, device):
+    copy = pltpu.make_async_remote_copy(
+        src_ref=source,
+        dst_ref=target,
+        send_sem=sems[0],
+        recv_sem=sems[1],
+        device_id=device,
+        device_id_type=MESH,
+    )
+    copy.start()
+    return copy
+
+
+def arrived(ref, sem):
+    pltpu.make_async_copy(ref, ref, sem).wait()
+
+
+CHUNKS = ((0, 2), (1, 2), (1, 1), (0, 3), (0, 1), (1, 3), (1, 0), (0, 0))
+
+
+def project_kernel(
+    tokens, cot, in_weight, o_weight, token_out, cot_out, proj_out, d_attn_out,
+    blocks, proj_send, proj_recv, cot_send, cot_recv,
+    a2a_s, a2a_r, up_s, up_r, down_s, down_r, far_s, far_r, core_s, core_r, sum_s, sum_r, keep,
+):
+    place = here()
+    h, x, z, low, core = place
+    seat = z * 2 + core
+    height = blocks.shape[2] // 8
+    width = blocks.shape[3]
+    right, left = near(place, dx=1), near(place, dx=-1)
+    above, below = near(place, dz=1), near(place, dz=-1)
+    twin, across = near(place, dc=1), near(place, dh=1)
+    shifts = [shift for shift in CHUNKS if shift != (0, 0)]
+    greet([near(place, dh=dh, dx=dx) for dh, dx in shifts] + [above, below, twin])
+    sent = []
+
+    def rows(a, dh, dx, at):
+        return blocks.at[a, dh * 4 + dx, pl.ds(pl.multiple_of(at * height, height), height)]
+
+    def level(dz):
+        return (z + dz + 4) % 4 * 2 + core
+
+    def index(dh, dx):
+        return dh * 4 + dx
+
+    def start_blocks(a, source):
+        for dh, dx in CHUNKS:
+            target = near(place, dh=dh, dx=dx)
+            piece = source.at[
+                pl.ds(pl.multiple_of(seat * height, height), height),
+                pl.ds(pl.multiple_of(target[0] * width, width), width),
+            ]
+            j = index(dh, dx)
+            if j:
+                sent.append(send(piece, rows(a, dh, dx, seat), (a2a_s.at[a, j], a2a_r.at[a, j]), target))
+            else:
+                pltpu.make_async_copy(piece, rows(a, 0, 0, seat), a2a_r.at[a, 0]).start()
+
+    def to_twin(a, dh, dx, which, at):
+        j = index(dh, dx)
+        piece = rows(a, dh, dx, at)
+        sent.append(send(piece, piece, (core_s.at[a, j, which], core_r.at[a, j, which]), twin))
+
+    def first_stage(a, dh, dx):
+        j = index(dh, dx)
+        piece = rows(a, dh, dx, seat)
+        arrived(piece, a2a_r.at[a, j])
+        sent.append(send(piece, piece, (up_s.at[a, j], up_r.at[a, j]), above))
+        sent.append(send(piece, piece, (down_s.at[a, j], down_r.at[a, j]), below))
+        to_twin(a, dh, dx, 0, seat)
+
+    def second_stage(a, dh, dx):
+        j = index(dh, dx)
+        sems = (far_s.at[a, j], far_r.at[a, j])
+        lower, upper = rows(a, dh, dx, level(-1)), rows(a, dh, dx, level(1))
+        arrived(lower, up_r.at[a, j])
+        if dh == 0:
+            sent.append(send(lower, lower, sems, above))
+        to_twin(a, dh, dx, 1, level(-1))
+        arrived(upper, down_r.at[a, j])
+        if dh == 1:
+            sent.append(send(upper, upper, sems, below))
+        to_twin(a, dh, dx, 2, level(1))
+
+    def third_stage(a, dh, dx):
+        j = index(dh, dx)
+        arrived(rows(a, dh, dx, level(2)), far_r.at[a, j])
+        to_twin(a, dh, dx, 3, level(2))
+
+    def complete(a, dh, dx):
+        j = index(dh, dx)
+        for which, dz in enumerate((0, -1, 1, 2)):
+            seat_there = (z + dz + 4) % 4 * 2 + (1 - core)
+            arrived(rows(a, dh, dx, seat_there), core_r.at[a, j, which])
+
+    weights = (in_weight, o_weight)
+    outgoing = (proj_send, cot_send)
+    incoming = (proj_recv, cot_recv)
+    results = (proj_out, d_attn_out)
+    adds = {4: (0,), 5: (1,), 6: (2, 5), 7: (3, 4, 6)}
+    ways = (left, right, left, right, left, right, across)
+
+    def chunk(a, k):
+        dh, dx = CHUNKS[k]
+        j = index(dh, dx)
+        third_stage(a, dh, dx)
+        complete(a, dh, dx)
+        terms = adds.get(k, ())
+        for term in terms:
+            arrived(incoming[a].at[term], sum_r.at[a, term])
+        target = outgoing[a].at[k] if k < 7 else results[a]
+        tile = blocks.shape[2] // 2
+
+        @pl.loop(0, 2)
+        def _(step):
+            part = pl.ds(pl.multiple_of(step * tile, tile), tile)
+            total = jnp.dot(blocks[a, j, part, :], weights[a][...], preferred_element_type=F32)
+            for term in terms:
+                total = total + incoming[a][term, part, :].astype(F32)
+            target[part, :] = total.astype(target.dtype)
+
+        if k < 7:
+            sent.append(send(target, incoming[a].at[k], (sum_s.at[a, k], sum_r.at[a, k]), ways[k]))
+
+    start_blocks(0, tokens)
+    start_blocks(1, cot)
+    for shift in CHUNKS:
+        first_stage(0, *shift)
+    for shift in CHUNKS:
+        second_stage(0, *shift)
+    for shift in CHUNKS:
+        first_stage(1, *shift)
+    for k in range(6):
+        chunk(0, k)
+        second_stage(1, *CHUNKS[k])
+    for k in (6, 7):
+        second_stage(1, *CHUNKS[k])
+    for k in range(4):
+        chunk(1, k)
+    chunk(0, 6)
+    for k in (4, 5):
+        chunk(1, k)
+    chunk(0, 7)
+    chunk(1, 6)
+    chunk(1, 7)
+    keeps = [
+        pltpu.make_async_copy(blocks.at[0], token_out, keep.at[0]),
+        pltpu.make_async_copy(blocks.at[1], cot_out, keep.at[1]),
+    ]
+    for copy in keeps:
+        copy.start()
+    for copy in sent:
+        copy.wait_send()
+    for copy in keeps:
+        copy.wait()
+
+
+def project(tokens, cot, in_weight, o_weight):
+    length = tokens.shape[0]
+    width = tokens.shape[1] // 8
+    in_width, o_width = in_weight.shape[1], o_weight.shape[1]
+    dma = pltpu.SemaphoreType.DMA
+    pair = [dma((2, 8)), dma((2, 8))]
+    block = jax.ShapeDtypeStruct((8, length, width), BF16)
+    return pl.pallas_call(
+        project_kernel,
+        out_shape=(
+            block,
+            block,
+            jax.ShapeDtypeStruct((length, in_width), F32),
+            jax.ShapeDtypeStruct((length, o_width), BF16),
+        ),
+        in_specs=[pl.BlockSpec(memory_space=pl.ANY)] * 2
+        + [pl.BlockSpec(memory_space=pltpu.VMEM)] * 2,
+        out_specs=(pl.BlockSpec(memory_space=pl.ANY),) * 2
+        + (pl.BlockSpec(memory_space=pltpu.VMEM),) * 2,
+        scratch_shapes=[
+            pltpu.VMEM((2, 8, length, width), BF16),
+            pltpu.VMEM((7, length, in_width), BF16),
+            pltpu.VMEM((7, length, in_width), BF16),
+            pltpu.VMEM((7, length, o_width), BF16),
+            pltpu.VMEM((7, length, o_width), BF16),
+            *pair,
+            *pair,
+            *pair,
+            *pair,
+            dma((2, 8, 4)),
+            dma((2, 8, 4)),
+            dma((2, 7)),
+            dma((2, 7)),
+            dma((2,)),
+        ],
+        compiler_params=pltpu.CompilerParams(
+            collective_id=0, has_side_effects=True, vmem_limit_bytes=56 * MIB
+        ),
+        name="project",
+    )(tokens, cot, in_weight, o_weight)
 
 
 def spread_ring(block, side, ring):
@@ -188,11 +375,8 @@
     blk, tp = lax.axis_index("blk"), lax.axis_index("tp")
     place = (blk // 4, blk % 4, tp // 4, tp // 2 % 2, tp % 2)
     core = place[4]
-    token_block = column_block(tokens, place)
-    cot_block = column_block(cotangent, place)
     in_weight = jnp.concatenate([q_weight, key_value_weight], axis=1)
-    projected = reduce_blk(token_block, in_weight)
-    d_attn = low_bits(reduce_blk(cot_block, o_weight))
+    token_block, cot_block, projected, d_attn = project(tokens, cotangent, in_weight, o_weight)
     cosine, sine = rope_tables(length, HEAD_SIZE)
     cos_heads = cosine[:, None, :]
     sin_heads = sine[:, None, :]

time: 587 us -> 509 us (0.87)
  the two profiles are of different devices: /device:TPU:1 before, /device:TPU:21 now
where the time goes in v2:
time: 509 us; the launch traced here: 502 us
  Pallas kernels  158 us (31%)
  waiting for transfers between devices  114 us (22%)
  starting transfers between devices  92.2 us (18%)
  matrix products  73.5 us (14%)
  local copies, waits for them, and re-layouts  50 us (10%)
  other arithmetic  12.8 us (3%)
    pallas_call x1, Pallas kernels, project(): pl.pallas_call(project_kernel, out_shape=(block, block, jax.ShapeDtypeStr...  158 us
    ppermute x53, waiting for transfers between devices, move(): return lax.ppermute(block, ('blk', 'tp'), route)  114 us
    ppermute x53, starting transfers between devices, move(): return lax.ppermute(block, ('blk', 'tp'), route)  70.4 us
    dot_general x16, matrix products, product_t(): jnp.einsum('tc,dc->td', left, right, preferred_element_type=jnp.float32)  27 us
    unnamed x63, local copies, waits for them, and re-layouts  23.5 us
    ppermute x2, starting transfers between devices, hand_over(): return lax.ppermute(block, ('blk', 'tp'), route)  21.9 us
    dot_general x1, matrix products, shards(): jnp.einsum('tr,tc->rc', cot_rows, attn_all, preferred_element_type=jnp.fl...  10.3 us
  transfers between devices with their start and end apart: 55, of which 23 were waited for; matrix products, arithmetic and copies ran while one was open for 19% of the time, Pallas kernels for 0%

profile of v2, /device:TPU:21, one launch (start us, length us, event | category | flops | bytes accessed | tf_op | source)
XLA Modules:
  0.0 501.8 jit_solution(11374202791885677504)
XLA Ops:
  4.0 157.5 %project.1 = (bf16[8,512,1024]{2,1,0:T(8,128)(2,1)}, bf16[8,512,1024]{2,1,0:T(8,128)(2,1)}, f32[512,640]{1,0:T(8,128)}, bf16[512,512]{1,0:T(8,128)(2,1)}) custom-call(bf16[512,8192]{1,0:T(8,128)(2,1)} %tokens.1, bf16[512,8192]{1,0:T(8,128)(2,1)} %cot.1, bf16[1024,640]{1,0:T(8,128)(2,1)} %copy-done.1, bf16[1024,512]{1,0:T(8,128)(2,1)} %o_weight.1), custom_call_target="tpu_custom_call" | custom-call | tf_op jit(solution)/shard_map/project/pallas_call | solution.py:275
  169.1 1.8 fusion.117
  170.9 2.8 fusion.118
  174.0 4.9 fusion.148
  178.9 7.0 %fusion.12 = f32[512,4,128]{2,0,1:T(8,128)S(1)} fusion(f32[512,512,4]{1,0,2:T(8,128)} %fusion.118, bf16[512,64]{1,0:T(8,128)(2,1)S(1)} %copy-done.18, bf16[512,64]{1,0:T(8,128)(2,1)S(1)} %copy-done.19, f32[4,512,512]{1,2,0:T(8,128)} %get-tuple-element.43, f32[4,512]{1,0:T(4,128)S(1)} %get-tuple-element.42), kind=kOutput, calls=%fused_computation.35 | convolution fusion | flops 276040192 | bytes 9576448 | tf_op jit(solution)/shard_map/hqk,kd->qhd/dot_general | solution.py:416
  185.9 7.9 %fusion.33 = f32[512,128]{1,0:T(8,128)S(1)} fusion(f32[512,512,4]{1,0,2:T(8,128)} %fusion.118, bf16[512,4,64]{2,0,1:T(8,128)(2,1)S(1)} %get-tuple-element.17, bf16[512,4,64]{2,0,1:T(8,128)(2,1)S(1)} %get-tuple-element.16, f32[4,512,512]{1,2,0:T(8,128)} %get-tuple-element.43, f32[4,512]{1,0:T(4,128)S(1)} %get-tuple-element.42), kind=kOutput, calls=%fused_computation.49 | convolution fusion | flops 276826624 | bytes 9183232 | tf_op jit(solution)/shard_map/hqk,qhd->kd/dot_general | solution.py:418
  193.9 3.0 fusion.42
  197.4 1.4 convolution_convert_fusion.10
  199.4 2.6 collective-permute-start.4
  206.9 2.8 collective-permute-start.36
  209.9 2.6 collective-permute-done.1
  214.2 2.7 collective-permute-start.5
  216.9 1.9 constant_dynamic-update-slice_fusion.9
  218.9 3.8 collective-permute-done.3
  223.5 3.0 collective-permute-done.36
  229.1 1.9 constant_dynamic-update-slice_fusion.8
  231.1 6.8 %collective-permute-done.2 = bf16[512,512]{0,1:T(8,128)(2,1)} collective-permute-done((bf16[512,512]{0,1:T(8,128)(2,1)}, bf16[512,512]{0,1:T(8,128)(2,1)}, u32[]{:S(2)}, u32[]{:S(2)}) %collective-permute-start.2) | collective-permute-done | bytes 524320 | tf_op jit(solution)/shard_map/ppermute | solution.py:60
  240.1 1.9 constant_dynamic-update-slice_fusion.7
  242.0 7.1 %collective-permute-done.5 = bf16[512,512]{0,1:T(8,128)(2,1)} collective-permute-done((bf16[512,512]{0,1:T(8,128)(2,1)S(1)}, bf16[512,512]{0,1:T(8,128)(2,1)}, u32[]{:S(2)}, u32[]{:S(2)}) %collective-permute-start.5) | collective-permute-done | bytes 524320 | tf_op jit(solution)/shard_map/ppermute | solution.py:60
  249.9 1.9 constant_dynamic-update-slice_fusion.6
  253.3 1.9 constant_dynamic-update-slice_fusion.4
  255.3 2.3 collective-permute-start.42
  257.6 5.4 %collective-permute-done.37 = bf16[512,640]{0,1:T(8,128)(2,1)S(1)} collective-permute-done((bf16[512,640]{0,1:T(8,128)(2,1)S(1)}, bf16[512,640]{0,1:T(8,128)(2,1)S(1)}, u32[]{:S(2)}, u32[]{:S(2)}) %collective-permute-start.37) | collective-permute-done | bytes 655392 | tf_op jit(solution)/shard_map/ppermute | solution.py:60
  265.7 11.4 %collective-permute-done.40 = bf16[512,640]{0,1:T(8,128)(2,1)S(1)} collective-permute-done((bf16[512,640]{0,1:T(8,128)(2,1)S(1)}, bf16[512,640]{0,1:T(8,128)(2,1)S(1)}, u32[]{:S(2)}, u32[]{:S(2)}) %collective-permute-start.40) | collective-permute-done | bytes 655392 | tf_op jit(solution)/shard_map/ppermute | solution.py:60
  279.7 6.6 %copy.48 = bf16[4096,512]{1,0:T(8,128)(2,1)} copy(bf16[4096,512]{0,1:T(8,128)(2,1)} %constant_dynamic-update-slice_fusion.2) | data formatting | bytes 8388608 | tf_op jit(solution)/shard_map/concatenate | solution.py:408
  286.3 3.1 convolution_convert_fusion.7
  290.3 2.9 convolution_convert_fusion.8
  293.2 1.7 convolution_convert_fusion.6
  295.4 1.7 convolution_convert_fusion.9
  298.9 8.0 %copy.81 = bf16[4096,640]{1,0:T(8,128)(2,1)} copy(bf16[4096,640]{0,1:T(8,128)(2,1)} %constant_dynamic-update-slice_fusion.10) | data formatting | bytes 10485760 | tf_op jit(solution)/shard_map/reshape | solution.py:326
  306.9 2.5 convolution_convert_fusion.3
  310.1 2.3 convolution_convert_fusion.2
  314.6 2.0 convert_add_fusion.4
  317.2 2.0 convert_add_fusion.3
  319.4 2.0 add_convert_fusion.1
  322.5 2.5 collective-permute-start.11
  330.0 5.8 %collective-permute-done.16 = bf16[512,512]{1,0:T(8,128)(2,1)S(1)} collective-permute-done((bf16[512,512]{1,0:T(8,128)(2,1)S(1)}, bf16[512,512]{1,0:T(8,128)(2,1)S(1)}, u32[]{:S(2)}, u32[]{:S(2)}) %collective-permute-start.16) | collective-permute-done | bytes 524320 | tf_op jit(solution)/shard_map/ppermute | solution.py:60
  337.7 9.4 %collective-permute-done.51 = bf16[512,512]{1,0:T(8,128)(2,1)S(1)} collective-permute-done((bf16[512,512]{1,0:T(8,128)(2,1)S(1)}, bf16[512,512]{1,0:T(8,128)(2,1)S(1)}, u32[]{:S(2)}, u32[]{:S(2)}) %collective-permute-start.51) | collective-permute-done | bytes 524320 | tf_op jit(solution)/shard_map/ppermute | solution.py:60
  347.0 11.0 %collective-permute-done.46 = bf16[512,512]{1,0:T(8,128)(2,1)S(1)} collective-permute-done((bf16[512,512]{1,0:T(8,128)(2,1)S(1)}, bf16[512,512]{1,0:T(8,128)(2,1)S(1)}, u32[]{:S(2)}, u32[]{:S(2)}) %collective-permute-start.46) | collective-permute-done | bytes 524320 | tf_op jit(solution)/shard_map/ppermute | solution.py:60
  358.0 3.4 collective-permute-start.12
  361.9 1.4 collective-permute-start.49
  363.4 6.1 %collective-permute-done.17 = bf16[512,512]{1,0:T(8,128)(2,1)S(1)} collective-permute-done((bf16[512,512]{1,0:T(8,128)(2,1)S(1)}, bf16[512,512]{1,0:T(8,128)(2,1)S(1)}, u32[]{:S(2)}, u32[]{:S(2)}) %collective-permute-start.17) | collective-permute-done | bytes 524320 | tf_op jit(solution)/shard_map/ppermute | solution.py:60
  369.5 1.5 collective-permute-done.12
  371.0 3.7 collective-permute-start.47
  375.1 1.8 collective-permute-start.18
  377.9 4.3 collective-permute-done.50
  382.3 9.7 %collective-permute-done.52 = bf16[512,512]{1,0:T(8,128)(2,1)S(1)} collective-permute-done((bf16[512,512]{1,0:T(8,128)(2,1)S(1)}, bf16[512,512]{1,0:T(8,128)(2,1)S(1)}, u32[]{:S(2)}, u32[]{:S(2)}) %collective-permute-start.52) | collective-permute-done | bytes 524320 | tf_op jit(solution)/shard_map/ppermute | solution.py:60
  392.0 1.5 collective-permute-done.47
  393.9 1.8 collective-permute-start.53
  397.0 5.3 %collective-permute-start.19 = (bf16[512,512]{1,0:T(8,128)(2,1)}, bf16[512,512]{1,0:T(8,128)(2,1)S(1)}, u32[]{:S(2)}, u32[]{:S(2)}) collective-permute-start(bf16[512,512]{1,0:T(8,128)(2,1)} %add_convert_fusion.4), channel_id=1, source_target_pairs={{0,0},{1,1},{2,48},{3,49},{4,32},{5,33},{6,16},{7,17},{8,64},{9,65... | collective-permute-start | bytes 1572872 | tf_op jit(solution)/shard_map/ppermute | solution.py:70
  402.5 2.9 collective-permute-done.53
  405.4 2.3 add_convert_fusion.2
  407.8 16.6 %collective-permute-start.54 = (bf16[512,512]{1,0:T(8,128)(2,1)S(1)}, bf16[512,512]{1,0:T(8,128)(2,1)S(1)}, u32[]{:S(2)}, u32[]{:S(2)}) collective-permute-start(bf16[512,512]{1,0:T(8,128)(2,1)S(1)} %add_convert_fusion.2), channel_id=1, source_target_pairs={{0,0},{1,1},{2,48},{3,49},{4,32},{5,33},{6,16},{7,17},{8,64},{9,65... | collective-permute-start | bytes 1572872 | tf_op jit(solution)/shard_map/ppermute | solution.py:70
  424.3 2.8 collective-permute-start.21
  427.2 10.3 %convolution_convert_fusion.1 = bf16[1024,512]{1,0:T(8,128)(2,1)} fusion(bf16[4096,1024]{1,0:T(8,128)(2,1)} %bitcast.215, bf16[4096,512]{0,1:T(8,128)(2,1)} %constant_dynamic-update-slice_fusion.2), kind=kOutput, calls=%fused_computation.26 | convolution fusion | flops 4295491584 | bytes 13631488 | tf_op jit(solution)/shard_map/tr,tc->rc/dot_general | solution.py:440
  437.5 4.9 collective-permute-start.20
  442.4 13.0 %collective-permute-start.25 = (bf16[512,512]{1,0:T(8,128)(2,1)S(1)}, bf16[512,512]{1,0:T(8,128)(2,1)S(1)}, u32[]{:S(2)}, u32[]{:S(2)}) collective-permute-start(bf16[512,512]{1,0:T(8,128)(2,1)S(1)} %collective-permute-done.19), channel_id=1, source_target_pairs={{0,12},{1,13},{2,14},{3,15},{4,0},{5,1},{6,2},{7,3},{8,4},{9,5},{1... | collective-permute-start | bytes 1572872 | tf_op jit(solution)/shard_map/ppermute | solution.py:60
  455.3 9.2 %collective-permute-done.21 = bf16[512,512]{1,0:T(8,128)(2,1)S(1)} collective-permute-done((bf16[512,512]{1,0:T(8,128)(2,1)S(1)}, bf16[512,512]{1,0:T(8,128)(2,1)S(1)}, u32[]{:S(2)}, u32[]{:S(2)}) %collective-permute-start.21) | collective-permute-done | bytes 524320 | tf_op jit(solution)/shard_map/ppermute | solution.py:60
  465.0 2.9 collective-permute-start.31
  467.9 9.3 %convolution_convert_fusion = bf16[1024,640]{1,0:T(8,128)(2,1)S(1)} fusion(bf16[4096,1024]{1,0:T(8,128)(2,1)S(1)} %bitcast.214, bf16[4096,640]{0,1:T(8,128)(2,1)} %constant_dynamic-update-slice_fusion.10), kind=kOutput, calls=%fused_computation.25 | convolution fusion | flops 5369364480 | bytes 14942208 | tf_op jit(solution)/shard_map/tr,tc->rc/dot_general | solution.py:437
  480.6 2.0 collective-permute-start.32
  485.3 7.8 %collective-permute-done.29 = bf16[512,512]{1,0:T(8,128)(2,1)S(1)} collective-permute-done((bf16[512,512]{1,0:T(8,128)(2,1)S(1)}, bf16[512,512]{1,0:T(8,128)(2,1)S(1)}, u32[]{:S(2)}, u32[]{:S(2)}) %collective-permute-start.29) | collective-permute-done | bytes 524320 | tf_op jit(solution)/shard_map/ppermute | solution.py:60
  493.1 1.4 collective-permute-start.34
  498.6 2.7 copy-done.5
  (195 shorter events, 61.2 us)
Async XLA Ops:
  162.5 5.2 %collective-permute-start = (bf16[512,128]{1,0:T(8,128)(2,1)S(1)}, bf16[512,128]{1,0:T(8,128)(2,1)S(1)}, u32[]{:S(2)}, u32[]{:S(2)}) collective-permute-start(bf16[512,128]{1,0:T(8,128)(2,1)S(1)} %slice.217), channel_id=1, source_target_pairs={{0,1},{1,0},{2,3},{3,2},{4,5},{5,4},{6,7},{7,6},{8,9},{9,8},{10,11... | collective-permute-start | bytes 393224 | tf_op jit(solution)/shard_map/ppermute | solution.py:60
  185.9 7.9 %copy-start.10 = (bf16[512,512]{0,1:T(8,128)(2,1)S(1)}, bf16[512,512]{0,1:T(8,128)(2,1)}, u32[]{:S(2)}) copy-start(bf16[512,512]{0,1:T(8,128)(2,1)} %copy-done.9) | copy-start | bytes 1572868
  197.4 7.1 %copy-start.8 = (f32[512,64]{1,0:T(8,128)S(1)}, f32[512,64]{1,0:T(8,128)}, u32[]{:S(2)}) copy-start(f32[512,64]{1,0:T(8,128)} %copy-done.7) | copy-start | bytes 393220
  198.8 13.8 %collective-permute-start.1 = (bf16[512,512]{0,1:T(8,128)(2,1)}, bf16[512,512]{0,1:T(8,128)(2,1)}, u32[]{:S(2)}, u32[]{:S(2)}) collective-permute-start(bf16[512,512]{0,1:T(8,128)(2,1)} %bitcast.5), channel_id=1, source_target_pairs={{0,16},{1,17},{2,18},{3,19},{4,20},{5,21},{6,22},{7,23},{8,24},{9,... | collective-permute-start | bytes 1572872 | tf_op jit(solution)/shard_map/ppermute | solution.py:60
  199.4 14.9 %collective-permute-start.4 = (bf16[512,512]{0,1:T(8,128)(2,1)}, bf16[512,512]{0,1:T(8,128)(2,1)S(1)}, u32[]{:S(2)}, u32[]{:S(2)}) collective-permute-start(bf16[512,512]{0,1:T(8,128)(2,1)} %bitcast.5), channel_id=1, source_target_pairs={{0,64},{1,65},{2,66},{3,67},{4,68},{5,69},{6,70},{7,71},{8,72},{9,... | collective-permute-start | bytes 1572872 | tf_op jit(solution)/shard_map/ppermute | solution.py:60
  203.4 2.1 collective-permute-start.35
  206.9 19.6 %collective-permute-start.36 = (bf16[512,640]{0,1:T(8,128)(2,1)}, bf16[512,640]{0,1:T(8,128)(2,1)S(1)}, u32[]{:S(2)}, u32[]{:S(2)}) collective-permute-start(bf16[512,640]{0,1:T(8,128)(2,1)} %get-tuple-element.26), channel_id=1, source_target_pairs={{0,16},{1,17},{2,18},{3,19},{4,20},{5,21},{6,22},{7,23},{8,24},{9,... | collective-permute-start | bytes 1966088 | tf_op jit(solution)/shard_map/ppermute | solution.py:60
  209.7 18.6 %collective-permute-start.39 = (bf16[512,640]{0,1:T(8,128)(2,1)}, bf16[512,640]{0,1:T(8,128)(2,1)S(1)}, u32[]{:S(2)}, u32[]{:S(2)}) collective-permute-start(bf16[512,640]{0,1:T(8,128)(2,1)} %get-tuple-element.26), channel_id=1, source_target_pairs={{0,64},{1,65},{2,66},{3,67},{4,68},{5,69},{6,70},{7,71},{8,72},{9,... | collective-permute-start | bytes 1966088 | tf_op jit(solution)/shard_map/ppermute | solution.py:60
  209.9 12.7 %collective-permute-start.3 = (bf16[512,512]{0,1:T(8,128)(2,1)}, bf16[512,512]{0,1:T(8,128)(2,1)S(1)}, u32[]{:S(2)}, u32[]{:S(2)}) collective-permute-start(bf16[512,512]{0,1:T(8,128)(2,1)} %bitcast.5), channel_id=1, source_target_pairs={{0,48},{1,49},{2,50},{3,51},{4,52},{5,53},{6,54},{7,55},{8,56},{9,... | collective-permute-start | bytes 1572872 | tf_op jit(solution)/shard_map/ppermute | solution.py:60
  212.6 25.3 %collective-permute-start.2 = (bf16[512,512]{0,1:T(8,128)(2,1)}, bf16[512,512]{0,1:T(8,128)(2,1)}, u32[]{:S(2)}, u32[]{:S(2)}) collective-permute-start(bf16[512,512]{0,1:T(8,128)(2,1)} %collective-permute-done.1), channel_id=1, source_target_pairs={{0,16},{1,17},{2,18},{3,19},{4,20},{5,21},{6,22},{7,23},{8,24},{9,... | collective-permute-start | bytes 1572872 | tf_op jit(solution)/shard_map/ppermute | solution.py:60
  214.2 34.8 %collective-permute-start.5 = (bf16[512,512]{0,1:T(8,128)(2,1)S(1)}, bf16[512,512]{0,1:T(8,128)(2,1)}, u32[]{:S(2)}, u32[]{:S(2)}) collective-permute-start(bf16[512,512]{0,1:T(8,128)(2,1)S(1)} %collective-permute-done.4), channel_id=1, source_target_pairs={{0,16},{1,17},{2,18},{3,19},{4,20},{5,21},{6,22},{7,23},{8,24},{9,... | collective-permute-start | bytes 1572872 | tf_op jit(solution)/shard_map/ppermute | solution.py:60
  222.7 30.1 %collective-permute-start.6 = (bf16[512,512]{0,1:T(8,128)(2,1)S(1)}, bf16[512,512]{0,1:T(8,128)(2,1)S(1)}, u32[]{:S(2)}, u32[]{:S(2)}) collective-permute-start(bf16[512,512]{0,1:T(8,128)(2,1)S(1)} %collective-permute-done.4), channel_id=1, source_target_pairs={{0,48},{1,49},{2,50},{3,51},{4,52},{5,53},{6,54},{7,55},{8,56},{9,... | collective-permute-start | bytes 1572872 | tf_op jit(solution)/shard_map/ppermute | solution.py:60
  226.5 36.5 %collective-permute-start.37 = (bf16[512,640]{0,1:T(8,128)(2,1)S(1)}, bf16[512,640]{0,1:T(8,128)(2,1)S(1)}, u32[]{:S(2)}, u32[]{:S(2)}) collective-permute-start(bf16[512,640]{0,1:T(8,128)(2,1)S(1)} %collective-permute-done.36), channel_id=1, source_target_pairs={{0,16},{1,17},{2,18},{3,19},{4,20},{5,21},{6,22},{7,23},{8,24},{9,... | collective-permute-start | bytes 1966088 | tf_op jit(solution)/shard_map/ppermute | solution.py:60
  228.3 27.0 %collective-permute-start.41 = (bf16[512,640]{0,1:T(8,128)(2,1)S(1)}, bf16[512,640]{0,1:T(8,128)(2,1)S(1)}, u32[]{:S(2)}, u32[]{:S(2)}) collective-permute-start(bf16[512,640]{0,1:T(8,128)(2,1)S(1)} %collective-permute-done.39), channel_id=1, source_target_pairs={{0,48},{1,49},{2,50},{3,51},{4,52},{5,53},{6,54},{7,55},{8,56},{9,... | collective-permute-start | bytes 1966088 | tf_op jit(solution)/shard_map/ppermute | solution.py:60
  237.8 26.1 %collective-permute-start.38 = (bf16[512,640]{0,1:T(8,128)(2,1)}, bf16[512,640]{0,1:T(8,128)(2,1)S(1)}, u32[]{:S(2)}, u32[]{:S(2)}) collective-permute-start(bf16[512,640]{0,1:T(8,128)(2,1)} %get-tuple-element.26), channel_id=1, source_target_pairs={{0,48},{1,49},{2,50},{3,51},{4,52},{5,53},{6,54},{7,55},{8,56},{9,... | collective-permute-start | bytes 1966088 | tf_op jit(solution)/shard_map/ppermute | solution.py:60
  249.1 28.0 %collective-permute-start.40 = (bf16[512,640]{0,1:T(8,128)(2,1)S(1)}, bf16[512,640]{0,1:T(8,128)(2,1)S(1)}, u32[]{:S(2)}, u32[]{:S(2)}) collective-permute-start(bf16[512,640]{0,1:T(8,128)(2,1)S(1)} %collective-permute-done.39), channel_id=1, source_target_pairs={{0,16},{1,17},{2,18},{3,19},{4,20},{5,21},{6,22},{7,23},{8,24},{9,... | collective-permute-start | bytes 1966088 | tf_op jit(solution)/shard_map/ppermute | solution.py:60
  252.7 25.2 %collective-permute-start.7 = (bf16[512,512]{0,1:T(8,128)(2,1)S(1)}, bf16[512,512]{0,1:T(8,128)(2,1)S(1)}, u32[]{:S(2)}, u32[]{:S(2)}) collective-permute-start(bf16[512,512]{0,1:T(8,128)(2,1)S(1)} %collective-permute-done.6), channel_id=1, source_target_pairs={{0,48},{1,49},{2,50},{3,51},{4,52},{5,53},{6,54},{7,55},{8,56},{9,... | collective-permute-start | bytes 1572872 | tf_op jit(solution)/shard_map/ppermute | solution.py:60
  255.3 41.9 %collective-permute-start.42 = (bf16[512,640]{0,1:T(8,128)(2,1)S(1)}, bf16[512,640]{0,1:T(8,128)(2,1)S(1)}, u32[]{:S(2)}, u32[]{:S(2)}) collective-permute-start(bf16[512,640]{0,1:T(8,128)(2,1)S(1)} %collective-permute-done.41), channel_id=1, source_target_pairs={{0,48},{1,49},{2,50},{3,51},{4,52},{5,53},{6,54},{7,55},{8,56},{9,... | collective-permute-start | bytes 1966088 | tf_op jit(solution)/shard_map/ppermute | solution.py:60
  279.6 6.6 %copy-start.6 = (bf16[1024,512]{1,0:T(8,128)(2,1)S(1)}, bf16[1024,512]{1,0:T(8,128)(2,1)}, u32[]{:S(2)}) copy-start(bf16[1024,512]{1,0:T(8,128)(2,1)} %o_weight.1) | copy-start | bytes 3145732
  286.3 6.9 %copy-start.3 = (bf16[4096,512]{1,0:T(8,128)(2,1)S(1)}, bf16[4096,512]{1,0:T(8,128)(2,1)}, u32[]{:S(2)}) copy-start(bf16[4096,512]{1,0:T(8,128)(2,1)} %copy.48) | copy-start | bytes 12582916
  289.4 29.9 %collective-permute-start.10 = (bf16[1024,512]{1,0:T(8,128)(2,1)}, bf16[1024,512]{1,0:T(8,128)(2,1)}, u32[]{:S(2)}, u32[]{:S(2)}) collective-permute-start(bf16[1024,512]{1,0:T(8,128)(2,1)} %convolution_convert_fusion.7), channel_id=1, source_target_pairs={{0,1},{1,0},{2,3},{3,2},{4,5},{5,4},{6,7},{7,6},{8,9},{9,8},{10,11... | collective-permute-start | bytes 3145736 | tf_op jit(solution)/shard_map/ppermute | solution.py:60
  293.2 21.3 %collective-permute-start.9 = (bf16[1024,512]{1,0:T(8,128)(2,1)}, bf16[1024,512]{1,0:T(8,128)(2,1)}, u32[]{:S(2)}, u32[]{:S(2)}) collective-permute-start(bf16[1024,512]{1,0:T(8,128)(2,1)} %convolution_convert_fusion.8), channel_id=1, source_target_pairs={{0,1},{1,0},{2,3},{3,2},{4,5},{5,4},{6,7},{7,6},{8,9},{9,8},{10,11... | collective-permute-start | bytes 3145736 | tf_op jit(solution)/shard_map/ppermute | solution.py:60
  294.9 21.8 %collective-permute-start.13 = (bf16[1024,512]{1,0:T(8,128)(2,1)}, bf16[1024,512]{1,0:T(8,128)(2,1)}, u32[]{:S(2)}, u32[]{:S(2)}) collective-permute-start(bf16[1024,512]{1,0:T(8,128)(2,1)} %convolution_convert_fusion.6), channel_id=1, source_target_pairs={{0,1},{1,0},{2,3},{3,2},{4,5},{5,4},{6,7},{7,6},{8,9},{9,8},{10,11... | collective-permute-start | bytes 3145736 | tf_op jit(solution)/shard_map/ppermute | solution.py:60
  297.1 24.3 %collective-permute-start.8 = (bf16[1024,512]{1,0:T(8,128)(2,1)}, bf16[1024,512]{1,0:T(8,128)(2,1)S(1)}, u32[]{:S(2)}, u32[]{:S(2)}) collective-permute-start(bf16[1024,512]{1,0:T(8,128)(2,1)} %convolution_convert_fusion.9), channel_id=1, source_target_pairs={{0,1},{1,0},{2,3},{3,2},{4,5},{5,4},{6,7},{7,6},{8,9},{9,8},{10,11... | collective-permute-start | bytes 3145736 | tf_op jit(solution)/shard_map/ppermute | solution.py:60
  298.9 8.0 %copy-start.2 = (bf16[1024,640]{1,0:T(8,128)(2,1)S(1)}, bf16[1024,640]{1,0:T(8,128)(2,1)}, u32[]{:S(2)}) copy-start(bf16[1024,640]{1,0:T(8,128)(2,1)} %copy-done.1) | copy-start | bytes 3932164
  309.3 16.8 %collective-permute-start.45 = (bf16[1024,512]{1,0:T(8,128)(2,1)S(1)}, bf16[1024,512]{1,0:T(8,128)(2,1)S(1)}, u32[]{:S(2)}, u32[]{:S(2)}) collective-permute-start(bf16[1024,512]{1,0:T(8,128)(2,1)S(1)} %convolution_convert_fusion.3), channel_id=1, source_target_pairs={{0,1},{1,0},{2,3},{3,2},{4,5},{5,4},{6,7},{7,6},{8,9},{9,8},{10,11... | collective-permute-start | bytes 3145736 | tf_op jit(solution)/shard_map/ppermute | solution.py:60
  314.5 13.3 %collective-permute-start.48 = (bf16[1024,512]{1,0:T(8,128)(2,1)S(1)}, bf16[1024,512]{1,0:T(8,128)(2,1)S(1)}, u32[]{:S(2)}, u32[]{:S(2)}) collective-permute-start(bf16[1024,512]{1,0:T(8,128)(2,1)S(1)} %convolution_convert_fusion.2), channel_id=1, source_target_pairs={{0,1},{1,0},{2,3},{3,2},{4,5},{5,4},{6,7},{7,6},{8,9},{9,8},{10,11... | collective-permute-start | bytes 3145736 | tf_op jit(solution)/shard_map/ppermute | solution.py:60
  316.7 5.8 %collective-permute-start.44 = (bf16[1024,512]{1,0:T(8,128)(2,1)S(1)}, bf16[1024,512]{1,0:T(8,128)(2,1)S(1)}, u32[]{:S(2)}, u32[]{:S(2)}) collective-permute-start(bf16[1024,512]{1,0:T(8,128)(2,1)S(1)} %convolution_convert_fusion.4), channel_id=1, source_target_pairs={{0,1},{1,0},{2,3},{3,2},{4,5},{5,4},{6,7},{7,6},{8,9},{9,8},{10,11... | collective-permute-start | bytes 3145736 | tf_op jit(solution)/shard_map/ppermute | solution.py:60
  319.3 55.8 %collective-permute-start.43 = (bf16[1024,512]{1,0:T(8,128)(2,1)S(1)}, bf16[1024,512]{1,0:T(8,128)(2,1)S(1)}, u32[]{:S(2)}, u32[]{:S(2)}) collective-permute-start(bf16[1024,512]{1,0:T(8,128)(2,1)S(1)} %convolution_convert_fusion.5), channel_id=1, source_target_pairs={{0,1},{1,0},{2,3},{3,2},{4,5},{5,4},{6,7},{7,6},{8,9},{9,8},{10,11... | collective-permute-start | bytes 3145736 | tf_op jit(solution)/shard_map/ppermute | solution.py:60
  321.5 14.3 %collective-permute-start.16 = (bf16[512,512]{1,0:T(8,128)(2,1)S(1)}, bf16[512,512]{1,0:T(8,128)(2,1)S(1)}, u32[]{:S(2)}, u32[]{:S(2)}) collective-permute-start(bf16[512,512]{1,0:T(8,128)(2,1)S(1)} %get-tuple-element.22), channel_id=1, source_target_pairs={{0,4},{1,5},{2,6},{3,7},{4,8},{5,9},{6,10},{7,11},{8,12},{9,13},{1... | collective-permute-start | bytes 1572872 | tf_op jit(solution)/shard_map/ppermute | solution.py:60
  322.5 14.0 %collective-permute-start.11 = (bf16[512,512]{1,0:T(8,128)(2,1)S(1)}, bf16[512,512]{1,0:T(8,128)(2,1)S(1)}, u32[]{:S(2)}, u32[]{:S(2)}) collective-permute-start(bf16[512,512]{1,0:T(8,128)(2,1)S(1)} %get-tuple-element.23), channel_id=1, source_target_pairs={{0,12},{1,13},{2,14},{3,15},{4,0},{5,1},{6,2},{7,3},{8,4},{9,5},{1... | collective-permute-start | bytes 1572872 | tf_op jit(solution)/shard_map/ppermute | solution.py:60
  326.2 35.7 %collective-permute-start.15 = (bf16[512,512]{1,0:T(8,128)(2,1)S(1)}, bf16[512,512]{1,0:T(8,128)(2,1)S(1)}, u32[]{:S(2)}, u32[]{:S(2)}) collective-permute-start(bf16[512,512]{1,0:T(8,128)(2,1)S(1)} %slice.215), channel_id=1, source_target_pairs={{0,12},{1,13},{2,14},{3,15},{4,0},{5,1},{6,2},{7,3},{8,4},{9,5},{1... | collective-permute-start | bytes 1572872 | tf_op jit(solution)/shard_map/ppermute | solution.py:60
  327.9 19.2 %collective-permute-start.51 = (bf16[512,512]{1,0:T(8,128)(2,1)S(1)}, bf16[512,512]{1,0:T(8,128)(2,1)S(1)}, u32[]{:S(2)}, u32[]{:S(2)}) collective-permute-start(bf16[512,512]{1,0:T(8,128)(2,1)S(1)} %get-tuple-element.20), channel_id=1, source_target_pairs={{0,4},{1,5},{2,6},{3,7},{4,8},{5,9},{6,10},{7,11},{8,12},{9,13},{1... | collective-permute-start | bytes 1572872 | tf_op jit(solution)/shard_map/ppermute | solution.py:60
  335.8 22.2 %collective-permute-start.46 = (bf16[512,512]{1,0:T(8,128)(2,1)S(1)}, bf16[512,512]{1,0:T(8,128)(2,1)S(1)}, u32[]{:S(2)}, u32[]{:S(2)}) collective-permute-start(bf16[512,512]{1,0:T(8,128)(2,1)S(1)} %get-tuple-element.21), channel_id=1, source_target_pairs={{0,12},{1,13},{2,14},{3,15},{4,0},{5,1},{6,2},{7,3},{8,4},{9,5},{1... | collective-permute-start | bytes 1572872 | tf_op jit(solution)/shard_map/ppermute | solution.py:60
  336.5 25.4 %collective-permute-start.14 = (bf16[512,512]{1,0:T(8,128)(2,1)S(1)}, bf16[512,512]{1,0:T(8,128)(2,1)S(1)}, u32[]{:S(2)}, u32[]{:S(2)}) collective-permute-start(bf16[512,512]{1,0:T(8,128)(2,1)S(1)} %slice.216), channel_id=1, source_target_pairs={{0,4},{1,5},{2,6},{3,7},{4,8},{5,9},{6,10},{7,11},{8,12},{9,13},{1... | collective-permute-start | bytes 1572872 | tf_op jit(solution)/shard_map/ppermute | solution.py:60
  347.0 22.5 %collective-permute-start.17 = (bf16[512,512]{1,0:T(8,128)(2,1)S(1)}, bf16[512,512]{1,0:T(8,128)(2,1)S(1)}, u32[]{:S(2)}, u32[]{:S(2)}) collective-permute-start(bf16[512,512]{1,0:T(8,128)(2,1)S(1)} %fusion.47), channel_id=1, source_target_pairs={{0,4},{1,5},{2,6},{3,7},{4,8},{5,9},{6,10},{7,11},{8,12},{9,13},{1... | collective-permute-start | bytes 1572872 | tf_op jit(solution)/shard_map/ppermute | solution.py:60
  358.0 13.0 %collective-permute-start.12 = (bf16[512,512]{1,0:T(8,128)(2,1)S(1)}, bf16[512,512]{1,0:T(8,128)(2,1)S(1)}, u32[]{:S(2)}, u32[]{:S(2)}) collective-permute-start(bf16[512,512]{1,0:T(8,128)(2,1)S(1)} %fusion.49), channel_id=1, source_target_pairs={{0,12},{1,13},{2,14},{3,15},{4,0},{5,1},{6,2},{7,3},{8,4},{9,5},{1... | collective-permute-start | bytes 1572872 | tf_op jit(solution)/shard_map/ppermute | solution.py:60
  361.8 20.4 %collective-permute-start.50 = (bf16[512,512]{1,0:T(8,128)(2,1)S(1)}, bf16[512,512]{1,0:T(8,128)(2,1)S(1)}, u32[]{:S(2)}, u32[]{:S(2)}) collective-permute-start(bf16[512,512]{1,0:T(8,128)(2,1)S(1)} %slice.213), channel_id=1, source_target_pairs={{0,12},{1,13},{2,14},{3,15},{4,0},{5,1},{6,2},{7,3},{8,4},{9,5},{1... | collective-permute-start | bytes 1572872 | tf_op jit(solution)/shard_map/ppermute | solution.py:60
  361.9 20.3 %collective-permute-start.49 = (bf16[512,512]{1,0:T(8,128)(2,1)S(1)}, bf16[512,512]{1,0:T(8,128)(2,1)S(1)}, u32[]{:S(2)}, u32[]{:S(2)}) collective-permute-start(bf16[512,512]{1,0:T(8,128)(2,1)S(1)} %slice.214), channel_id=1, source_target_pairs={{0,4},{1,5},{2,6},{3,7},{4,8},{5,9},{6,10},{7,11},{8,12},{9,13},{1... | collective-permute-start | bytes 1572872 | tf_op jit(solution)/shard_map/ppermute | solution.py:60
  369.5 22.5 %collective-permute-start.52 = (bf16[512,512]{1,0:T(8,128)(2,1)S(1)}, bf16[512,512]{1,0:T(8,128)(2,1)S(1)}, u32[]{:S(2)}, u32[]{:S(2)}) collective-permute-start(bf16[512,512]{1,0:T(8,128)(2,1)S(1)} %fusion.43), channel_id=1, source_target_pairs={{0,4},{1,5},{2,6},{3,7},{4,8},{5,9},{6,10},{7,11},{8,12},{9,13},{1... | collective-permute-start | bytes 1572872 | tf_op jit(solution)/shard_map/ppermute | solution.py:60
  371.0 22.5 %collective-permute-start.47 = (bf16[512,512]{1,0:T(8,128)(2,1)S(1)}, bf16[512,512]{1,0:T(8,128)(2,1)S(1)}, u32[]{:S(2)}, u32[]{:S(2)}) collective-permute-start(bf16[512,512]{1,0:T(8,128)(2,1)S(1)} %fusion.45), channel_id=1, source_target_pairs={{0,12},{1,13},{2,14},{3,15},{4,0},{5,1},{6,2},{7,3},{8,4},{9,5},{1... | collective-permute-start | bytes 1572872 | tf_op jit(solution)/shard_map/ppermute | solution.py:60
  375.1 20.6 %collective-permute-start.18 = (bf16[512,512]{1,0:T(8,128)(2,1)S(1)}, bf16[512,512]{1,0:T(8,128)(2,1)S(1)}, u32[]{:S(2)}, u32[]{:S(2)}) collective-permute-start(bf16[512,512]{1,0:T(8,128)(2,1)S(1)} %select_convert_fusion.1), channel_id=1, source_target_pairs={{0,2},{1,3},{2,0},{3,1},{4,6},{5,7},{6,4},{7,5},{8,10},{9,11},{10,... | collective-permute-start | bytes 1572872 | tf_op jit(solution)/shard_map/ppermute | solution.py:60
  382.2 14.8 %copy-start.11 = (bf16[512,512]{1,0:T(8,128)(2,1)}, bf16[512,512]{1,0:T(8,128)(2,1)S(1)}, u32[]{:S(2)}) copy-start(bf16[512,512]{1,0:T(8,128)(2,1)S(1)} %collective-permute-done.50) | copy-start | bytes 1572868
  382.3 14.8 %copy-start.12 = (bf16[512,512]{1,0:T(8,128)(2,1)}, bf16[512,512]{1,0:T(8,128)(2,1)S(1)}, u32[]{:S(2)}) copy-start(bf16[512,512]{1,0:T(8,128)(2,1)S(1)} %collective-permute-done.49) | copy-start | bytes 1572868
  393.9 11.5 %collective-permute-start.53 = (bf16[512,512]{1,0:T(8,128)(2,1)S(1)}, bf16[512,512]{1,0:T(8,128)(2,1)}, u32[]{:S(2)}, u32[]{:S(2)}) collective-permute-start(bf16[512,512]{1,0:T(8,128)(2,1)S(1)} %select_convert_fusion), channel_id=1, source_target_pairs={{0,2},{1,3},{2,0},{3,1},{4,6},{5,7},{6,4},{7,5},{8,10},{9,11},{10,... | collective-permute-start | bytes 1572872 | tf_op jit(solution)/shard_map/ppermute | solution.py:60
  397.0 27.3 %collective-permute-start.19 = (bf16[512,512]{1,0:T(8,128)(2,1)}, bf16[512,512]{1,0:T(8,128)(2,1)S(1)}, u32[]{:S(2)}, u32[]{:S(2)}) collective-permute-start(bf16[512,512]{1,0:T(8,128)(2,1)} %add_convert_fusion.4), channel_id=1, source_target_pairs={{0,0},{1,1},{2,48},{3,49},{4,32},{5,33},{6,16},{7,17},{8,64},{9,65... | collective-permute-start | bytes 1572872 | tf_op jit(solution)/shard_map/ppermute | solution.py:70
  405.4 62.5 %slice-start = ((s8[8388608]{0:T(1024)(128)(4,1)}), s8[4194304]{0:T(1024)(128)(4,1)S(1)}, s32[]{:S(2)}) async-start(s8[8388608]{0:T(1024)(128)(4,1)} %bitcast.212), calls=%async_computation | async-start | bytes 8388608
  407.8 57.2 %collective-permute-start.54 = (bf16[512,512]{1,0:T(8,128)(2,1)S(1)}, bf16[512,512]{1,0:T(8,128)(2,1)S(1)}, u32[]{:S(2)}, u32[]{:S(2)}) collective-permute-start(bf16[512,512]{1,0:T(8,128)(2,1)S(1)} %add_convert_fusion.2), channel_id=1, source_target_pairs={{0,0},{1,1},{2,48},{3,49},{4,32},{5,33},{6,16},{7,17},{8,64},{9,65... | collective-permute-start | bytes 1572872 | tf_op jit(solution)/shard_map/ppermute | solution.py:70
  424.3 40.2 %collective-permute-start.21 = (bf16[512,512]{1,0:T(8,128)(2,1)S(1)}, bf16[512,512]{1,0:T(8,128)(2,1)S(1)}, u32[]{:S(2)}, u32[]{:S(2)}) collective-permute-start(bf16[512,512]{1,0:T(8,128)(2,1)S(1)} %collective-permute-done.19), channel_id=1, source_target_pairs={{0,4},{1,5},{2,6},{3,7},{4,8},{5,9},{6,10},{7,11},{8,12},{9,13},{1... | collective-permute-start | bytes 1572872 | tf_op jit(solution)/shard_map/ppermute | solution.py:60
  427.2 37.8 %collective-permute-start.27 = (bf16[512,512]{1,0:T(8,128)(2,1)S(1)}, bf16[512,512]{1,0:T(8,128)(2,1)S(1)}, u32[]{:S(2)}, u32[]{:S(2)}) collective-permute-start(bf16[512,512]{1,0:T(8,128)(2,1)S(1)} %collective-permute-done.19), channel_id=1, source_target_pairs={{0,2},{1,3},{2,0},{3,1},{4,6},{5,7},{6,4},{7,5},{8,10},{9,11},{10,... | collective-permute-start | bytes 1572872 | tf_op jit(solution)/shard_map/ppermute | solution.py:60
  427.2 40.7 %slice-start.1 = ((s8[8388608]{0:T(1024)(128)(4,1)}), s8[4194304]{0:T(1024)(128)(4,1)S(1)}, s32[]{:S(2)}) async-start(s8[8388608]{0:T(1024)(128)(4,1)} %bitcast.212), calls=%async_computation.1 | async-start | bytes 8388608
  437.5 41.5 %collective-permute-start.20 = (bf16[512,512]{1,0:T(8,128)(2,1)S(1)}, bf16[512,512]{1,0:T(8,128)(2,1)S(1)}, u32[]{:S(2)}, u32[]{:S(2)}) collective-permute-start(bf16[512,512]{1,0:T(8,128)(2,1)S(1)} %collective-permute-done.19), channel_id=1, source_target_pairs={{0,1},{1,0},{2,3},{3,2},{4,5},{5,4},{6,7},{7,6},{8,9},{9,8},{10,11... | collective-permute-start | bytes 1572872 | tf_op jit(solution)/shard_map/ppermute | solution.py:60
  442.4 41.3 %collective-permute-start.25 = (bf16[512,512]{1,0:T(8,128)(2,1)S(1)}, bf16[512,512]{1,0:T(8,128)(2,1)S(1)}, u32[]{:S(2)}, u32[]{:S(2)}) collective-permute-start(bf16[512,512]{1,0:T(8,128)(2,1)S(1)} %collective-permute-done.19), channel_id=1, source_target_pairs={{0,12},{1,13},{2,14},{3,15},{4,0},{5,1},{6,2},{7,3},{8,4},{9,5},{1... | collective-permute-start | bytes 1572872 | tf_op jit(solution)/shard_map/ppermute | solution.py:60
  464.5 20.6 %collective-permute-start.22 = (bf16[512,512]{1,0:T(8,128)(2,1)S(1)}, bf16[512,512]{1,0:T(8,128)(2,1)S(1)}, u32[]{:S(2)}, u32[]{:S(2)}) collective-permute-start(bf16[512,512]{1,0:T(8,128)(2,1)S(1)} %collective-permute-done.21), channel_id=1, source_target_pairs={{0,1},{1,0},{2,3},{3,2},{4,5},{5,4},{6,7},{7,6},{8,9},{9,8},{10,11... | collective-permute-start | bytes 1572872 | tf_op jit(solution)/shard_map/ppermute | solution.py:60
  465.0 14.8 %collective-permute-start.23 = (bf16[512,512]{1,0:T(8,128)(2,1)S(1)}, bf16[512,512]{1,0:T(8,128)(2,1)S(1)}, u32[]{:S(2)}, u32[]{:S(2)}) collective-permute-start(bf16[512,512]{1,0:T(8,128)(2,1)S(1)} %collective-permute-done.21), channel_id=1, source_target_pairs={{0,4},{1,5},{2,6},{3,7},{4,8},{5,9},{6,10},{7,11},{8,12},{9,13},{1... | collective-permute-start | bytes 1572872 | tf_op jit(solution)/shard_map/ppermute | solution.py:60
  465.0 15.5 %collective-permute-start.31 = (bf16[512,512]{1,0:T(8,128)(2,1)S(1)}, bf16[512,512]{1,0:T(8,128)(2,1)S(1)}, u32[]{:S(2)}, u32[]{:S(2)}) collective-permute-start(bf16[512,512]{1,0:T(8,128)(2,1)S(1)} %collective-permute-done.27), channel_id=1, source_target_pairs={{0,12},{1,13},{2,14},{3,15},{4,0},{5,1},{6,2},{7,3},{8,4},{9,5},{1... | collective-permute-start | bytes 1572872 | tf_op jit(solution)/shard_map/ppermute | solution.py:60
  479.0 14.1 %collective-permute-start.29 = (bf16[512,512]{1,0:T(8,128)(2,1)S(1)}, bf16[512,512]{1,0:T(8,128)(2,1)S(1)}, u32[]{:S(2)}, u32[]{:S(2)}) collective-permute-start(bf16[512,512]{1,0:T(8,128)(2,1)S(1)} %collective-permute-done.27), channel_id=1, source_target_pairs={{0,4},{1,5},{2,6},{3,7},{4,8},{5,9},{6,10},{7,11},{8,12},{9,13},{1... | collective-permute-start | bytes 1572872 | tf_op jit(solution)/shard_map/ppermute | solution.py:60
  479.8 14.8 %collective-permute-start.24 = (bf16[512,512]{1,0:T(8,128)(2,1)S(1)}, bf16[512,512]{1,0:T(8,128)(2,1)S(1)}, u32[]{:S(2)}, u32[]{:S(2)}) collective-permute-start(bf16[512,512]{1,0:T(8,128)(2,1)S(1)} %collective-permute-done.23), channel_id=1, source_target_pairs={{0,1},{1,0},{2,3},{3,2},{4,5},{5,4},{6,7},{7,6},{8,9},{9,8},{10,11... | collective-permute-start | bytes 1572872 | tf_op jit(solution)/shard_map/ppermute | solution.py:60
  480.6 14.0 %collective-permute-start.32 = (bf16[512,512]{1,0:T(8,128)(2,1)S(1)}, bf16[512,512]{1,0:T(8,128)(2,1)S(1)}, u32[]{:S(2)}, u32[]{:S(2)}) collective-permute-start(bf16[512,512]{1,0:T(8,128)(2,1)S(1)} %collective-permute-done.31), channel_id=1, source_target_pairs={{0,12},{1,13},{2,14},{3,15},{4,0},{5,1},{6,2},{7,3},{8,4},{9,5},{1... | collective-permute-start | bytes 1572872 | tf_op jit(solution)/shard_map/ppermute | solution.py:60
  483.7 11.5 %collective-permute-start.26 = (bf16[512,512]{1,0:T(8,128)(2,1)S(1)}, bf16[512,512]{1,0:T(8,128)(2,1)S(1)}, u32[]{:S(2)}, u32[]{:S(2)}) collective-permute-start(bf16[512,512]{1,0:T(8,128)(2,1)S(1)} %collective-permute-done.25), channel_id=1, source_target_pairs={{0,1},{1,0},{2,3},{3,2},{4,5},{5,4},{6,7},{7,6},{8,9},{9,8},{10,11... | collective-permute-start | bytes 1572872 | tf_op jit(solution)/shard_map/ppermute | solution.py:60
  485.1 10.3 %collective-permute-start.28 = (bf16[512,512]{1,0:T(8,128)(2,1)S(1)}, bf16[512,512]{1,0:T(8,128)(2,1)S(1)}, u32[]{:S(2)}, u32[]{:S(2)}) collective-permute-start(bf16[512,512]{1,0:T(8,128)(2,1)S(1)} %collective-permute-done.27), channel_id=1, source_target_pairs={{0,1},{1,0},{2,3},{3,2},{4,5},{5,4},{6,7},{7,6},{8,9},{9,8},{10,11... | collective-permute-start | bytes 1572872 | tf_op jit(solution)/shard_map/ppermute | solution.py:60
  493.1 4.6 collective-permute-start.34
  494.5 2.3 collective-permute-start.30
  494.5 3.0 collective-permute-start.33
  (15 other events, 55.0 us)

commit v3 on v2

v3 whole, which is shorter than its diff:
```python
import math

import jax
import jax.numpy as jnp
from jax import lax
from jax.experimental import pallas as pl
from jax.experimental.pallas import tpu as pltpu
from jax.sharding import PartitionSpec as P

HEAD_SIZE = 128


THETA = 10000.0


def rope_tables(length, width):
    half_width = width // 2
    position = jnp.arange(length, dtype=jnp.float32)[:, None]
    channel = jnp.arange(half_width, dtype=jnp.float32)[None, :]
    angle = position * jnp.power(THETA, -2.0 * channel / width)
    return (jnp.cos(angle), jnp.sin(angle))


MESH = pl.DeviceIdType.MESH
BF16 = jnp.bfloat16
F32 = jnp.float32
MIB = 1 << 20


def here():
    blk, tp = lax.axis_index("blk"), lax.axis_index("tp")
    return blk // 4, blk % 4, tp // 4, tp // 2 % 2, tp % 2


def near(place, dh=0, dx=0, dz=0, dl=0, dc=0):
    h, x, z, low, core = place
    h, low, core = (h + dh) % 2, (low + dl) % 2, (core + dc) % 2
    x, z = (x + dx + 4) % 4, (z + dz + 4) % 4
    return h * 4 + x, z * 4 + low * 2 + core


def greet(devices):
    barrier = pltpu.get_barrier_semaphore()
    for device in devices:
        pl.semaphore_signal(barrier, inc=1, device_id=device, device_id_type=MESH)
    pl.semaphore_wait(barrier, len(devices))


def send(source, target, sems, device):
    copy = pltpu.make_async_remote_copy(
        src_ref=source,
        dst_ref=target,
        send_sem=sems[0],
        recv_sem=sems[1],
        device_id=device,
        device_id_type=MESH,
    )
    copy.start()
    return copy


def arrived(ref, sem):
    pltpu.make_async_copy(ref, ref, sem).wait()


CHUNKS = ((0, 2), (1, 2), (1, 1), (0, 3), (0, 1), (1, 3), (1, 0), (0, 0))


def project_kernel(
    tokens, cot, in_weight, o_weight, token_out, cot_out, proj_out, d_attn_out,
    blocks, proj_send, proj_recv, cot_send, cot_recv,
    a2a_s, a2a_r, up_s, up_r, down_s, down_r, far_s, far_r, core_s, core_r, sum_s, sum_r, keep,
):
    place = here()
    h, x, z, low, core = place
    seat = z * 2 + core
    height = blocks.shape[2] // 8
    width = blocks.shape[3]
    right, left = near(place, dx=1), near(place, dx=-1)
    above, below = near(place, dz=1), near(place, dz=-1)
    twin, across = near(place, dc=1), near(place, dh=1)
    shifts = [shift for shift in CHUNKS if shift != (0, 0)]
    greet([near(place, dh=dh, dx=dx) for dh, dx in shifts] + [above, below, twin])
    sent = []

    def rows(a, dh, dx, at):
        return blocks.at[a, dh * 4 + dx, pl.ds(pl.multiple_of(at * height, height), height)]

    def level(dz):
        return (z + dz + 4) % 4 * 2 + core

    def index(dh, dx):
        return dh * 4 + dx

    def start_blocks(a, source):
        for dh, dx in CHUNKS:
            target = near(place, dh=dh, dx=dx)
            piece = source.at[
                pl.ds(pl.multiple_of(seat * height, height), height),
                pl.ds(pl.multiple_of(target[0] * width, width), width),
            ]
            j = index(dh, dx)
            if j:
                sent.append(send(piece, rows(a, dh, dx, seat), (a2a_s.at[a, j], a2a_r.at[a, j]), target))
            else:
                pltpu.make_async_copy(piece, rows(a, 0, 0, seat), a2a_r.at[a, 0]).start()

    def to_twin(a, dh, dx, which, at):
        j = index(dh, dx)
        piece = rows(a, dh, dx, at)
        sent.append(send(piece, piece, (core_s.at[a, j, which], core_r.at[a, j, which]), twin))

    def first_stage(a, dh, dx):
        j = index(dh, dx)
        piece = rows(a, dh, dx, seat)
        arrived(piece, a2a_r.at[a, j])
        sent.append(send(piece, piece, (up_s.at[a, j], up_r.at[a, j]), above))
        sent.append(send(piece, piece, (down_s.at[a, j], down_r.at[a, j]), below))
        to_twin(a, dh, dx, 0, seat)

    def second_stage(a, dh, dx):
        j = index(dh, dx)
        sems = (far_s.at[a, j], far_r.at[a, j])
        lower, upper = rows(a, dh, dx, level(-1)), rows(a, dh, dx, level(1))
        arrived(lower, up_r.at[a, j])
        if dh == 0:
            sent.append(send(lower, lower, sems, above))
        to_twin(a, dh, dx, 1, level(-1))
        arrived(upper, down_r.at[a, j])
        if dh == 1:
            sent.append(send(upper, upper, sems, below))
        to_twin(a, dh, dx, 2, level(1))

    def third_stage(a, dh, dx):
        j = index(dh, dx)
        arrived(rows(a, dh, dx, level(2)), far_r.at[a, j])
        to_twin(a, dh, dx, 3, level(2))

    def complete(a, dh, dx):
        j = index(dh, dx)
        for which, dz in enumerate((0, -1, 1, 2)):
            seat_there = (z + dz + 4) % 4 * 2 + (1 - core)
            arrived(rows(a, dh, dx, seat_there), core_r.at[a, j, which])

    weights = (in_weight, o_weight)
    outgoing = (proj_send, cot_send)
    incoming = (proj_recv, cot_recv)
    results = (proj_out, d_attn_out)
    adds = {4: (0,), 5: (1,), 6: (2, 5), 7: (3, 4, 6)}
    ways = (left, right, left, right, left, right, across)

    def chunk(a, k):
        dh, dx = CHUNKS[k]
        j = index(dh, dx)
        third_stage(a, dh, dx)
        complete(a, dh, dx)
        terms = adds.get(k, ())
        for term in terms:
            arrived(incoming[a].at[term], sum_r.at[a, term])
        target = outgoing[a].at[k] if k < 7 else results[a]
        tile = blocks.shape[2] // 2

        @pl.loop(0, 2)
        def _(step):
            part = pl.ds(pl.multiple_of(step * tile, tile), tile)
            total = jnp.dot(blocks[a, j, part, :], weights[a][...], preferred_element_type=F32)
            for term in terms:
                total = total + incoming[a][term, part, :].astype(F32)
            target[part, :] = total.astype(target.dtype)

        if k < 7:
            sent.append(send(target, incoming[a].at[k], (sum_s.at[a, k], sum_r.at[a, k]), ways[k]))

    start_blocks(0, tokens)
    start_blocks(1, cot)
    for shift in CHUNKS:
        first_stage(0, *shift)
    for shift in CHUNKS:
        second_stage(0, *shift)
    for shift in CHUNKS:
        first_stage(1, *shift)
    for k in range(6):
        chunk(0, k)
        second_stage(1, *CHUNKS[k])
    for k in (6, 7):
        second_stage(1, *CHUNKS[k])
    for k in range(4):
        chunk(1, k)
    chunk(0, 6)
    for k in (4, 5):
        chunk(1, k)
    chunk(0, 7)
    chunk(1, 6)
    chunk(1, 7)
    keeps = [
        pltpu.make_async_copy(blocks.at[0], token_out, keep.at[0]),
        pltpu.make_async_copy(blocks.at[1], cot_out, keep.at[1]),
    ]
    for copy in keeps:
        copy.start()
    for copy in sent:
        copy.wait_send()
    for copy in keeps:
        copy.wait()


def project(tokens, cot, in_weight, o_weight):
    length = tokens.shape[0]
    width = tokens.shape[1] // 8
    in_width, o_width = in_weight.shape[1], o_weight.shape[1]
    dma = pltpu.SemaphoreType.DMA
    pair = [dma((2, 8)), dma((2, 8))]
    block = jax.ShapeDtypeStruct((8, length, width), BF16)
    return pl.pallas_call(
        project_kernel,
        out_shape=(
            block,
            block,
            jax.ShapeDtypeStruct((length, in_width), F32),
            jax.ShapeDtypeStruct((length, o_width), BF16),
        ),
        in_specs=[pl.BlockSpec(memory_space=pl.ANY)] * 2
        + [pl.BlockSpec(memory_space=pltpu.VMEM)] * 2,
        out_specs=(pl.BlockSpec(memory_space=pl.ANY),) * 2
        + (pl.BlockSpec(memory_space=pltpu.VMEM),) * 2,
        scratch_shapes=[
            pltpu.VMEM((2, 8, length, width), BF16),
            pltpu.VMEM((7, length, in_width), BF16),
            pltpu.VMEM((7, length, in_width), BF16),
            pltpu.VMEM((7, length, o_width), BF16),
            pltpu.VMEM((7, length, o_width), BF16),
            *pair,
            *pair,
            *pair,
            *pair,
            dma((2, 8, 4)),
            dma((2, 8, 4)),
            dma((2, 7)),
            dma((2, 7)),
            dma((2,)),
        ],
        compiler_params=pltpu.CompilerParams(
            collective_id=0, has_side_effects=True, vmem_limit_bytes=56 * MIB
        ),
        name="project",
    )(tokens, cot, in_weight, o_weight)


def nt(left, right):
    return lax.dot_general(left, right, (((1,), (1,)), ((), ())), preferred_element_type=F32)


def tn(left, right):
    return lax.dot_general(left, right, (((0,), (0,)), ((), ())), preferred_element_type=F32)


def swap_halves(array):
    return pltpu.roll(array, array.shape[1] // 2, 1)


LEVELS = (2, -1, 1, 0)


def finish_kernel(
    proj, d_attn, cosine, sine, seg_col, seg_row, in_weight, o_weight, token_blocks, cot_blocks,
    mixed, d_tokens, q_grad, kv_grad, o_grad,
    attn_all, grad_all, q_rot, probs, bias, keys, values, kv_send, kv_recv, key_sum, value_sum,
    kv_grad_send, kv_grad_recv,
    half_send, half_recv, level_send, level_recv, side_send, side_recv, last_send, last_recv,
    column, grad_sum,
    kv_sems, ring_s, ring_r, half_s, half_r, level_s, level_r, side_sems, hand_s, hand_r,
    mixed_s, mixed_r, twin_s, twin_r, column_sem, out_sem,
):
    place = here()
    h, x, z, low, core = place
    blk, tp = h * 4 + x, z * 4 + low * 2 + core
    length, q_width = d_attn.shape
    tile = length // 2
    score_scale = 1.0 / math.sqrt(HEAD_SIZE)
    right, left = near(place, dx=1), near(place, dx=-1)
    above, below = near(place, dz=1), near(place, dz=-1)
    twin, across, beside = near(place, dc=1), near(place, dh=1), near(place, dl=1)
    halves = []
    group = z * 2 + low
    home = (group, blk * 2 + core)
    away = group != blk
    sent = []

    barrier = pltpu.get_barrier_semaphore()
    for device in (right, left, above, below, twin, across, beside):
        pl.semaphore_signal(barrier, inc=1, device_id=device, device_id_type=MESH)

    @pl.when(away)
    def _():
        pl.semaphore_signal(barrier, inc=1, device_id=home, device_id_type=MESH)

    pl.semaphore_wait(barrier, 7 + jnp.where(away, 1, 0))

    def post(source, target, sems, device):
        sent.append(send(source, target, sems, device))

    lane = lax.broadcasted_iota(jnp.int32, (length, HEAD_SIZE), 1)
    in_front = lane < HEAD_SIZE // 2
    is_lower = jnp.full((length, HEAD_SIZE), core) == 0
    kv_send[...] = proj[:, q_width:].astype(BF16)
    post(kv_send, kv_recv, (kv_sems.at[0], kv_sems.at[1]), twin)

    @pl.loop(0, 2)
    def _(step):
        start = pl.multiple_of(step * tile, tile)
        part = pl.ds(start, tile)
        row = lax.broadcasted_iota(jnp.int32, (tile, length), 0) + start
        key = lax.broadcasted_iota(jnp.int32, (tile, length), 1)
        allowed = (key <= row) & (seg_col[part, :] == seg_row[...])
        bias[part, :] = jnp.where(allowed, 0.0, -jnp.inf)

    @pl.loop(0, q_width // HEAD_SIZE)
    def _(head):
        cols = pl.ds(pl.multiple_of(head * HEAD_SIZE, HEAD_SIZE), HEAD_SIZE)
        query = proj[:, cols]
        q_rot[:, cols] = (query * cosine[...] + swap_halves(query) * sine[...]).astype(BF16)

    arrived(kv_recv, kv_sems.at[1])
    own, other = kv_send[...].astype(F32), kv_recv[...].astype(F32)
    lower, upper = jnp.where(is_lower, own, other), jnp.where(is_lower, other, own)
    key = jnp.where(in_front, lower, swap_halves(upper))
    keys[...] = (key * cosine[...] + swap_halves(key) * sine[...]).astype(BF16)
    values[...] = jnp.where(in_front, swap_halves(lower), upper).astype(BF16)

    @pl.loop(0, q_width // HEAD_SIZE)
    def _(head):
        cols = pl.ds(pl.multiple_of(head * HEAD_SIZE, HEAD_SIZE), HEAD_SIZE)

        @pl.loop(0, 2)
        def _(step):
            part = pl.ds(pl.multiple_of(step * tile, tile), tile)
            scores = nt(q_rot[part, cols], keys[...]) * score_scale + bias[part, :]
            raised = jnp.exp(scores - jnp.max(scores, axis=1, keepdims=True))
            prob = raised / jnp.sum(raised, axis=1, keepdims=True)
            probs[head, part, :] = prob
            mixed_values = jnp.dot(prob.astype(BF16), values[...], preferred_element_type=F32)
            attn_all[0, part, cols] = mixed_values.astype(BF16)

    rings = (attn_all, grad_all)

    def hop(i, k, source, target, device):
        ring = rings[i]
        post(ring.at[source], ring.at[target], (ring_s.at[i, k], ring_r.at[i, k]), device)

    def ring_wait(i, k, target):
        arrived(rings[i].at[target], ring_r.at[i, k])

    def ring_start(i):
        hop(i, 0, 0, 4, across)
        hop(i, 1, 0, 1, right)
        hop(i, 2, 0, 3, left)

    def ring_side(i):
        ring_wait(i, 0, 4)
        hop(i, 3, 4, 5, right)
        hop(i, 4, 4, 7, left)

    def ring_forward(i):
        ring_wait(i, 1, 1)
        hop(i, 5, 1, 2, right)
        ring_wait(i, 4, 7)
        hop(i, 6, 7, 6, left)

    def ring_end(i):
        for k, target in ((2, 3), (3, 5), (5, 2), (6, 6)):
            ring_wait(i, k, target)

    ring_start(0)

    key_sum[...] = jnp.zeros_like(key_sum)
    value_sum[...] = jnp.zeros_like(value_sum)

    @pl.loop(0, q_width // HEAD_SIZE)
    def _(head):
        cols = pl.ds(pl.multiple_of(head * HEAD_SIZE, HEAD_SIZE), HEAD_SIZE)

        @pl.loop(0, 2)
        def _(step):
            part = pl.ds(pl.multiple_of(step * tile, tile), tile)
            d_out = d_attn[part, cols]
            prob = probs[head, part, :]
            d_prob = nt(d_out, values[...])
            row_delta = jnp.sum(prob * d_prob, axis=1, keepdims=True)
            d_score = (prob * (d_prob - row_delta) * score_scale).astype(BF16)
            d_query = jnp.dot(d_score, keys[...], preferred_element_type=F32)
            d_query = d_query * cosine[part, :] - swap_halves(d_query) * sine[part, :]
            grad_all[0, part, cols] = d_query.astype(BF16)
            key_sum[...] += tn(d_score, q_rot[part, cols])
            value_sum[...] += tn(prob.astype(BF16), d_out)

    d_key = key_sum[...] * cosine[...] - swap_halves(key_sum[...]) * sine[...]
    d_key, d_value = d_key.astype(BF16).astype(F32), value_sum[...].astype(BF16).astype(F32)
    lower = jnp.where(in_front, d_key, swap_halves(d_value))
    upper = jnp.where(in_front, swap_halves(d_key), d_value)
    kv_grad_send[...] = jnp.where(is_lower, upper, lower).astype(BF16)
    post(kv_grad_send, kv_grad_recv, (kv_sems.at[2], kv_sems.at[3]), twin)
    own = jnp.where(is_lower, lower, upper)
    arrived(kv_grad_recv, kv_sems.at[3])
    grad_all[0, :, q_width:] = (own + kv_grad_recv[...].astype(F32)).astype(BF16)

    weights = (o_weight, in_weight)
    half = o_weight.shape[0] // 2

    def spot(dz, side):
        there = (z + dz + 4) % 4 * 2 + side
        return (h + there // 4) % 2 * 4 + (x - there % 4 + 4) % 4

    def term(i, dz, side, which, part):
        rows = pl.ds(pl.multiple_of(which * half, half), half)
        return nt(rings[i][spot(dz, side), part, :], weights[i][rows, :])

    def give_half(i):
        for q, dz in enumerate(LEVELS):
            if i:
                halves[q].wait_send()
            for side in range(2):

                @pl.loop(0, 2)
                def _(step):
                    part = pl.ds(pl.multiple_of(step * tile, tile), tile)
                    half_send[q, side, part, :] = term(i, dz, side, 1 - core, part).astype(BF16)

            sems = (half_s.at[i, q], half_r.at[i, q])
            halves.append(send(half_send.at[q], half_recv.at[i, q], sems, twin))

    def half_wait(i, q):
        arrived(half_recv.at[i, q], half_r.at[i, q])

    def add_up(i, q, side, target, terms):
        @pl.loop(0, 2)
        def _(step):
            part = pl.ds(pl.multiple_of(step * tile, tile), tile)
            total = term(i, LEVELS[q], side, core, part)
            total = total + half_recv[i, q, side, part, :].astype(F32)
            for ref in terms:
                total = total + ref[part, :].astype(F32)
            target[part, :] = total.astype(target.dtype)

    def level_hop(i, k, slot, device):
        sems = (level_s.at[i, k], level_r.at[i, slot])
        post(level_send.at[i, k], level_recv.at[i, slot], sems, device)

    def level_wait(i, slot):
        arrived(level_recv.at[i, slot], level_r.at[i, slot])

    def far_level(i):
        half_wait(i, 0)
        add_up(i, 0, 0, level_send.at[i, 0], ())
        level_hop(i, 0, 0, below)
        add_up(i, 0, 1, level_send.at[i, 1], ())
        level_hop(i, 1, 1, above)

    def near_level(i):
        half_wait(i, 1)
        add_up(i, 1, 1, level_send.at[i, 2], ())
        level_hop(i, 2, 3, below)
        half_wait(i, 2)
        add_up(i, 2, 0, level_send.at[i, 3], ())
        level_hop(i, 3, 4, above)

    def pass_level(i):
        level_wait(i, 0)
        add_up(i, 1, 0, level_send.at[i, 4], (level_recv.at[i, 0],))
        level_hop(i, 4, 2, below)
        level_wait(i, 1)
        add_up(i, 2, 1, level_send.at[i, 5], (level_recv.at[i, 1],))
        level_hop(i, 5, 5, above)

    def own_level(i):
        half_wait(i, 3)
        for slot in range(2, 6):
            level_wait(i, slot)
        terms = (level_recv.at[i, 2 + 1 - low], level_recv.at[i, 4 + 1 - low])
        add_up(i, 3, 1 - low, side_send.at[i], terms)
        post(side_send.at[i], side_recv.at[i], (side_sems.at[i, 0], side_sems.at[i, 1]), beside)

    tp_width = half

    def columns(t):
        return mixed.at[:, pl.ds(pl.multiple_of(t * tp_width, tp_width), tp_width)]

    def last_target(i):
        return columns(tp) if i == 0 else last_recv

    def last_level(i):
        arrived(side_recv.at[i], side_sems.at[i, 1])
        terms = (level_recv.at[i, 2 + low], level_recv.at[i, 4 + low], side_recv.at[i])
        add_up(i, 3, low, last_send.at[i], terms)
        there = columns(home[1]) if i == 0 else last_recv

        @pl.when(away)
        def _():
            send(last_send.at[i], there, (hand_s.at[i], hand_r.at[i]), home)

        @pl.when(group == blk)
        def _():
            pltpu.make_async_copy(last_send.at[i], last_target(i), hand_r.at[i]).start()

    def hand_end(i):
        arrived(last_target(i), hand_r.at[i])

    def hand_sent(i):
        @pl.when(away)
        def _():
            arrived(last_send.at[i], hand_s.at[i])

    def tp_at(dz, dl, dc=0):
        return (z + dz + 4) % 4 * 4 + (low + dl) % 2 * 2 + (core + dc) % 2

    def mixed_hop(k, t, device):
        post(columns(t), columns(t), (mixed_s.at[k], mixed_r.at[k]), device)

    def mixed_wait(k, t):
        arrived(columns(t), mixed_r.at[k])

    def mixed_twin(k, t):
        post(columns(t), columns(t), (twin_s.at[k], twin_r.at[k]), twin)

    def mixed_start():
        hand_end(0)
        mixed_hop(0, tp, beside)
        mixed_hop(1, tp, above)
        mixed_hop(2, tp, below)
        mixed_twin(0, tp)

    def mixed_side():
        mixed_wait(0, tp_at(0, 1))
        mixed_hop(3, tp_at(0, 1), above)
        mixed_hop(4, tp_at(0, 1), below)
        mixed_twin(1, tp_at(0, 1))

    def mixed_forward():
        mixed_wait(1, tp_at(-1, 0))
        mixed_hop(5, tp_at(-1, 0), above)
        mixed_twin(2, tp_at(-1, 0))
        mixed_wait(2, tp_at(1, 0))
        mixed_twin(3, tp_at(1, 0))
        mixed_wait(4, tp_at(1, 1))
        mixed_hop(6, tp_at(1, 1), below)
        mixed_twin(4, tp_at(1, 1))

    def mixed_end():
        mixed_wait(3, tp_at(-1, 1))
        mixed_twin(5, tp_at(-1, 1))
        mixed_wait(5, tp_at(2, 0))
        mixed_twin(6, tp_at(2, 0))
        mixed_wait(6, tp_at(2, 1))
        mixed_twin(7, tp_at(2, 1))
        sources = ((0, 0), (0, 1), (-1, 0), (1, 0), (1, 1), (-1, 1), (2, 0), (2, 1))
        for k, (dz, dl) in enumerate(sources):
            arrived(columns(tp_at(dz, dl, 1)), twin_r.at[k])

    sources = (cot_blocks, token_blocks)
    order = (0, 4, 1, 3, 5, 7, 2, 6)
    steps = [(i, j) for i in range(2) for j in order]

    def load(n):
        i, j = steps[n]
        pltpu.make_async_copy(sources[i].at[j], column.at[n % 2], column_sem.at[n % 2]).start()

    def grad_step(n):
        i, j = steps[n]
        slot = n % 2
        arrived(column.at[slot], column_sem.at[slot])
        width = rings[i].shape[2]
        strip = 256

        @pl.loop(0, column.shape[2] // strip)
        def _(step):
            part = pl.ds(pl.multiple_of(step * strip, strip), strip)
            value = tn(column[slot, :, part], rings[i][j])
            if n % 8:
                value = value + grad_sum[part, :width]
            if n % 8 < 7:
                grad_sum[part, :width] = value
            elif i == 0:
                o_grad[part, :] = value.astype(BF16)
            else:
                q_grad[part, :] = value[:, :q_width].astype(BF16)
                kv_grad[part, :] = value[:, q_width:].astype(BF16)

        if n + 2 < len(steps):
            load(n + 2)

    load(0)
    load(1)
    ring_side(0)
    ring_start(1)
    grad_step(0)
    ring_forward(0)
    ring_side(1)
    grad_step(1)
    ring_end(0)
    give_half(0)
    ring_forward(1)
    far_level(0)
    near_level(0)
    for n in range(2, 5):
        grad_step(n)
    pass_level(0)
    for n in range(5, 8):
        grad_step(n)
    ring_end(1)
    give_half(1)
    far_level(1)
    near_level(1)
    own_level(0)
    grad_step(8)
    grad_step(9)
    last_level(0)
    pass_level(1)
    grad_step(10)
    grad_step(11)
    mixed_start()
    grad_step(12)
    grad_step(13)
    mixed_side()
    own_level(1)
    grad_step(14)
    grad_step(15)
    mixed_forward()
    last_level(1)
    mixed_end()
    hand_end(1)
    out = pltpu.make_async_copy(last_recv, d_tokens, out_sem)
    out.start()
    for copy in sent + halves[4:]:
        copy.wait_send()
    hand_sent(0)
    hand_sent(1)
    out.wait()


def finish(proj, d_attn, cosine, sine, segments, in_weight, o_weight, token_blocks, cot_blocks):
    length, q_width = d_attn.shape
    in_width = in_weight.shape[1]
    depth = in_weight.shape[0]
    half = depth // 2
    heads = q_width // HEAD_SIZE
    dma = pltpu.SemaphoreType.DMA
    vmem = pl.BlockSpec(memory_space=pltpu.VMEM)
    hbm = pl.BlockSpec(memory_space=pl.ANY)
    part = pltpu.VMEM((length, HEAD_SIZE), BF16)
    part_sum = pltpu.VMEM((length, HEAD_SIZE), F32)
    return pl.pallas_call(
        finish_kernel,
        out_shape=(
            jax.ShapeDtypeStruct((length, 16 * half), BF16),
            jax.ShapeDtypeStruct((length, half), BF16),
            jax.ShapeDtypeStruct((depth, q_width), BF16),
            jax.ShapeDtypeStruct((depth, in_width - q_width), BF16),
            jax.ShapeDtypeStruct((depth, q_width), BF16),
        ),
        in_specs=[vmem] * 8 + [hbm] * 2,
        out_specs=(hbm, hbm, vmem, vmem, vmem),
        scratch_shapes=[
            pltpu.VMEM((8, length, q_width), BF16),
            pltpu.VMEM((8, length, in_width), BF16),
            pltpu.VMEM((length, q_width), BF16),
            pltpu.VMEM((heads, length, length), F32),
            pltpu.VMEM((length, length), F32),
            part,
            part,
            part,
            part,
            part_sum,
            part_sum,
            part,
            part,
            pltpu.VMEM((4, 2, length, half), BF16),
            pltpu.VMEM((2, 4, 2, length, half), BF16),
            pltpu.VMEM((2, 6, length, half), BF16),
            pltpu.VMEM((2, 6, length, half), BF16),
            pltpu.VMEM((2, length, half), BF16),
            pltpu.VMEM((2, length, half), BF16),
            pltpu.VMEM((2, length, half), BF16),
            pltpu.VMEM((length, half), BF16),
            pltpu.VMEM((2, length, depth), BF16),
            pltpu.VMEM((depth, in_width), F32),
            dma((4,)),
            dma((2, 7)),
            dma((2, 7)),
            dma((2, 4)),
            dma((2, 4)),
            dma((2, 6)),
            dma((2, 6)),
            dma((2, 2)),
            dma((2,)),
            dma((2,)),
            dma((7,)),
            dma((7,)),
            dma((8,)),
            dma((8,)),
            dma((2,)),
            dma,
        ],
        compiler_params=pltpu.CompilerParams(
            collective_id=1, has_side_effects=True, vmem_limit_bytes=63 * MIB
        ),
        name="finish",
    )(
        proj, d_attn, cosine, sine, segments.reshape(length, 1), segments.reshape(1, length),
        in_weight, o_weight, token_blocks, cot_blocks,
    )


def shards(tokens, segment_ids, q_weight, key_value_weight, o_weight, cotangent):
    in_weight = jnp.concatenate([q_weight, key_value_weight], axis=1)
    token_blocks, cot_blocks, proj, d_attn = project(tokens, cotangent, in_weight, o_weight)
    cosine, sine = rope_tables(tokens.shape[0], HEAD_SIZE)
    cosine = jnp.concatenate([cosine, cosine], axis=1)
    sine = jnp.concatenate([-sine, sine], axis=1)
    return finish(
        proj, d_attn, cosine, sine, segment_ids[0], in_weight, o_weight, token_blocks, cot_blocks
    )


def solution(mesh):
    in_specs = (
        P("blk", None),
        P("blk", None),
        P("blk", "tp"),
        P("blk", "tp"),
        P("blk", "tp"),
        P("blk", None),
    )
    out_specs = (P("blk", None), P("blk", "tp"), P("blk", "tp"), P("blk", "tp"), P("blk", "tp"))
    return jax.shard_map(shards, mesh=mesh, in_specs=in_specs, out_specs=out_specs, check_vma=False)
```

time: 509 us -> 417 us (0.82)
  the two profiles are of different devices: /device:TPU:21 before, /device:TPU:114 now
where the time goes in v3:
time: 417 us
  Pallas kernels  398 us (95%)
  local copies, waits for them, and re-layouts  15.7 us (4%)
    pallas_call x1, Pallas kernels, finish(): pl.pallas_call(finish_kernel, out_shape=(jax.ShapeDtypeStruct((length, 16...  243 us
    pallas_call x1, Pallas kernels, project(): pl.pallas_call(project_kernel, out_shape=(block, block, jax.ShapeDtypeStr...  156 us
    unnamed x20, local copies, waits for them, and re-layouts  14 us

profile of v3, /device:TPU:114, one launch (start us, length us, event | category | flops | bytes accessed | tf_op | source)
XLA Modules:
  0.0 416.8 jit_solution(1588173126189297726)
XLA Ops:
  0.6 0.0 copy-start.1
  0.7 1.6 copy.11.seg_col
  2.3 1.0 fusion.2
  3.3 1.0 pad_maximum_fusion
  4.3 0.0 copy-start.5
  4.3 0.0 copy-done.1
  4.3 0.1 constant_dynamic-update-slice_fusion.1
  4.3 0.9 copy-done.5
  5.2 0.1 constant_dynamic-update-slice_fusion.in_weight
  5.3 0.0 copy-start
  5.3 1.0 copy-done
  6.3 155.6 %project.1 = (bf16[8,512,1024]{2,1,0:T(8,128)(2,1)}, bf16[8,512,1024]{2,1,0:T(8,128)(2,1)}, f32[512,640]{1,0:T(8,128)}, bf16[512,512]{1,0:T(8,128)(2,1)}) custom-call(bf16[512,8192]{1,0:T(8,128)(2,1)} %tokens.1, bf16[512,8192]{1,0:T(8,128)(2,1)} %cot.1, bf16[1024,640]{1,0:T(8,128)(2,1)} %copy-done, bf16[1024,512]{1,0:T(8,128)(2,1)} %o_weight.3), custom_call_target="tpu_custom_call" | custom-call | tf_op jit(solution)/shard_map/project/pallas_call | solution.py:214
  162.0 242.7 %finish.1 = (bf16[512,8192]{1,0:T(8,128)(2,1)}, bf16[512,512]{1,0:T(8,128)(2,1)}, bf16[1024,512]{1,0:T(8,128)(2,1)}, bf16[1024,128]{1,0:T(8,128)(2,1)}, bf16[1024,512]{1,0:T(8,128)(2,1)}) custom-call(f32[512,640]{1,0:T(8,128)} %get-tuple-element.9.proj, bf16[512,512]{1,0:T(8,128)(2,1)} %get-tuple-element.10.d_attn, f32[512,128]{1,0:T(8,128)} %get-tuple-element.16.cosine, ...), custom_call_target="tpu_custom_call" | custom-call | tf_op jit(solution)/shard_map/finish/pallas_call | solution.py:650
  404.7 0.0 copy-start.4
  404.7 7.8 %copy.18 = bf16[512,8192]{1,0:T(8,128)(2,1)} copy(bf16[512,8192]{1,0:T(8,128)(2,1)} %get-tuple-element.23) | data formatting | bytes 16777216
  412.6 0.0 copy-done.4
  412.6 0.0 copy-start.3
  412.6 0.8 copy.19
  413.4 0.6 copy-done.3
  414.0 0.0 copy-start.6
  414.0 0.0 copy-start.2
  414.0 1.0 copy.20
  415.0 0.1 copy-done.6
  415.1 0.7 copy.21
  415.8 0.0 copy-done.2
  415.8 1.0 copy.22
  (1 shorter events, 0.0 us)
Async XLA Ops:
  0.6 3.6 copy-start.1
  4.3 0.9 copy-start.5
  5.3 1.1 copy-start
  404.7 7.8 %copy-start.4 = (bf16[512,512]{1,0:T(8,128)(2,1)S(1)}, bf16[512,512]{1,0:T(8,128)(2,1)}, u32[]{:S(2)}) copy-start(bf16[512,512]{1,0:T(8,128)(2,1)} %get-tuple-element.24) | copy-start | bytes 1572868
  412.6 1.4 copy-start.3
  414.0 1.1 copy-start.6
  414.0 1.8 copy-start.2

commit v4 on v3

--- a/solution.py
+++ b/solution.py
@@ -152,7 +152,6 @@
     def chunk(a, k):
         dh, dx = CHUNKS[k]
         j = index(dh, dx)
-        third_stage(a, dh, dx)
         complete(a, dh, dx)
         terms = adds.get(k, ())
         for term in terms:
@@ -173,25 +172,18 @@
 
     start_blocks(0, tokens)
     start_blocks(1, cot)
-    for shift in CHUNKS:
-        first_stage(0, *shift)
-    for shift in CHUNKS:
-        second_stage(0, *shift)
-    for shift in CHUNKS:
-        first_stage(1, *shift)
-    for k in range(6):
-        chunk(0, k)
-        second_stage(1, *CHUNKS[k])
-    for k in (6, 7):
-        second_stage(1, *CHUNKS[k])
-    for k in range(4):
-        chunk(1, k)
-    chunk(0, 6)
-    for k in (4, 5):
-        chunk(1, k)
-    chunk(0, 7)
-    chunk(1, 6)
-    chunk(1, 7)
+    pieces = [(a, k) for a in range(2) for k in range(8)]
+    waiting = [(0, 0), (0, 1), (0, 2), (0, 3), (0, 4), (0, 5), (0, 6), (1, 0), (1, 1), (1, 2), (1, 3)]
+    waiting += [(0, 7), (1, 4), (1, 5), (1, 6), (1, 7)]
+    late = {(0, 6): 7, (0, 7): 9}
+    for step in range(len(pieces) + 5):
+        for stage, lag in ((first_stage, 0), (second_stage, 2), (third_stage, 4)):
+            if 0 <= step - lag < len(pieces):
+                a, k = pieces[step - lag]
+                stage(a, *CHUNKS[k])
+        while waiting and pieces.index(waiting[0]) + late.get(waiting[0], 5) <= step:
+            chunk(*waiting.pop(0))
+    assert not waiting
     keeps = [
         pltpu.make_async_copy(blocks.at[0], token_out, keep.at[0]),
         pltpu.make_async_copy(blocks.at[1], cot_out, keep.at[1]),
@@ -350,8 +342,10 @@
     def ring_wait(i, k, target):
         arrived(rings[i].at[target], ring_r.at[i, k])
 
+    def ring_across(i):
+        hop(i, 0, 0, 4, across)
+
     def ring_start(i):
-        hop(i, 0, 0, 4, across)
         hop(i, 1, 0, 1, right)
         hop(i, 2, 0, 3, left)
 
@@ -370,6 +364,7 @@
         for k, target in ((2, 3), (3, 5), (5, 2), (6, 6)):
             ring_wait(i, k, target)
 
+    ring_across(0)
     ring_start(0)
 
     key_sum[...] = jnp.zeros_like(key_sum)
@@ -589,41 +584,41 @@
 
     load(0)
     load(1)
+    ring_across(1)
     ring_side(0)
-    ring_start(1)
     grad_step(0)
     ring_forward(0)
+    ring_start(1)
     ring_side(1)
     grad_step(1)
     ring_end(0)
     give_half(0)
-    ring_forward(1)
     far_level(0)
     near_level(0)
-    for n in range(2, 5):
+    grad_step(2)
+    ring_forward(1)
+    pass_level(0)
+    for n in range(3, 8):
         grad_step(n)
-    pass_level(0)
-    for n in range(5, 8):
-        grad_step(n)
+    own_level(0)
     ring_end(1)
     give_half(1)
     far_level(1)
+    last_level(0)
     near_level(1)
-    own_level(0)
     grad_step(8)
     grad_step(9)
-    last_level(0)
+    mixed_start()
     pass_level(1)
     grad_step(10)
     grad_step(11)
-    mixed_start()
+    mixed_side()
     grad_step(12)
     grad_step(13)
-    mixed_side()
+    mixed_forward()
     own_level(1)
     grad_step(14)
     grad_step(15)
-    mixed_forward()
     last_level(1)
     mixed_end()
     hand_end(1)

time: 417 us -> 389 us (0.933)
  the two profiles are of different devices: /device:TPU:114 before, /device:TPU:120 now
where the time goes in v4:
time: 389 us
  Pallas kernels  371 us (95%)
  local copies, waits for them, and re-layouts  15.7 us (4%)
    pallas_call x1, Pallas kernels, finish(): pl.pallas_call(finish_kernel, out_shape=(jax.ShapeDtypeStruct((length, 16...  237 us
    pallas_call x1, Pallas kernels, project(): pl.pallas_call(project_kernel, out_shape=(block, block, jax.ShapeDtypeStr...  134 us
    unnamed x20, local copies, waits for them, and re-layouts  14 us

profile of v4, /device:TPU:120, one launch (start us, length us, event | category | flops | bytes accessed | tf_op | source)
XLA Modules:
  0.0 389.2 jit_solution(2715398503042420590)
XLA Ops:
  0.6 0.0 copy-start.1
  0.7 1.6 copy.11.seg_col
  2.3 1.0 fusion.2
  3.3 1.0 pad_maximum_fusion
  4.3 0.0 copy-start.5
  4.3 0.0 copy-done.1
  4.3 0.1 constant_dynamic-update-slice_fusion.1
  4.3 0.9 copy-done.5
  5.2 0.1 constant_dynamic-update-slice_fusion.in_weight
  5.3 0.0 copy-start
  5.3 1.0 copy-done
  6.3 133.6 %project.1 = (bf16[8,512,1024]{2,1,0:T(8,128)(2,1)}, bf16[8,512,1024]{2,1,0:T(8,128)(2,1)}, f32[512,640]{1,0:T(8,128)}, bf16[512,512]{1,0:T(8,128)(2,1)}) custom-call(bf16[512,8192]{1,0:T(8,128)(2,1)} %tokens.1, bf16[512,8192]{1,0:T(8,128)(2,1)} %cot.1, bf16[1024,640]{1,0:T(8,128)(2,1)} %copy-done, bf16[1024,512]{1,0:T(8,128)(2,1)} %o_weight.3), custom_call_target="tpu_custom_call" | custom-call | tf_op jit(solution)/shard_map/project/pallas_call | solution.py:206
  140.0 237.2 %finish.1 = (bf16[512,8192]{1,0:T(8,128)(2,1)}, bf16[512,512]{1,0:T(8,128)(2,1)}, bf16[1024,512]{1,0:T(8,128)(2,1)}, bf16[1024,128]{1,0:T(8,128)(2,1)}, bf16[1024,512]{1,0:T(8,128)(2,1)}) custom-call(f32[512,640]{1,0:T(8,128)} %get-tuple-element.9.proj, bf16[512,512]{1,0:T(8,128)(2,1)} %get-tuple-element.10.d_attn, f32[512,128]{1,0:T(8,128)} %get-tuple-element.16.cosine, ...), custom_call_target="tpu_custom_call" | custom-call | tf_op jit(solution)/shard_map/finish/pallas_call | solution.py:645
  377.2 0.0 copy-start.4
  377.2 7.8 %copy.18 = bf16[512,8192]{1,0:T(8,128)(2,1)} copy(bf16[512,8192]{1,0:T(8,128)(2,1)} %get-tuple-element.23) | data formatting | bytes 16777216
  385.0 0.0 copy-done.4
  385.0 0.0 copy-start.3
  385.0 0.8 copy.19
  385.8 0.6 copy-done.3
  386.5 0.0 copy-start.6
  386.5 0.0 copy-start.2
  386.5 1.0 copy.20
  387.4 0.1 copy-done.6
  387.5 0.7 copy.21
  388.3 0.0 copy-done.2
  388.3 1.0 copy.22
  (1 shorter events, 0.0 us)
Async XLA Ops:
  0.6 3.6 copy-start.1
  4.3 0.9 copy-start.5
  5.3 1.1 copy-start
  377.2 7.8 %copy-start.4 = (bf16[512,512]{1,0:T(8,128)(2,1)S(1)}, bf16[512,512]{1,0:T(8,128)(2,1)}, u32[]{:S(2)}) copy-start(bf16[512,512]{1,0:T(8,128)(2,1)} %get-tuple-element.24) | copy-start | bytes 1572868
  385.0 1.4 copy-start.3
  386.5 1.1 copy-start.6
  386.5 1.8 copy-start.2

commit v5 on v4

--- a/solution.py
+++ b/solution.py
@@ -265,7 +265,7 @@
 ):
     place = here()
     h, x, z, low, core = place
-    blk, tp = h * 4 + x, z * 4 + low * 2 + core
+    blk = h * 4 + x
     length, q_width = d_attn.shape
     tile = length // 2
     score_scale = 1.0 / math.sqrt(HEAD_SIZE)
@@ -273,20 +273,30 @@
     above, below = near(place, dz=1), near(place, dz=-1)
     twin, across, beside = near(place, dc=1), near(place, dh=1), near(place, dl=1)
     halves = []
-    group = z * 2 + low
-    home = (group, blk * 2 + core)
-    away = group != blk
-    sent = []
+    far_h, far_x = z // 2, z % 2 * 2 + low
+    origin = z * 2 + low
+    origin_h, origin_x = (origin // 4 + h) % 2, (origin % 4 - x + 4) % 4
+    homes = (
+        near(place, dh=far_h, dx=-far_x),
+        (near(place, dh=far_h, dx=-far_x)[0], blk * 2 + core),
+    )
+    givers = (
+        near(place, dh=far_h, dx=far_x),
+        (origin, (origin_h * 2 + origin_x // 2) * 4 + origin_x % 2 * 2 + core),
+    )
+    stays = (z * 2 + low == 0, z * 2 + low + blk == 0)
+    sent, halves = [], []
 
     barrier = pltpu.get_barrier_semaphore()
     for device in (right, left, above, below, twin, across, beside):
         pl.semaphore_signal(barrier, inc=1, device_id=device, device_id_type=MESH)
-
-    @pl.when(away)
-    def _():
-        pl.semaphore_signal(barrier, inc=1, device_id=home, device_id_type=MESH)
-
-    pl.semaphore_wait(barrier, 7 + jnp.where(away, 1, 0))
+    for i in range(2):
+
+        @pl.when(jnp.logical_not(stays[i]))
+        def _():
+            pl.semaphore_signal(barrier, inc=1, device_id=givers[i], device_id_type=MESH)
+
+    pl.semaphore_wait(barrier, 9 - jnp.where(stays[0], 1, 0) - jnp.where(stays[1], 1, 0))
 
     def post(source, target, sems, device):
         sent.append(send(source, target, sems, device))
@@ -354,9 +364,11 @@
         hop(i, 3, 4, 5, right)
         hop(i, 4, 4, 7, left)
 
-    def ring_forward(i):
+    def ring_pass(i):
         ring_wait(i, 1, 1)
         hop(i, 5, 1, 2, right)
+
+    def ring_back(i):
         ring_wait(i, 4, 7)
         hop(i, 6, 7, 6, left)
 
@@ -402,8 +414,7 @@
     half = o_weight.shape[0] // 2
 
     def spot(dz, side):
-        there = (z + dz + 4) % 4 * 2 + side
-        return (h + there // 4) % 2 * 4 + (x - there % 4 + 4) % 4
+        return (z + dz + 4) % 4 * 2 + side
 
     def term(i, dz, side, which, part):
         rows = pl.ds(pl.multiple_of(which * half, half), half)
@@ -479,20 +490,25 @@
     def columns(t):
         return mixed.at[:, pl.ds(pl.multiple_of(t * tp_width, tp_width), tp_width)]
 
+    def tp_at(dz, dl, dc=0):
+        level, side = (z + dz + 4) % 4, (low + dl) % 2
+        owner = (h + level // 2) % 2 * 4 + (x + level % 2 * 2 + side) % 4
+        return owner * 2 + (core + dc) % 2
+
     def last_target(i):
-        return columns(tp) if i == 0 else last_recv
+        return columns(tp_at(0, 0)) if i == 0 else last_recv
 
     def last_level(i):
         arrived(side_recv.at[i], side_sems.at[i, 1])
         terms = (level_recv.at[i, 2 + low], level_recv.at[i, 4 + low], side_recv.at[i])
         add_up(i, 3, low, last_send.at[i], terms)
-        there = columns(home[1]) if i == 0 else last_recv
-
-        @pl.when(away)
+        there = columns(blk * 2 + core) if i == 0 else last_recv
+
+        @pl.when(jnp.logical_not(stays[i]))
         def _():
-            send(last_send.at[i], there, (hand_s.at[i], hand_r.at[i]), home)
-
-        @pl.when(group == blk)
+            send(last_send.at[i], there, (hand_s.at[i], hand_r.at[i]), homes[i])
+
+        @pl.when(stays[i])
         def _():
             pltpu.make_async_copy(last_send.at[i], last_target(i), hand_r.at[i]).start()
 
@@ -500,55 +516,85 @@
         arrived(last_target(i), hand_r.at[i])
 
     def hand_sent(i):
-        @pl.when(away)
+        @pl.when(jnp.logical_not(stays[i]))
         def _():
             arrived(last_send.at[i], hand_s.at[i])
 
-    def tp_at(dz, dl, dc=0):
-        return (z + dz + 4) % 4 * 4 + (low + dl) % 2 * 2 + (core + dc) % 2
-
-    def mixed_hop(k, t, device):
-        post(columns(t), columns(t), (mixed_s.at[k], mixed_r.at[k]), device)
-
-    def mixed_wait(k, t):
-        arrived(columns(t), mixed_r.at[k])
-
-    def mixed_twin(k, t):
-        post(columns(t), columns(t), (twin_s.at[k], twin_r.at[k]), twin)
+    whole, top, bottom = (0, length), (0, tile), (tile, tile)
+    quarters = ((tile, tile // 2), (tile + tile // 2, tile // 2))
+
+    def cell(t, rows):
+        return columns(t).at[pl.ds(*rows)]
+
+    def mixed_hop(k, t, rows, device):
+        post(cell(t, rows), cell(t, rows), (mixed_s.at[k], mixed_r.at[k]), device)
+
+    def mixed_wait(k, t, rows):
+        arrived(cell(t, rows), mixed_r.at[k])
+
+    given = []
+
+    def mixed_twin(dz, dl, rows):
+        k, t = len(given), tp_at(dz, dl)
+        given.append((tp_at(dz, dl, 1), rows))
+        post(cell(t, rows), cell(t, rows), (twin_s.at[k], twin_r.at[k]), twin)
 
     def mixed_start():
         hand_end(0)
-        mixed_hop(0, tp, beside)
-        mixed_hop(1, tp, above)
-        mixed_hop(2, tp, below)
-        mixed_twin(0, tp)
+        mixed_hop(0, tp_at(0, 0), top, beside)
+        mixed_hop(7, tp_at(0, 0), bottom, above)
+        mixed_hop(8, tp_at(0, 0), bottom, below)
+        mixed_hop(1, tp_at(0, 0), top, above)
+        mixed_hop(2, tp_at(0, 0), top, below)
+        mixed_hop(11, tp_at(0, 0), bottom, beside)
+        mixed_twin(0, 0, whole)
 
     def mixed_side():
-        mixed_wait(0, tp_at(0, 1))
-        mixed_hop(3, tp_at(0, 1), above)
-        mixed_hop(4, tp_at(0, 1), below)
-        mixed_twin(1, tp_at(0, 1))
-
-    def mixed_forward():
-        mixed_wait(1, tp_at(-1, 0))
-        mixed_hop(5, tp_at(-1, 0), above)
-        mixed_twin(2, tp_at(-1, 0))
-        mixed_wait(2, tp_at(1, 0))
-        mixed_twin(3, tp_at(1, 0))
-        mixed_wait(4, tp_at(1, 1))
-        mixed_hop(6, tp_at(1, 1), below)
-        mixed_twin(4, tp_at(1, 1))
+        mixed_wait(0, tp_at(0, 1), top)
+        mixed_hop(3, tp_at(0, 1), top, above)
+        mixed_hop(4, tp_at(0, 1), top, below)
+        mixed_twin(0, 1, top)
+
+    def mixed_bottom():
+        mixed_wait(7, tp_at(-1, 0), bottom)
+        mixed_hop(9, tp_at(-1, 0), quarters[0], above)
+        mixed_hop(12, tp_at(-1, 0), bottom, beside)
+        mixed_twin(-1, 0, bottom)
+        mixed_wait(8, tp_at(1, 0), bottom)
+        mixed_hop(10, tp_at(1, 0), quarters[1], below)
+        mixed_hop(13, tp_at(1, 0), bottom, beside)
+        mixed_twin(1, 0, bottom)
+
+    def mixed_pass():
+        mixed_wait(1, tp_at(-1, 0), top)
+        mixed_hop(5, tp_at(-1, 0), top, above)
+        mixed_twin(-1, 0, top)
+        mixed_wait(2, tp_at(1, 0), top)
+        mixed_twin(1, 0, top)
+
+    def mixed_back():
+        mixed_wait(4, tp_at(1, 1), top)
+        mixed_hop(6, tp_at(1, 1), top, below)
+        mixed_twin(1, 1, top)
+
+    def mixed_far():
+        mixed_wait(9, tp_at(2, 0), quarters[0])
+        mixed_wait(10, tp_at(2, 0), quarters[1])
+        mixed_hop(14, tp_at(2, 0), bottom, beside)
+        mixed_twin(2, 0, bottom)
+        mixed_wait(11, tp_at(0, 1), bottom)
+        mixed_twin(0, 1, bottom)
+        mixed_wait(12, tp_at(-1, 1), bottom)
+        mixed_twin(-1, 1, bottom)
+        mixed_wait(13, tp_at(1, 1), bottom)
+        mixed_twin(1, 1, bottom)
 
     def mixed_end():
-        mixed_wait(3, tp_at(-1, 1))
-        mixed_twin(5, tp_at(-1, 1))
-        mixed_wait(5, tp_at(2, 0))
-        mixed_twin(6, tp_at(2, 0))
-        mixed_wait(6, tp_at(2, 1))
-        mixed_twin(7, tp_at(2, 1))
-        sources = ((0, 0), (0, 1), (-1, 0), (1, 0), (1, 1), (-1, 1), (2, 0), (2, 1))
-        for k, (dz, dl) in enumerate(sources):
-            arrived(columns(tp_at(dz, dl, 1)), twin_r.at[k])
+        for k, dz, dl, rows in ((3, -1, 1, top), (5, 2, 0, top), (6, 2, 1, top), (14, 2, 1, bottom)):
+            mixed_wait(k, tp_at(dz, dl), rows)
+            mixed_twin(dz, dl, rows)
+        for k, (t, rows) in enumerate(given):
+            arrived(cell(t, rows), twin_r.at[k])
 
     sources = (cot_blocks, token_blocks)
     order = (0, 4, 1, 3, 5, 7, 2, 6)
@@ -585,21 +631,26 @@
     load(0)
     load(1)
     ring_across(1)
+    grad_step(0)
     ring_side(0)
-    grad_step(0)
-    ring_forward(0)
+    grad_step(1)
+    ring_pass(0)
+    grad_step(2)
+    ring_back(0)
     ring_start(1)
     ring_side(1)
-    grad_step(1)
     ring_end(0)
     give_half(0)
     far_level(0)
     near_level(0)
-    grad_step(2)
-    ring_forward(1)
+    ring_pass(1)
+    grad_step(3)
     pass_level(0)
-    for n in range(3, 8):
-        grad_step(n)
+    grad_step(4)
+    grad_step(5)
+    ring_back(1)
+    grad_step(6)
+    grad_step(7)
     own_level(0)
     ring_end(1)
     give_half(1)
@@ -607,19 +658,22 @@
     last_level(0)
     near_level(1)
     grad_step(8)
+    pass_level(1)
+    mixed_start()
     grad_step(9)
-    mixed_start()
-    pass_level(1)
     grad_step(10)
     grad_step(11)
     mixed_side()
     grad_step(12)
+    own_level(1)
+    mixed_bottom()
     grad_step(13)
-    mixed_forward()
-    own_level(1)
+    mixed_pass()
     grad_step(14)
     grad_step(15)
     last_level(1)
+    mixed_far()
+    mixed_back()
     mixed_end()
     hand_end(1)
     out = pltpu.make_async_copy(last_recv, d_tokens, out_sem)
@@ -687,10 +741,10 @@
             dma((2, 2)),
             dma((2,)),
             dma((2,)),
-            dma((7,)),
-            dma((7,)),
-            dma((8,)),
-            dma((8,)),
+            dma((15,)),
+            dma((15,)),
+            dma((15,)),
+            dma((15,)),
             dma((2,)),
             dma,
         ],

time: 389 us -> 344 us (0.88)
  the two profiles are of different devices: /device:TPU:120 before, /device:TPU:15 now
where the time goes in v5:
time: 344 us
  Pallas kernels  326 us (95%)
  local copies, waits for them, and re-layouts  15.7 us (5%)
    pallas_call x1, Pallas kernels, finish(): pl.pallas_call(finish_kernel, out_shape=(jax.ShapeDtypeStruct((length, 16...  192 us
    pallas_call x1, Pallas kernels, project(): pl.pallas_call(project_kernel, out_shape=(block, block, jax.ShapeDtypeStr...  134 us
    unnamed x20, local copies, waits for them, and re-layouts  14 us

profile of v5, /device:TPU:15, one launch (start us, length us, event | category | flops | bytes accessed | tf_op | source)
XLA Modules:
  0.0 344.1 jit_solution(16184187991118420832)
XLA Ops:
  0.6 0.0 copy-start.1
  0.7 1.6 copy.11.seg_col
  2.3 1.0 fusion.2
  3.3 1.0 pad_maximum_fusion
  4.3 0.0 copy-start.5
  4.3 0.0 copy-done.1
  4.3 0.1 constant_dynamic-update-slice_fusion.1
  4.3 0.9 copy-done.5
  5.2 0.1 constant_dynamic-update-slice_fusion.in_weight
  5.3 0.0 copy-start
  5.3 1.0 copy-done
  6.3 133.6 %project.1 = (bf16[8,512,1024]{2,1,0:T(8,128)(2,1)}, bf16[8,512,1024]{2,1,0:T(8,128)(2,1)}, f32[512,640]{1,0:T(8,128)}, bf16[512,512]{1,0:T(8,128)(2,1)}) custom-call(bf16[512,8192]{1,0:T(8,128)(2,1)} %tokens.1, bf16[512,8192]{1,0:T(8,128)(2,1)} %cot.1, bf16[1024,640]{1,0:T(8,128)(2,1)} %copy-done, bf16[1024,512]{1,0:T(8,128)(2,1)} %o_weight.3), custom_call_target="tpu_custom_call" | custom-call | tf_op jit(solution)/shard_map/project/pallas_call | solution.py:206
  139.9 192.2 %finish.1 = (bf16[512,8192]{1,0:T(8,128)(2,1)}, bf16[512,512]{1,0:T(8,128)(2,1)}, bf16[1024,512]{1,0:T(8,128)(2,1)}, bf16[1024,128]{1,0:T(8,128)(2,1)}, bf16[1024,512]{1,0:T(8,128)(2,1)}) custom-call(f32[512,640]{1,0:T(8,128)} %get-tuple-element.9.proj, bf16[512,512]{1,0:T(8,128)(2,1)} %get-tuple-element.10.d_attn, f32[512,128]{1,0:T(8,128)} %get-tuple-element.16.cosine, ...), custom_call_target="tpu_custom_call" | custom-call | tf_op jit(solution)/shard_map/finish/pallas_call | solution.py:699
  332.1 0.0 copy-start.4
  332.1 7.8 %copy.18 = bf16[512,8192]{1,0:T(8,128)(2,1)} copy(bf16[512,8192]{1,0:T(8,128)(2,1)} %get-tuple-element.23) | data formatting | bytes 16777216
  339.9 0.0 copy-done.4
  339.9 0.0 copy-start.3
  339.9 0.8 copy.19
  340.7 0.6 copy-done.3
  341.4 0.0 copy-start.6
  341.4 0.0 copy-start.2
  341.4 1.0 copy.20
  342.3 0.1 copy-done.6
  342.4 0.7 copy.21
  343.1 0.0 copy-done.2
  343.2 1.0 copy.22
  (1 shorter events, 0.0 us)
Async XLA Ops:
  0.6 3.6 %copy-start.1 = (bf16[1024,512]{1,0:T(8,128)(2,1)S(1)}, bf16[1024,512]{1,0:T(8,128)(2,1)}, u32[]{:S(2)}) copy-start(bf16[1024,512]{1,0:T(8,128)(2,1)} %param.8) | copy-start | bytes 3145732
  4.3 0.9 copy-start.5
  5.3 1.1 copy-start
  332.1 7.8 %copy-start.4 = (bf16[512,512]{1,0:T(8,128)(2,1)S(1)}, bf16[512,512]{1,0:T(8,128)(2,1)}, u32[]{:S(2)}) copy-start(bf16[512,512]{1,0:T(8,128)(2,1)} %get-tuple-element.24) | copy-start | bytes 1572868
  339.9 1.4 copy-start.3
  341.4 1.1 copy-start.6
  341.4 1.8 copy-start.2

commit v6 on v5

--- a/solution.py
+++ b/solution.py
@@ -63,12 +63,25 @@
     pltpu.make_async_copy(ref, ref, sem).wait()
 
 
+def load_weights(q_weight, kv_weight, o_source, in_weight, o_weight, sems):
+    width = q_weight.shape[1]
+    kv_part = pl.ds(width, kv_weight.shape[1])
+    loads = [
+        pltpu.make_async_copy(q_weight, in_weight.at[:, pl.ds(0, width)], sems.at[0]),
+        pltpu.make_async_copy(kv_weight, in_weight.at[:, kv_part], sems.at[1]),
+        pltpu.make_async_copy(o_source, o_weight, sems.at[2]),
+    ]
+    for held in loads:
+        held.start()
+    return loads
+
+
 CHUNKS = ((0, 2), (1, 2), (1, 1), (0, 3), (0, 1), (1, 3), (1, 0), (0, 0))
 
 
 def project_kernel(
-    tokens, cot, in_weight, o_weight, token_out, cot_out, proj_out, d_attn_out,
-    blocks, proj_send, proj_recv, cot_send, cot_recv,
+    tokens, cot, q_weight, kv_weight, o_source, token_out, cot_out, proj_out, d_attn_out,
+    in_weight, o_weight, weight_sem, blocks, proj_send, proj_recv, cot_send, cot_recv,
     a2a_s, a2a_r, up_s, up_r, down_s, down_r, far_s, far_r, core_s, core_r, sum_s, sum_r, keep,
 ):
     place = here()
@@ -80,6 +93,7 @@
     above, below = near(place, dz=1), near(place, dz=-1)
     twin, across = near(place, dc=1), near(place, dh=1)
     shifts = [shift for shift in CHUNKS if shift != (0, 0)]
+    loads = load_weights(q_weight, kv_weight, o_source, in_weight, o_weight, weight_sem)
     greet([near(place, dh=dh, dx=dx) for dh, dx in shifts] + [above, below, twin])
     sent = []
 
@@ -181,6 +195,9 @@
             if 0 <= step - lag < len(pieces):
                 a, k = pieces[step - lag]
                 stage(a, *CHUNKS[k])
+        if step == 4:
+            for held in loads:
+                held.wait()
         while waiting and pieces.index(waiting[0]) + late.get(waiting[0], 5) <= step:
             chunk(*waiting.pop(0))
     assert not waiting
@@ -196,10 +213,11 @@
         copy.wait()
 
 
-def project(tokens, cot, in_weight, o_weight):
+def project(tokens, cot, q_weight, kv_weight, o_weight):
     length = tokens.shape[0]
     width = tokens.shape[1] // 8
-    in_width, o_width = in_weight.shape[1], o_weight.shape[1]
+    in_width, o_width = q_weight.shape[1] + kv_weight.shape[1], o_weight.shape[1]
+    depth = q_weight.shape[0]
     dma = pltpu.SemaphoreType.DMA
     pair = [dma((2, 8)), dma((2, 8))]
     block = jax.ShapeDtypeStruct((8, length, width), BF16)
@@ -211,11 +229,13 @@
             jax.ShapeDtypeStruct((length, in_width), F32),
             jax.ShapeDtypeStruct((length, o_width), BF16),
         ),
-        in_specs=[pl.BlockSpec(memory_space=pl.ANY)] * 2
-        + [pl.BlockSpec(memory_space=pltpu.VMEM)] * 2,
+        in_specs=[pl.BlockSpec(memory_space=pl.ANY)] * 5,
         out_specs=(pl.BlockSpec(memory_space=pl.ANY),) * 2
         + (pl.BlockSpec(memory_space=pltpu.VMEM),) * 2,
         scratch_shapes=[
+            pltpu.VMEM((depth, in_width), BF16),
+            pltpu.VMEM((depth, o_width), BF16),
+            dma((3,)),
             pltpu.VMEM((2, 8, length, width), BF16),
             pltpu.VMEM((7, length, in_width), BF16),
             pltpu.VMEM((7, length, in_width), BF16),
@@ -235,7 +255,7 @@
             collective_id=0, has_side_effects=True, vmem_limit_bytes=56 * MIB
         ),
         name="project",
-    )(tokens, cot, in_weight, o_weight)
+    )(tokens, cot, q_weight, kv_weight, o_weight)
 
 
 def nt(left, right):
@@ -254,13 +274,15 @@
 
 
 def finish_kernel(
-    proj, d_attn, cosine, sine, seg_col, seg_row, in_weight, o_weight, token_blocks, cot_blocks,
-    mixed, d_tokens, q_grad, kv_grad, o_grad,
-    attn_all, grad_all, q_rot, probs, bias, keys, values, kv_send, kv_recv, key_sum, value_sum,
+    proj, d_attn, cosine, sine, seg_row, q_weight, kv_weight, o_source, token_blocks, cot_blocks,
+    mixed, d_tokens, q_grad, kv_grad, o_grad, in_weight, o_weight, weight_sem,
+    attn_all, grad_all, q_rot, probs, bias, seg_cols, keys, values, kv_send, kv_recv, key_sum, value_sum,
     kv_grad_send, kv_grad_recv,
-    half_send, half_recv, level_send, level_recv, side_send, side_recv, last_send, last_recv,
+    half_send, half_recv, level_send, level_recv, side_send, side_recv, cross_send, cross_recv,
+    plane_send, plane_recv, last_send, last_recv,
     column, grad_sum,
-    kv_sems, ring_s, ring_r, half_s, half_r, level_s, level_r, side_sems, hand_s, hand_r,
+    kv_sems, ring_s, ring_r, half_s, half_r, level_s, level_r, side_sems, cross_s, cross_r,
+    plane_s, plane_r, hand_s, hand_r,
     mixed_s, mixed_r, twin_s, twin_r, column_sem, out_sem,
 ):
     place = here()
@@ -286,6 +308,7 @@
     )
     stays = (z * 2 + low == 0, z * 2 + low + blk == 0)
     sent, halves = [], []
+    loads = load_weights(q_weight, kv_weight, o_source, in_weight, o_weight, weight_sem)
 
     barrier = pltpu.get_barrier_semaphore()
     for device in (right, left, above, below, twin, across, beside):
@@ -306,6 +329,8 @@
     is_lower = jnp.full((length, HEAD_SIZE), core) == 0
     kv_send[...] = proj[:, q_width:].astype(BF16)
     post(kv_send, kv_recv, (kv_sems.at[0], kv_sems.at[1]), twin)
+    seg_col = jnp.transpose(jnp.broadcast_to(seg_row[...].astype(F32), (HEAD_SIZE, length)))[:, :1]
+    seg_cols[...] = jnp.broadcast_to(seg_col, seg_cols.shape)
 
     @pl.loop(0, 2)
     def _(step):
@@ -313,7 +338,7 @@
         part = pl.ds(start, tile)
         row = lax.broadcasted_iota(jnp.int32, (tile, length), 0) + start
         key = lax.broadcasted_iota(jnp.int32, (tile, length), 1)
-        allowed = (key <= row) & (seg_col[part, :] == seg_row[...])
+        allowed = (key <= row) & (seg_cols[part, :1] == seg_row[...].astype(F32))
         bias[part, :] = jnp.where(allowed, 0.0, -jnp.inf)
 
     @pl.loop(0, q_width // HEAD_SIZE)
@@ -437,15 +462,15 @@
     def half_wait(i, q):
         arrived(half_recv.at[i, q], half_r.at[i, q])
 
-    def add_up(i, q, side, target, terms):
-        @pl.loop(0, 2)
-        def _(step):
-            part = pl.ds(pl.multiple_of(step * tile, tile), tile)
-            total = term(i, LEVELS[q], side, core, part)
-            total = total + half_recv[i, q, side, part, :].astype(F32)
-            for ref in terms:
-                total = total + ref[part, :].astype(F32)
-            target[part, :] = total.astype(target.dtype)
+    def add_up(i, q, side, target, first, count, terms):
+        part = pl.ds(first, count)
+        total = term(i, LEVELS[q], side, core, part)
+        total = total + half_recv[i, q, side, part, :].astype(F32)
+        for ref in terms:
+            total = total + ref[...].astype(F32)
+        target[...] = total.astype(target.dtype)
+
+    few = tile // 2
 
     def level_hop(i, k, slot, device):
         sems = (level_s.at[i, k], level_r.at[i, slot])
@@ -454,35 +479,68 @@
     def level_wait(i, slot):
         arrived(level_recv.at[i, slot], level_r.at[i, slot])
 
+    def cross(i, q):
+        add_up(i, q, 1 - low, cross_send.at[i, q], tile, tile, ())
+        post(cross_send.at[i, q], cross_recv.at[i, q], (cross_s.at[i, q], cross_r.at[i, q]), beside)
+
+    def cross_wait(i, q):
+        arrived(cross_recv.at[i, q], cross_r.at[i, q])
+
+    def slab(ref, which):
+        return ref.at[pl.ds(which * few, few)]
+
     def far_level(i):
         half_wait(i, 0)
-        add_up(i, 0, 0, level_send.at[i, 0], ())
+        cross(i, 0)
+        add_up(i, 0, 0, level_send.at[i, 0], 0, tile, ())
         level_hop(i, 0, 0, below)
-        add_up(i, 0, 1, level_send.at[i, 1], ())
+        add_up(i, 0, 1, level_send.at[i, 1], 0, tile, ())
         level_hop(i, 1, 1, above)
 
     def near_level(i):
         half_wait(i, 1)
-        add_up(i, 1, 1, level_send.at[i, 2], ())
+        cross(i, 1)
+        add_up(i, 1, 1, level_send.at[i, 2], 0, tile, ())
         level_hop(i, 2, 3, below)
         half_wait(i, 2)
-        add_up(i, 2, 0, level_send.at[i, 3], ())
+        cross(i, 2)
+        add_up(i, 2, 0, level_send.at[i, 3], 0, tile, ())
         level_hop(i, 3, 4, above)
+        half_wait(i, 3)
+        cross(i, 3)
+
+    def far_plane(i):
+        cross_wait(i, 0)
+        add_up(i, 0, low, plane_send.at[i, 0], tile, tile, (cross_recv.at[i, 0],))
+        for which, k, device in ((0, 0, below), (1, 3, above)):
+            sems = (plane_s.at[i, k], plane_r.at[i, k])
+            post(slab(plane_send.at[i, 0], which), slab(plane_recv.at[i, 0], which), sems, device)
 
     def pass_level(i):
         level_wait(i, 0)
-        add_up(i, 1, 0, level_send.at[i, 4], (level_recv.at[i, 0],))
+        add_up(i, 1, 0, level_send.at[i, 4], 0, tile, (level_recv.at[i, 0],))
         level_hop(i, 4, 2, below)
         level_wait(i, 1)
-        add_up(i, 2, 1, level_send.at[i, 5], (level_recv.at[i, 1],))
+        add_up(i, 2, 1, level_send.at[i, 5], 0, tile, (level_recv.at[i, 1],))
         level_hop(i, 5, 5, above)
 
+    def pass_plane(i):
+        for q, joins, k, device in ((1, 0, 0, below), (2, 1, 3, above)):
+            cross_wait(i, q)
+            arrived(slab(plane_recv.at[i, 0], joins), plane_r.at[i, k])
+            for which in range(2):
+                terms = [slab(cross_recv.at[i, q], which)]
+                if which == joins:
+                    terms.append(slab(plane_recv.at[i, 0], which))
+                add_up(i, q, low, slab(plane_send.at[i, q], which), tile + which * few, few, terms)
+            sems = (plane_s.at[i, q], plane_r.at[i, q])
+            post(plane_send.at[i, q], plane_recv.at[i, q], sems, device)
+
     def own_level(i):
-        half_wait(i, 3)
         for slot in range(2, 6):
             level_wait(i, slot)
         terms = (level_recv.at[i, 2 + 1 - low], level_recv.at[i, 4 + 1 - low])
-        add_up(i, 3, 1 - low, side_send.at[i], terms)
+        add_up(i, 3, 1 - low, side_send.at[i], 0, tile, terms)
         post(side_send.at[i], side_recv.at[i], (side_sems.at[i, 0], side_sems.at[i, 1]), beside)
 
     tp_width = half
@@ -499,9 +557,14 @@
         return columns(tp_at(0, 0)) if i == 0 else last_recv
 
     def last_level(i):
+        cross_wait(i, 3)
+        for q in (1, 2):
+            arrived(plane_recv.at[i, q], plane_r.at[i, q])
+        terms = (cross_recv.at[i, 3], plane_recv.at[i, 1], plane_recv.at[i, 2])
+        add_up(i, 3, low, last_send.at[i, pl.ds(tile, tile)], tile, tile, terms)
         arrived(side_recv.at[i], side_sems.at[i, 1])
         terms = (level_recv.at[i, 2 + low], level_recv.at[i, 4 + low], side_recv.at[i])
-        add_up(i, 3, low, last_send.at[i], terms)
+        add_up(i, 3, low, last_send.at[i, pl.ds(0, tile)], 0, tile, terms)
         there = columns(blk * 2 + core) if i == 0 else last_recv
 
         @pl.when(jnp.logical_not(stays[i]))
@@ -640,35 +703,41 @@
     ring_start(1)
     ring_side(1)
     ring_end(0)
+    for held in loads:
+        held.wait()
     give_half(0)
     far_level(0)
     near_level(0)
     ring_pass(1)
+    far_plane(0)
+    pass_level(0)
     grad_step(3)
-    pass_level(0)
     grad_step(4)
+    pass_plane(0)
     grad_step(5)
     ring_back(1)
+    own_level(0)
     grad_step(6)
     grad_step(7)
-    own_level(0)
+    last_level(0)
     ring_end(1)
     give_half(1)
     far_level(1)
-    last_level(0)
     near_level(1)
-    grad_step(8)
+    far_plane(1)
     pass_level(1)
     mixed_start()
+    grad_step(8)
     grad_step(9)
+    pass_plane(1)
     grad_step(10)
+    mixed_side()
     grad_step(11)
-    mixed_side()
-    grad_step(12)
     own_level(1)
     mixed_bottom()
+    grad_step(12)
+    mixed_pass()
     grad_step(13)
-    mixed_pass()
     grad_step(14)
     grad_step(15)
     last_level(1)
@@ -685,10 +754,10 @@
     out.wait()
 
 
-def finish(proj, d_attn, cosine, sine, segments, in_weight, o_weight, token_blocks, cot_blocks):
+def finish(proj, d_attn, cosine, sine, segments, weights, blocks):
     length, q_width = d_attn.shape
-    in_width = in_weight.shape[1]
-    depth = in_weight.shape[0]
+    in_width = proj.shape[1]
+    depth = weights[0].shape[0]
     half = depth // 2
     heads = q_width // HEAD_SIZE
     dma = pltpu.SemaphoreType.DMA
@@ -705,14 +774,18 @@
             jax.ShapeDtypeStruct((depth, in_width - q_width), BF16),
             jax.ShapeDtypeStruct((depth, q_width), BF16),
         ),
-        in_specs=[vmem] * 8 + [hbm] * 2,
+        in_specs=[vmem] * 5 + [hbm] * 5,
         out_specs=(hbm, hbm, vmem, vmem, vmem),
         scratch_shapes=[
+            pltpu.VMEM((depth, in_width), BF16),
+            pltpu.VMEM((depth, q_width), BF16),
+            dma((3,)),
             pltpu.VMEM((8, length, q_width), BF16),
             pltpu.VMEM((8, length, in_width), BF16),
             pltpu.VMEM((length, q_width), BF16),
             pltpu.VMEM((heads, length, length), F32),
             pltpu.VMEM((length, length), F32),
+            pltpu.VMEM((length, HEAD_SIZE), F32),
             part,
             part,
             part,
@@ -723,10 +796,14 @@
             part,
             pltpu.VMEM((4, 2, length, half), BF16),
             pltpu.VMEM((2, 4, 2, length, half), BF16),
-            pltpu.VMEM((2, 6, length, half), BF16),
-            pltpu.VMEM((2, 6, length, half), BF16),
-            pltpu.VMEM((2, length, half), BF16),
-            pltpu.VMEM((2, length, half), BF16),
+            pltpu.VMEM((2, 6, length // 2, half), BF16),
+            pltpu.VMEM((2, 6, length // 2, half), BF16),
+            pltpu.VMEM((2, length // 2, half), BF16),
+            pltpu.VMEM((2, length // 2, half), BF16),
+            pltpu.VMEM((2, 4, length // 2, half), BF16),
+            pltpu.VMEM((2, 4, length // 2, half), BF16),
+            pltpu.VMEM((2, 3, length // 2, half), BF16),
+            pltpu.VMEM((2, 3, length // 2, half), BF16),
             pltpu.VMEM((2, length, half), BF16),
             pltpu.VMEM((length, half), BF16),
             pltpu.VMEM((2, length, depth), BF16),
@@ -739,6 +816,10 @@
             dma((2, 6)),
             dma((2, 6)),
             dma((2, 2)),
+            dma((2, 4)),
+            dma((2, 4)),
+            dma((2, 4)),
+            dma((2, 4)),
             dma((2,)),
             dma((2,)),
             dma((15,)),
@@ -753,20 +834,18 @@
         ),
         name="finish",
     )(
-        proj, d_attn, cosine, sine, segments.reshape(length, 1), segments.reshape(1, length),
-        in_weight, o_weight, token_blocks, cot_blocks,
+        proj, d_attn, cosine, sine, segments, *weights, *blocks
     )
 
 
 def shards(tokens, segment_ids, q_weight, key_value_weight, o_weight, cotangent):
-    in_weight = jnp.concatenate([q_weight, key_value_weight], axis=1)
-    token_blocks, cot_blocks, proj, d_attn = project(tokens, cotangent, in_weight, o_weight)
+    weights = (q_weight, key_value_weight, o_weight)
+    token_blocks, cot_blocks, proj, d_attn = project(tokens, cotangent, *weights)
     cosine, sine = rope_tables(tokens.shape[0], HEAD_SIZE)
     cosine = jnp.concatenate([cosine, cosine], axis=1)
     sine = jnp.concatenate([-sine, sine], axis=1)
-    return finish(
-        proj, d_attn, cosine, sine, segment_ids[0], in_weight, o_weight, token_blocks, cot_blocks
-    )
+    blocks = (token_blocks, cot_blocks)
+    return finish(proj, d_attn, cosine, sine, segment_ids, weights, blocks)
 
 
 def solution(mesh):

time: 344 us -> 336 us (0.977)
  the two profiles are of different devices: /device:TPU:15 before, /device:TPU:73 now
where the time goes in v6:
time: 336 us
  Pallas kernels  322 us (96%)
  local copies, waits for them, and re-layouts  11.4 us (3%)
    pallas_call x1, Pallas kernels, finish(): pl.pallas_call(finish_kernel, out_shape=(jax.ShapeDtypeStruct((length, 16...  195 us
    pallas_call x1, Pallas kernels, project(): pl.pallas_call(project_kernel, out_shape=(block, block, jax.ShapeDtypeStr...  127 us
    unnamed x13, local copies, waits for them, and re-layouts  11.4 us

profile of v6, /device:TPU:73, one launch (start us, length us, event | category | flops | bytes accessed | tf_op | source)
XLA Modules:
  0.0 336.0 jit_solution(17184289071628300781)
XLA Ops:
  0.6 1.0 fusion.2
  1.6 1.0 pad_maximum_fusion
  2.6 126.8 %project.1 = (bf16[8,512,1024]{2,1,0:T(8,128)(2,1)}, bf16[8,512,1024]{2,1,0:T(8,128)(2,1)}, f32[512,640]{1,0:T(8,128)}, bf16[512,512]{1,0:T(8,128)(2,1)}) custom-call(bf16[512,8192]{1,0:T(8,128)(2,1)} %tokens.1, bf16[512,8192]{1,0:T(8,128)(2,1)} %cot.1, bf16[1024,512]{1,0:T(8,128)(2,1)} %q_weight.3, bf16[1024,128]{1,0:T(8,128)(2,1)} %kv_weight.3, ...), custom_call_target="tpu_custom_call" | custom-call | tf_op jit(solution)/shard_map/project/pallas_call | solution.py:224
  129.4 195.2 %finish.1 = (bf16[512,8192]{1,0:T(8,128)(2,1)}, bf16[512,512]{1,0:T(8,128)(2,1)}, bf16[1024,512]{1,0:T(8,128)(2,1)}, bf16[1024,128]{1,0:T(8,128)(2,1)}, bf16[1024,512]{1,0:T(8,128)(2,1)}) custom-call(f32[512,640]{1,0:T(8,128)} %get-tuple-element.9.proj, bf16[512,512]{1,0:T(8,128)(2,1)} %get-tuple-element.10.d_attn, f32[512,128]{1,0:T(8,128)} %get-tuple-element.16.cosine, ...), custom_call_target="tpu_custom_call" | custom-call | tf_op jit(solution)/shard_map/finish/pallas_call | solution.py:768
  324.6 0.0 copy-start.2
  324.6 0.0 copy-start.1
  324.6 0.0 copy-start.3
  324.7 0.0 copy-start
  324.7 7.9 %copy.16 = bf16[512,8192]{1,0:T(8,128)(2,1)} copy(bf16[512,8192]{1,0:T(8,128)(2,1)} %get-tuple-element.23) | data formatting | bytes 16777216
  332.6 0.0 copy-done.2
  332.6 0.8 copy.17
  333.4 0.0 copy-done.1
  333.4 1.0 copy.18
  334.4 0.0 copy-done.3
  334.4 0.7 copy.19
  335.1 0.0 copy-done
  335.1 1.0 copy.20
  (1 shorter events, 0.0 us)
Async XLA Ops:
  324.6 8.0 %copy-start.2 = (bf16[512,512]{1,0:T(8,128)(2,1)S(1)}, bf16[512,512]{1,0:T(8,128)(2,1)}, u32[]{:S(2)}) copy-start(bf16[512,512]{1,0:T(8,128)(2,1)} %get-tuple-element.24) | copy-start | bytes 1572868
  324.6 8.8 %copy-start.1 = (bf16[1024,512]{1,0:T(8,128)(2,1)S(1)}, bf16[1024,512]{1,0:T(8,128)(2,1)}, u32[]{:S(2)}) copy-start(bf16[1024,512]{1,0:T(8,128)(2,1)} %get-tuple-element.25) | copy-start | bytes 3145732
  324.6 9.7 %copy-start.3 = (bf16[1024,128]{1,0:T(8,128)(2,1)S(1)}, bf16[1024,128]{1,0:T(8,128)(2,1)}, u32[]{:S(2)}) copy-start(bf16[1024,128]{1,0:T(8,128)(2,1)} %get-tuple-element.26) | copy-start | bytes 786436
  324.7 10.4 %copy-start = (bf16[1024,512]{1,0:T(8,128)(2,1)S(1)}, bf16[1024,512]{1,0:T(8,128)(2,1)}, u32[]{:S(2)}) copy-start(bf16[1024,512]{1,0:T(8,128)(2,1)} %get-tuple-element.27) | copy-start | bytes 3145732

commit v7 on v6

--- a/solution.py
+++ b/solution.py
@@ -838,6 +838,42 @@
     )
 
 
+def settle_kernel(*refs):
+    count = (len(refs) - 2) // 3
+    sources, targets, buffers = refs[:count], refs[count : 2 * count], refs[2 * count : 3 * count]
+    in_sems, out_sems = refs[-2:]
+    parts = []
+    for source, target, buffer in zip(sources, targets, buffers, strict=True):
+        pieces = 16 if source.shape[1] > 1024 else 2
+        rows = source.shape[0] // pieces
+        for piece in range(pieces):
+            part = pl.ds(piece * rows, rows)
+            parts.append((source.at[part], buffer.at[part], target.at[part]))
+    ins = [pltpu.make_async_copy(a, b, in_sems.at[n]) for n, (a, b, _) in enumerate(parts)]
+    outs = [pltpu.make_async_copy(b, c, out_sems.at[n]) for n, (_, b, c) in enumerate(parts)]
+    for copy in ins:
+        copy.start()
+    for arrival, copy in zip(ins, outs, strict=True):
+        arrival.wait()
+        copy.start()
+    for copy in outs:
+        copy.wait()
+
+
+def settle(arrays):
+    hbm = pl.BlockSpec(memory_space=pl.ANY)
+    return pl.pallas_call(
+        settle_kernel,
+        out_shape=tuple(jax.ShapeDtypeStruct(a.shape, a.dtype) for a in arrays),
+        in_specs=[hbm] * len(arrays),
+        out_specs=(hbm,) * len(arrays),
+        scratch_shapes=[pltpu.VMEM(a.shape, a.dtype) for a in arrays]
+        + [pltpu.SemaphoreType.DMA((24,)), pltpu.SemaphoreType.DMA((24,))],
+        compiler_params=pltpu.CompilerParams(vmem_limit_bytes=63 * MIB),
+        name="settle",
+    )(*arrays)
+
+
 def shards(tokens, segment_ids, q_weight, key_value_weight, o_weight, cotangent):
     weights = (q_weight, key_value_weight, o_weight)
     token_blocks, cot_blocks, proj, d_attn = project(tokens, cotangent, *weights)
@@ -845,7 +881,7 @@
     cosine = jnp.concatenate([cosine, cosine], axis=1)
     sine = jnp.concatenate([-sine, sine], axis=1)
     blocks = (token_blocks, cot_blocks)
-    return finish(proj, d_attn, cosine, sine, segment_ids, weights, blocks)
+    return settle(finish(proj, d_attn, cosine, sine, segment_ids, weights, blocks))
 
 
 def solution(mesh):

time: 336 us -> 333 us (level)
  local copies, waits for them, and re-layouts: 11.4 us -> 0 us
  Pallas kernels: 322 us -> 330 us
    unnamed x13 -> x0, local copies, waits for them, and re-layouts: 11.4 us -> none
    pallas_call x0 -> x1, Pallas kernels: none -> 8.5 us  [settle(): pl.pallas_call(settle_kernel, out_shape=tuple((jax.ShapeDtypeStruct(a.sha...]
where the time goes in v7:
time: 333 us
  Pallas kernels  330 us (99%)
    pallas_call x1, Pallas kernels, finish(): pl.pallas_call(finish_kernel, out_shape=(jax.ShapeDtypeStruct((length, 16...  195 us
    pallas_call x1, Pallas kernels, project(): pl.pallas_call(project_kernel, out_shape=(block, block, jax.ShapeDtypeStr...  127 us
    pallas_call x1, Pallas kernels, settle(): pl.pallas_call(settle_kernel, out_shape=tuple((jax.ShapeDtypeStruct(a.sha...  8.5 us

profile of v7, /device:TPU:73, one launch (start us, length us, event | category | flops | bytes accessed | tf_op | source)
XLA Modules:
  0.0 333.3 jit_solution(4669014474561638583)
XLA Ops:
  0.6 1.0 fusion.2
  1.6 1.0 pad_maximum_fusion
  2.6 126.8 %project.1 = (bf16[8,512,1024]{2,1,0:T(8,128)(2,1)}, bf16[8,512,1024]{2,1,0:T(8,128)(2,1)}, f32[512,640]{1,0:T(8,128)}, bf16[512,512]{1,0:T(8,128)(2,1)}) custom-call(bf16[512,8192]{1,0:T(8,128)(2,1)} %tokens.1, bf16[512,8192]{1,0:T(8,128)(2,1)} %cot.1, bf16[1024,512]{1,0:T(8,128)(2,1)} %q_weight.3, bf16[1024,128]{1,0:T(8,128)(2,1)} %kv_weight.3, ...), custom_call_target="tpu_custom_call" | custom-call | tf_op jit(solution)/shard_map/project/pallas_call | solution.py:224
  129.4 195.1 %finish.1 = (bf16[512,8192]{1,0:T(8,128)(2,1)}, bf16[512,512]{1,0:T(8,128)(2,1)}, bf16[1024,512]{1,0:T(8,128)(2,1)}, bf16[1024,128]{1,0:T(8,128)(2,1)}, bf16[1024,512]{1,0:T(8,128)(2,1)}) custom-call(f32[512,640]{1,0:T(8,128)} %get-tuple-element.14.proj, bf16[512,512]{1,0:T(8,128)(2,1)} %get-tuple-element.15.d_attn, f32[512,128]{1,0:T(8,128)} %get-tuple-element.26.cosine, ...), custom_call_target="tpu_custom_call" | custom-call | tf_op jit(solution)/shard_map/finish/pallas_call | solution.py:768
  324.6 8.5 %settle.1 = (bf16[512,8192]{1,0:T(8,128)(2,1)}, bf16[512,512]{1,0:T(8,128)(2,1)}, bf16[1024,512]{1,0:T(8,128)(2,1)}, bf16[1024,128]{1,0:T(8,128)(2,1)}, bf16[1024,512]{1,0:T(8,128)(2,1)}) custom-call(bf16[512,8192]{1,0:T(8,128)(2,1)} %get-tuple-element.18.refs_0_, bf16[512,512]{1,0:T(8,128)(2,1)} %get-tuple-element.19.refs_1_, ...), custom_call_target="tpu_custom_call" | custom-call | tf_op jit(solution)/shard_map/settle/pallas_call | solution.py:865
  (1 shorter events, 0.0 us)

commit v8 on v7

--- a/solution.py
+++ b/solution.py
@@ -156,6 +156,7 @@
             seat_there = (z + dz + 4) % 4 * 2 + (1 - core)
             arrived(rows(a, dh, dx, seat_there), core_r.at[a, j, which])
 
+    outs, keeps = (token_out, cot_out), []
     weights = (in_weight, o_weight)
     outgoing = (proj_send, cot_send)
     incoming = (proj_recv, cot_recv)
@@ -167,6 +168,9 @@
         dh, dx = CHUNKS[k]
         j = index(dh, dx)
         complete(a, dh, dx)
+        copy = pltpu.make_async_copy(blocks.at[a, j], outs[a].at[j], keep.at[a, j])
+        copy.start()
+        keeps.append(copy)
         terms = adds.get(k, ())
         for term in terms:
             arrived(incoming[a].at[term], sum_r.at[a, term])
@@ -201,12 +205,6 @@
         while waiting and pieces.index(waiting[0]) + late.get(waiting[0], 5) <= step:
             chunk(*waiting.pop(0))
     assert not waiting
-    keeps = [
-        pltpu.make_async_copy(blocks.at[0], token_out, keep.at[0]),
-        pltpu.make_async_copy(blocks.at[1], cot_out, keep.at[1]),
-    ]
-    for copy in keeps:
-        copy.start()
     for copy in sent:
         copy.wait_send()
     for copy in keeps:
@@ -249,7 +247,7 @@
             dma((2, 8, 4)),
             dma((2, 7)),
             dma((2, 7)),
-            dma((2,)),
+            dma((2, 8)),
         ],
         compiler_params=pltpu.CompilerParams(
             collective_id=0, has_side_effects=True, vmem_limit_bytes=56 * MIB

time: 333 us -> 329 us (0.988)
  Pallas kernels: 330 us -> 326 us
    pallas_call x1, Pallas kernels: 127 us -> 122 us  [project(): pl.pallas_call(project_kernel, out_shape=(block, block, jax.ShapeDtypeStr...]
where the time goes in v8:
time: 329 us; the launch traced here: 328 us
  Pallas kernels  326 us (99%)
    pallas_call x1, Pallas kernels, finish(): pl.pallas_call(finish_kernel, out_shape=(jax.ShapeDtypeStruct((length, 16...  195 us
    pallas_call x1, Pallas kernels, project(): pl.pallas_call(project_kernel, out_shape=(block, block, jax.ShapeDtypeStr...  122 us
    pallas_call x1, Pallas kernels, settle(): pl.pallas_call(settle_kernel, out_shape=tuple((jax.ShapeDtypeStruct(a.sha...  8.5 us

profile of v8, /device:TPU:73, one launch (start us, length us, event | category | flops | bytes accessed | tf_op | source)
XLA Modules:
  0.0 328.4 jit_solution(8826538498666685727)
XLA Ops:
  0.6 1.0 fusion.2
  1.6 1.0 pad_maximum_fusion
  2.6 121.9 %project.1 = (bf16[8,512,1024]{2,1,0:T(8,128)(2,1)}, bf16[8,512,1024]{2,1,0:T(8,128)(2,1)}, f32[512,640]{1,0:T(8,128)}, bf16[512,512]{1,0:T(8,128)(2,1)}) custom-call(bf16[512,8192]{1,0:T(8,128)(2,1)} %tokens.1, bf16[512,8192]{1,0:T(8,128)(2,1)} %cot.1, bf16[1024,512]{1,0:T(8,128)(2,1)} %q_weight.3, bf16[1024,128]{1,0:T(8,128)(2,1)} %kv_weight.3, ...), custom_call_target="tpu_custom_call" | custom-call | tf_op jit(solution)/shard_map/project/pallas_call | solution.py:222
  124.5 195.1 %finish.1 = (bf16[512,8192]{1,0:T(8,128)(2,1)}, bf16[512,512]{1,0:T(8,128)(2,1)}, bf16[1024,512]{1,0:T(8,128)(2,1)}, bf16[1024,128]{1,0:T(8,128)(2,1)}, bf16[1024,512]{1,0:T(8,128)(2,1)}) custom-call(f32[512,640]{1,0:T(8,128)} %get-tuple-element.14.proj, bf16[512,512]{1,0:T(8,128)(2,1)} %get-tuple-element.15.d_attn, f32[512,128]{1,0:T(8,128)} %get-tuple-element.26.cosine, ...), custom_call_target="tpu_custom_call" | custom-call | tf_op jit(solution)/shard_map/finish/pallas_call | solution.py:766
  319.7 8.5 %settle.1 = (bf16[512,8192]{1,0:T(8,128)(2,1)}, bf16[512,512]{1,0:T(8,128)(2,1)}, bf16[1024,512]{1,0:T(8,128)(2,1)}, bf16[1024,128]{1,0:T(8,128)(2,1)}, bf16[1024,512]{1,0:T(8,128)(2,1)}) custom-call(bf16[512,8192]{1,0:T(8,128)(2,1)} %get-tuple-element.18.refs_0_, bf16[512,512]{1,0:T(8,128)(2,1)} %get-tuple-element.19.refs_1_, ...), custom_call_target="tpu_custom_call" | custom-call | tf_op jit(solution)/shard_map/settle/pallas_call | solution.py:863
  (1 shorter events, 0.0 us)
